TPU v7x, 32 devices: a whole 2x2x4 slice. The times are simulated.
32 devices in a mesh: groups: 2 (over y), row: 8 (over z, x), col: 2 (over core).
Axes of the slice: x: 2, y: 2, z: 4, core: 2. Of those that a mesh axis runs over, the one named last changes fastest.
Arguments:
- pair_rep: bfloat16 [576, 288, 128], P(('groups', 'row'), 'col'), parts along dimension 0, may hold values from -6 to 6
- slab_rep: bfloat16 [16, 288, 128], P(('groups', 'row')), parts along dimension 0, may hold values from -6 to 6
- length: int32 [2], P('groups'), parts along dimension 0, may hold values from 144 to 288
- weight_a: bfloat16 [128, 128], replicated, may hold values from -0.5 to 0.5
- gate_a: bfloat16 [128, 128], replicated, may hold values from -0.5 to 0.5
- weight_b: bfloat16 [128, 128], replicated, may hold values from -0.5 to 0.5
- gate_b: bfloat16 [128, 128], replicated, may hold values from -0.5 to 0.5
- weight_gate: bfloat16 [128, 128], replicated, may hold values from -0.5 to 0.5
- weight_out: bfloat16 [128, 128], replicated, may hold values from -0.5 to 0.5
Outputs:
- update: bfloat16 [16, 288, 128], P('groups', ('row', 'col')), parts along dimension 0
There are 2 independent parts, one for each index of `groups`. A program takes and returns all parts, laid end to end along the dimension named above; an argument that names none is the same for every part. Nothing has to cross between parts.
Inputs may be any that keep to these rules, and one draw needn't show every extreme that they name: Positions at index length or beyond are padding.
All inputs are finite; a program needn't handle non-finite values.
Results may differ from a plain program's by a relative error of at most 0.0085.
Values may be sent and summed in bfloat16 or wider, within the bound.
No kernel may reach another device: no remote copies, remote signals or barrier semaphores. Data moves between devices by JAX's collectives and lax.ppermute only.
A program may use at most 64 MiB of HBM per device.

v0:
```python
import jax
import jax.numpy as jnp
from jax import lax
from jax.sharding import PartitionSpec as P

epsilon = 1e-05


def passed_along(x, axis, by):
    count = lax.axis_size(axis)
    return lax.ppermute(x, axis, [(i, (i + by) % count) for i in range(count)])


def layer_norm(values):
    values = values.astype(jnp.float32)
    center = jnp.mean(values, axis=-1, keepdims=True)
    spread = jnp.mean((values - center) ** 2, axis=-1, keepdims=True)
    return (values - center) * lax.rsqrt(spread + epsilon)


def shards(pair_rep, slab_rep, length, weight_a, gate_a, weight_b, gate_b, weight_gate, weight_out):
    rows_dev, half_cols, width = pair_rep.shape
    slab_rows = slab_rep.shape[0]
    hidden_width = weight_a.shape[1]
    cycle_size = lax.axis_size("row")
    row_place = lax.axis_index("row")
    col_side = lax.axis_index("col")
    live_count = length[0]
    k_index = col_side * half_cols + jnp.arange(half_cols, dtype=jnp.int32)
    live_k = (k_index < live_count).astype(jnp.float32)
    j_index = row_place * rows_dev + jnp.arange(rows_dev, dtype=jnp.int32)
    live_j = (j_index < live_count).astype(jnp.float32)
    pair_norm = layer_norm(pair_rep).astype(jnp.bfloat16)
    right = jax.nn.sigmoid(jnp.dot(pair_norm, gate_b, preferred_element_type=jnp.float32))
    right = right * jnp.dot(pair_norm, weight_b, preferred_element_type=jnp.float32)
    right = (right * live_j[:, None, None] * live_k[None, :, None]).astype(jnp.bfloat16)
    slab_norm = layer_norm(slab_rep).astype(jnp.bfloat16)
    own_cols = lax.dynamic_slice_in_dim(slab_norm, col_side * half_cols, half_cols, 1)
    left = jax.nn.sigmoid(jnp.dot(own_cols, gate_a, preferred_element_type=jnp.float32))
    left = (
        left
        * jnp.dot(own_cols, weight_a, preferred_element_type=jnp.float32)
        * live_k[None, :, None]
    ).astype(jnp.bfloat16)
    quarter = rows_dev // 2
    picked = slab_norm.reshape(slab_rows, cycle_size, 2, quarter, width)
    picked = lax.dynamic_index_in_dim(picked, col_side, 2, keepdims=False)
    gate_vals = jax.nn.sigmoid(
        jnp.dot(picked, weight_gate, preferred_element_type=jnp.float32)
    ).astype(jnp.bfloat16)
    gate_vals = lax.all_to_all(gate_vals, "row", split_axis=1, concat_axis=0, tiled=True)
    gate_vals = gate_vals.reshape(slab_rows * cycle_size, quarter, width)

    def contract(edge_rows):
        return jnp.einsum("ikc,jkc->ijc", edge_rows, right, preferred_element_type=jnp.float32)

    running = jnp.zeros((slab_rows * cycle_size, rows_dev, hidden_width), jnp.float32)

    def cycle_step(turn_index, carry):
        cycle_block, running = carry
        anchor = (row_place - turn_index) % cycle_size
        running = lax.dynamic_update_slice_in_dim(
            running, contract(cycle_block), anchor * slab_rows, 0
        )
        cycle_block = passed_along(cycle_block, "row", 1)
        return (cycle_block, running)

    cycle_block, running = lax.fori_loop(0, cycle_size - 1, cycle_step, (left, running))
    anchor = (row_place - (cycle_size - 1)) % cycle_size
    partial_tri = lax.dynamic_update_slice_in_dim(
        running, contract(cycle_block), anchor * slab_rows, 0
    )
    summed = lax.psum_scatter(partial_tri, "col", scatter_dimension=1, tiled=True)
    tri_norm = layer_norm(summed).astype(jnp.bfloat16)
    projected = jnp.dot(tri_norm, weight_out, preferred_element_type=jnp.float32)
    return (projected * gate_vals.astype(jnp.float32)).astype(jnp.bfloat16)


def solution(mesh):
    placed = (
        P(("groups", "row"), "col", None),
        P(("groups", "row"), None, None),
        P("groups"),
        P(),
        P(),
        P(),
        P(),
        P(),
        P(),
    )
    return jax.shard_map(
        shards,
        mesh=mesh,
        in_specs=placed,
        out_specs=P("groups", ("row", "col"), None),
        check_vma=False,
    )
```

profile of v0, /device:TPU:0, one launch (start us, length us, event | category | flops | bytes accessed | tf_op | source)
XLA Modules:
  0.0 88.8 jit_solution(17433136549388199882)
XLA Ops:
  6.5 0.0 copy-start
  6.5 0.0 reduce-scatter.2.cloned.1.call-start
  6.5 1.1 %convert_reduce_fusion.1 = f32[288]{0:T(512)S(1)} fusion(bf16[1,288,128]{2,1,0:T(8,128)(2,1)} %param.12), kind=kLoop, calls=%fused_computation.28 | loop fusion | flops 73440 | bytes 74880 | tf_op jit(solution)/shard_map/reduce_sum | solution.py:16
  7.7 1.1 %fusion.21 = f32[288]{0:T(512)S(1)} fusion(bf16[1,288,128]{2,1,0:T(8,128)(2,1)} %param.12, f32[288]{0:T(512)S(1)} %broadcast_multiply_fusion.2), kind=kLoop, calls=%fused_computation.31 | loop fusion | flops 147168 | bytes 76032 | tf_op jit(solution)/shard_map/reduce_sum | solution.py:17
  8.8 1.0 %fusion.22 = bf16[1,288,128]{2,1,0:T(8,128)(2,1)S(1)} fusion(bf16[1,288,128]{2,1,0:T(8,128)(2,1)} %param.12, f32[288]{0:T(512)S(1)} %add_rsqrt_fusion.2, f32[288]{0:T(512)S(1)} %broadcast_multiply_fusion.2), kind=kLoop, calls=%fused_computation.32 | loop fusion | flops 147456 | bytes 149760 | tf_op jit(solution)/shard_map/convert_element_type | solution.py:37
  10.5 2.0 %convert_reduce_fusion = f32[36,144]{1,0:T(8,128)S(1)} fusion(bf16[36,144,128]{2,1,0:T(8,128)(2,1)} %param.11), kind=kLoop, calls=%fused_computation.3 | loop fusion | flops 1321920 | bytes 1347840 | tf_op jit(solution)/shard_map/reduce_sum | solution.py:16
  12.5 0.0 copy-done.1
  12.5 0.0 copy-start.5
  12.5 0.0 copy-start.3
  12.5 2.2 %fusion.2 = f32[36,144]{1,0:T(8,128)S(1)} fusion(bf16[36,144,128]{2,1,0:T(8,128)(2,1)S(1)} %copy-done.1, f32[36,144]{1,0:T(8,128)S(1)} %broadcast_multiply_fusion), kind=kLoop, calls=%fused_computation.6 | loop fusion | flops 2649024 | bytes 1368576 | tf_op jit(solution)/shard_map/reduce_sum | solution.py:17
  14.8 0.0 copy-start.6
  14.8 0.0 copy-done
  14.8 3.3 %fusion.17 = f32[36,144,128]{2,1,0:T(8,128)S(1)} fusion(bf16[36,144,128]{2,1,0:T(8,128)(2,1)S(1)} %copy-done.1, f32[36,144]{1,0:T(8,128)S(1)} %add_rsqrt_fusion, f32[36,144]{1,0:T(8,128)S(1)} %broadcast_multiply_fusion, bf16[128,128]{1,0:T(8,128)(2,1)S(1)} %copy-done), kind=kOutput, calls=%fused_computation.26 | convolution fusion | flops 172523520 | bytes 4055552 | tf_op jit(solution)/shard_map/dot_general | solution.py:34
  18.2 0.0 copy-done.5
  18.2 0.2 fusion.12
  18.4 0.0 copy-done.3
  18.4 0.2 fusion.15
  18.5 0.0 copy-done.6
  18.6 2.2 %multiply_convert_fusion = bf16[36,144,128]{2,1,0:T(8,128)(2,1)S(1)} fusion(f32[36,144,128]{2,1,0:T(8,128)S(1)} %fusion.17, f32[144]{0:T(256)S(1)} %compare_convert_fusion.1, f32[36]{0:T(128)S(1)} %compare_convert_fusion, bf16[36,144,128]{2,1,0:T(8,128)(2,1)S(1)} %copy-done.1, f32[36,144]{1,0:T(8,128)S(1)} %add_rsqrt_fusion, ...), kind=kOutput, calls=%fused_computation.9 | convolution fusion | flops 177168384 | bytes 5383376 | tf_op jit(solution)/shard_map/dot_general | solution.py:35
  20.8 0.0 copy-start.7
  20.8 48.3 %while.17 = (s32[]{:T(128)}, bf16[1,144,128]{2,1,0:T(8,128)(2,1)S(1)}, f32[8,36,128]{2,0,1:T(8,128)S(1)}, bf16[36,144,128]{2,1,0:T(8,128)(2,1)S(1)}, s32[]{:T(12...) while((s32[]{:T(128)}, bf16[1,144,128]{2,1,0:T(8,128)(2,1)S(1)}, f32[8,36,128]{2,0,1:T(8,128)S(1)}, ...), condition=%wide.region_5.6_spmd, body=%wide.region_4.5_spmd.sunk | while | flops 2004497 | bytes 1825060 | solution.py:68
  20.8 3.0 %collective-permute-start = (bf16[1,144,128]{2,1,0:T(8,128)(2,1)S(1)}, bf16[1,144,128]{2,1,0:T(8,128)(2,1)S(1)}, u32[]{:S(2)}, u32[]{:S(2)}) collective-permute-start(bf16[1,144,128]{2,1,0:T(8,128)(2,1)S(1)} %copy.51), channel_id=1, source_target_pairs={{0,2},{2,4},{4,6},{6,8},{8,10},{10,12},{12,14},{14,0},{1,3},{3,5},... | collective-permute-start | bytes 110600 | tf_op jit(solution)/shard_map/while/body/eval_jaxpr/ppermute | solution.py:11
  23.8 0.3 multiply_reduce_fusion.4
  24.1 0.1 dynamic_update_slice.15
  24.2 4.5 %collective-permute-done = bf16[1,144,128]{2,1,0:T(8,128)(2,1)S(1)} collective-permute-done((bf16[1,144,128]{2,1,0:T(8,128)(2,1)S(1)}, bf16[1,144,128]{2,1,0:T(8,128)(2,1)S(1)}, u32[]{:S(2)}, u32[]{:S(2)}) %collective-permute-start) | collective-permute-done | bytes 36896 | tf_op jit(solution)/shard_map/while/body/eval_jaxpr/ppermute | solution.py:11
  28.8 0.0 collective-permute-start
  28.8 0.3 multiply_reduce_fusion.4
  29.1 0.1 dynamic_update_slice.15
  29.2 6.2 %collective-permute-done = bf16[1,144,128]{2,1,0:T(8,128)(2,1)S(1)} collective-permute-done((bf16[1,144,128]{2,1,0:T(8,128)(2,1)S(1)}, bf16[1,144,128]{2,1,0:T(8,128)(2,1)S(1)}, u32[]{:S(2)}, u32[]{:S(2)}) %collective-permute-start) | collective-permute-done | bytes 36896 | tf_op jit(solution)/shard_map/while/body/eval_jaxpr/ppermute | solution.py:11
  35.4 0.0 collective-permute-start
  35.4 0.3 multiply_reduce_fusion.4
  35.8 0.1 dynamic_update_slice.15
  35.9 6.2 %collective-permute-done = bf16[1,144,128]{2,1,0:T(8,128)(2,1)S(1)} collective-permute-done((bf16[1,144,128]{2,1,0:T(8,128)(2,1)S(1)}, bf16[1,144,128]{2,1,0:T(8,128)(2,1)S(1)}, u32[]{:S(2)}, u32[]{:S(2)}) %collective-permute-start) | collective-permute-done | bytes 36896 | tf_op jit(solution)/shard_map/while/body/eval_jaxpr/ppermute | solution.py:11
  42.1 0.0 collective-permute-start
  42.1 0.3 multiply_reduce_fusion.4
  42.5 0.1 dynamic_update_slice.15
  42.6 6.2 %collective-permute-done = bf16[1,144,128]{2,1,0:T(8,128)(2,1)S(1)} collective-permute-done((bf16[1,144,128]{2,1,0:T(8,128)(2,1)S(1)}, bf16[1,144,128]{2,1,0:T(8,128)(2,1)S(1)}, u32[]{:S(2)}, u32[]{:S(2)}) %collective-permute-start) | collective-permute-done | bytes 36896 | tf_op jit(solution)/shard_map/while/body/eval_jaxpr/ppermute | solution.py:11
  48.8 0.0 collective-permute-start
  48.8 0.3 multiply_reduce_fusion.4
  49.1 0.1 dynamic_update_slice.15
  49.2 6.5 %collective-permute-done = bf16[1,144,128]{2,1,0:T(8,128)(2,1)S(1)} collective-permute-done((bf16[1,144,128]{2,1,0:T(8,128)(2,1)S(1)}, bf16[1,144,128]{2,1,0:T(8,128)(2,1)S(1)}, u32[]{:S(2)}, u32[]{:S(2)}) %collective-permute-start) | collective-permute-done | bytes 36896 | tf_op jit(solution)/shard_map/while/body/eval_jaxpr/ppermute | solution.py:11
  55.7 0.0 collective-permute-start
  55.8 0.3 multiply_reduce_fusion.4
  56.1 0.1 dynamic_update_slice.15
  56.2 6.2 %collective-permute-done = bf16[1,144,128]{2,1,0:T(8,128)(2,1)S(1)} collective-permute-done((bf16[1,144,128]{2,1,0:T(8,128)(2,1)S(1)}, bf16[1,144,128]{2,1,0:T(8,128)(2,1)S(1)}, u32[]{:S(2)}, u32[]{:S(2)}) %collective-permute-start) | collective-permute-done | bytes 36896 | tf_op jit(solution)/shard_map/while/body/eval_jaxpr/ppermute | solution.py:11
  62.4 0.0 collective-permute-start
  62.4 0.3 multiply_reduce_fusion.4
  62.8 0.1 dynamic_update_slice.15
  62.9 6.2 %collective-permute-done = bf16[1,144,128]{2,1,0:T(8,128)(2,1)S(1)} collective-permute-done((bf16[1,144,128]{2,1,0:T(8,128)(2,1)S(1)}, bf16[1,144,128]{2,1,0:T(8,128)(2,1)S(1)}, u32[]{:S(2)}, u32[]{:S(2)}) %collective-permute-start) | collective-permute-done | bytes 36896 | tf_op jit(solution)/shard_map/while/body/eval_jaxpr/ppermute | solution.py:11
  69.1 0.3 multiply_reduce_fusion.1
  69.4 0.1 dynamic_update_slice.13
  69.5 0.0 copy-start.2
  69.5 0.6 copy-done.2
  70.2 0.0 reduce-scatter.2.cloned.1.call-update
  70.2 0.0 copy-done.7
  70.2 0.8 fusion.14
  71.0 3.3 %all-to-all-start = ((bf16[1,8,18,128]{3,2,0,1:T(8,128)(2,1)}), bf16[1,8,18,128]{3,2,0,1:T(8,128)(2,1)S(1)}, u32[]{:S(2)}, u32[]{:S(2)}) async-start(bf16[1,8,18,128]{3,2,0,1:T(8,128)(2,1)} %fusion.14), calls=%async_computation.1 | async-start | bytes 98304 | tf_op jit(solution)/shard_map/all_to_all | solution.py:51
  74.4 0.9 reduce-scatter.2.cloned.1.call-done
  75.3 1.0 %reduce_sum.58 = f32[8,18]{0,1:T(8,128)S(1)} reduce(f32[8,18,128]{2,0,1:T(8,128)} %reduce-scatter.2.cloned.1.call-done, f32[]{:T(128)} %constant.88.clone.1), dimensions={2}, to_apply=%region_7.8 | reduce | flops 18288 | bytes 74308 | tf_op jit(solution)/shard_map/reduce_sum | solution.py:16
  76.3 1.0 %multiply_reduce_fusion.2 = f32[8,18]{0,1:T(8,128)S(1)} fusion(f32[8,18,128]{2,0,1:T(8,128)} %reduce-scatter.2.cloned.1.call-done, f32[8,18]{0,1:T(8,128)S(1)} %broadcast_multiply_fusion.1), kind=kLoop, calls=%fused_computation.34 | loop fusion | flops 55152 | bytes 74880 | tf_op jit(solution)/shard_map/reduce_sum | solution.py:17
  77.3 1.0 %multiply_convert_fusion.1 = bf16[8,18,128]{2,0,1:T(8,128)(2,1)S(1)} fusion(f32[8,18,128]{2,0,1:T(8,128)} %reduce-scatter.2.cloned.1.call-done, f32[8,18]{0,1:T(8,128)S(1)} %add_rsqrt_fusion.1, f32[8,18]{0,1:T(8,128)S(1)} %broadcast_multiply_fusion.1), kind=kLoop, calls=%fused_computation.33 | loop fusion | flops 55296 | bytes 111744 | tf_op jit(solution)/shard_map/convert_element_type | solution.py:74
  78.3 2.8 %all-to-all-done = bf16[1,8,18,128]{3,2,0,1:T(8,128)(2,1)S(1)} async-done(((bf16[1,8,18,128]{3,2,0,1:T(8,128)(2,1)}), bf16[1,8,18,128]{3,2,0,1:T(8,128)(2,1)S(1)}, u32[]{:S(2)}, u32[]{:S(2)}) %all-to-all-start) | async-done | bytes 36896 | tf_op jit(solution)/shard_map/all_to_all | solution.py:51
  81.1 0.2 fusion.7
  81.3 0.6 copy.17
  (36 shorter events, 0.3 us)
Async XLA Ops:
  6.5 8.3 %copy-start = (bf16[128,128]{1,0:T(8,128)(2,1)S(1)}, bf16[128,128]{1,0:T(8,128)(2,1)}, u32[]{:S(2)}) copy-start(bf16[128,128]{1,0:T(8,128)(2,1)} %param.17) | copy-start | bytes 98308
  6.5 6.0 %copy-start.1 = (bf16[36,144,128]{2,1,0:T(8,128)(2,1)S(1)}, bf16[36,144,128]{2,1,0:T(8,128)(2,1)}, u32[]{:S(2)}) copy-start(bf16[36,144,128]{2,1,0:T(8,128)(2,1)} %param.11) | copy-start | bytes 3981316
  6.5 68.7 %reduce-scatter.2.cloned.1.call-start = ((), (), s32[]{:S(2)}) async-start(), calls=%async_computation.2 | async-start | bytes 221184 | tf_op jit(solution)/shard_map/reduce_scatter | solution.py:73
  12.5 5.7 %copy-start.5 = (bf16[128,128]{1,0:T(8,128)(2,1)S(1)}, bf16[128,128]{1,0:T(8,128)(2,1)}, u32[]{:S(2)}) copy-start(bf16[128,128]{1,0:T(8,128)(2,1)} %param.15) | copy-start | bytes 98308
  12.5 5.9 %copy-start.3 = (bf16[128,128]{1,0:T(8,128)(2,1)S(1)}, bf16[128,128]{1,0:T(8,128)(2,1)}, u32[]{:S(2)}) copy-start(bf16[128,128]{1,0:T(8,128)(2,1)} %param.14) | copy-start | bytes 98308
  14.8 3.8 %copy-start.6 = (bf16[128,128]{1,0:T(8,128)(2,1)S(1)}, bf16[128,128]{1,0:T(8,128)(2,1)}, u32[]{:S(2)}) copy-start(bf16[128,128]{1,0:T(8,128)(2,1)} %param.16) | copy-start | bytes 98308
  20.8 49.5 %copy-start.7 = (bf16[128,128]{1,0:T(8,128)(2,1)S(1)}, bf16[128,128]{1,0:T(8,128)(2,1)}, u32[]{:S(2)}) copy-start(bf16[128,128]{1,0:T(8,128)(2,1)} %param.18) | copy-start | bytes 98308
  20.8 8.0 %collective-permute-start = (bf16[1,144,128]{2,1,0:T(8,128)(2,1)S(1)}, bf16[1,144,128]{2,1,0:T(8,128)(2,1)S(1)}, u32[]{:S(2)}, u32[]{:S(2)}) collective-permute-start(bf16[1,144,128]{2,1,0:T(8,128)(2,1)S(1)} %copy.51), channel_id=1, source_target_pairs={{0,2},{2,4},{4,6},{6,8},{8,10},{10,12},{12,14},{14,0},{1,3},{3,5},... | collective-permute-start | bytes 110600 | tf_op jit(solution)/shard_map/while/body/eval_jaxpr/ppermute | solution.py:11
  28.8 6.7 %collective-permute-start = (bf16[1,144,128]{2,1,0:T(8,128)(2,1)S(1)}, bf16[1,144,128]{2,1,0:T(8,128)(2,1)S(1)}, u32[]{:S(2)}, u32[]{:S(2)}) collective-permute-start(bf16[1,144,128]{2,1,0:T(8,128)(2,1)S(1)} %copy.51), channel_id=1, source_target_pairs={{0,2},{2,4},{4,6},{6,8},{8,10},{10,12},{12,14},{14,0},{1,3},{3,5},... | collective-permute-start | bytes 110600 | tf_op jit(solution)/shard_map/while/body/eval_jaxpr/ppermute | solution.py:11
  35.4 6.7 %collective-permute-start = (bf16[1,144,128]{2,1,0:T(8,128)(2,1)S(1)}, bf16[1,144,128]{2,1,0:T(8,128)(2,1)S(1)}, u32[]{:S(2)}, u32[]{:S(2)}) collective-permute-start(bf16[1,144,128]{2,1,0:T(8,128)(2,1)S(1)} %copy.51), channel_id=1, source_target_pairs={{0,2},{2,4},{4,6},{6,8},{8,10},{10,12},{12,14},{14,0},{1,3},{3,5},... | collective-permute-start | bytes 110600 | tf_op jit(solution)/shard_map/while/body/eval_jaxpr/ppermute | solution.py:11
  42.1 6.7 %collective-permute-start = (bf16[1,144,128]{2,1,0:T(8,128)(2,1)S(1)}, bf16[1,144,128]{2,1,0:T(8,128)(2,1)S(1)}, u32[]{:S(2)}, u32[]{:S(2)}) collective-permute-start(bf16[1,144,128]{2,1,0:T(8,128)(2,1)S(1)} %copy.51), channel_id=1, source_target_pairs={{0,2},{2,4},{4,6},{6,8},{8,10},{10,12},{12,14},{14,0},{1,3},{3,5},... | collective-permute-start | bytes 110600 | tf_op jit(solution)/shard_map/while/body/eval_jaxpr/ppermute | solution.py:11
  48.8 7.0 %collective-permute-start = (bf16[1,144,128]{2,1,0:T(8,128)(2,1)S(1)}, bf16[1,144,128]{2,1,0:T(8,128)(2,1)S(1)}, u32[]{:S(2)}, u32[]{:S(2)}) collective-permute-start(bf16[1,144,128]{2,1,0:T(8,128)(2,1)S(1)} %copy.51), channel_id=1, source_target_pairs={{0,2},{2,4},{4,6},{6,8},{8,10},{10,12},{12,14},{14,0},{1,3},{3,5},... | collective-permute-start | bytes 110600 | tf_op jit(solution)/shard_map/while/body/eval_jaxpr/ppermute | solution.py:11
  55.7 6.7 %collective-permute-start = (bf16[1,144,128]{2,1,0:T(8,128)(2,1)S(1)}, bf16[1,144,128]{2,1,0:T(8,128)(2,1)S(1)}, u32[]{:S(2)}, u32[]{:S(2)}) collective-permute-start(bf16[1,144,128]{2,1,0:T(8,128)(2,1)S(1)} %copy.51), channel_id=1, source_target_pairs={{0,2},{2,4},{4,6},{6,8},{8,10},{10,12},{12,14},{14,0},{1,3},{3,5},... | collective-permute-start | bytes 110600 | tf_op jit(solution)/shard_map/while/body/eval_jaxpr/ppermute | solution.py:11
  62.4 6.7 %collective-permute-start = (bf16[1,144,128]{2,1,0:T(8,128)(2,1)S(1)}, bf16[1,144,128]{2,1,0:T(8,128)(2,1)S(1)}, u32[]{:S(2)}, u32[]{:S(2)}) collective-permute-start(bf16[1,144,128]{2,1,0:T(8,128)(2,1)S(1)} %copy.51), channel_id=1, source_target_pairs={{0,2},{2,4},{4,6},{6,8},{8,10},{10,12},{12,14},{14,0},{1,3},{3,5},... | collective-permute-start | bytes 110600 | tf_op jit(solution)/shard_map/while/body/eval_jaxpr/ppermute | solution.py:11
  69.1 12.1 %copy-start.4 = (bf16[128,128]{1,0:T(8,128)(2,1)S(1)}, bf16[128,128]{1,0:T(8,128)(2,1)}, u32[]{:S(2)}) copy-start(bf16[128,128]{1,0:T(8,128)(2,1)} %param.19) | copy-start | bytes 98308
  69.5 0.7 copy-start.2
  71.0 10.1 %all-to-all-start = ((bf16[1,8,18,128]{3,2,0,1:T(8,128)(2,1)}), bf16[1,8,18,128]{3,2,0,1:T(8,128)(2,1)S(1)}, u32[]{:S(2)}, u32[]{:S(2)}) async-start(bf16[1,8,18,128]{3,2,0,1:T(8,128)(2,1)} %fusion.14), calls=%async_computation.1 | async-start | bytes 98304 | tf_op jit(solution)/shard_map/all_to_all | solution.py:51
Sparse Core Ops, SparseCore 0:
  70.3 4.9 reduce-scatter.1
where the time goes:
time: 89.2 us; the launch traced here: 88.8 us
  waiting for transfers between devices  45.7 us (51%)
  between operations  14.3 us (16%)
  other arithmetic  13 us (15%)
  matrix products  6.82 us (8%)
  starting transfers between devices  6.35 us (7%)
  local copies, waits for them, and re-layouts  2.24 us (3%)
    ppermute x7, waiting for transfers between devices, passed_along(): return lax.ppermute(x, axis, [(i, (i + by) % count) for i in range(count)])  42 us
    reduce_sum x3, other arithmetic, layer_norm(): spread = jnp.mean((values - center) ** 2, axis=-1, keepdims=True)  4.39 us
    reduce_sum x3, other arithmetic, layer_norm(): center = jnp.mean(values, axis=-1, keepdims=True)  4.08 us
    all_to_all x1, starting transfers between devices, shards(): lax.all_to_all(gate_vals, 'row', split_axis=1, concat_axis=0, tiled=True)  3.35 us
    dot_general x1, matrix products, shards(): jnp.dot(pair_norm, gate_b, preferred_element_type=jnp.float32)  3.33 us
    ppermute x7, starting transfers between devices, passed_along(): return lax.ppermute(x, axis, [(i, (i + by) % count) for i in range(count)])  3 us
    all_to_all x1, waiting for transfers between devices, shards(): lax.all_to_all(gate_vals, 'row', split_axis=1, concat_axis=0, tiled=True)  2.8 us
    dot_general x8, other arithmetic, contract(): jnp.einsum('ikc,jkc->ijc', edge_rows, right, preferred_element_type=jnp.f...  2.36 us
  transfers between devices with their start and end apart: 9, of which 9 were waited for; matrix products, arithmetic and copies ran while one was open for 8% of the time, Pallas kernels for 0%

commit v1 on v0

v1 whole, which is shorter than its diff:
```python
import functools

import jax
import jax.numpy as jnp
from jax import lax
from jax.experimental import pallas as pl
from jax.experimental.pallas import tpu as pltpu
from jax.sharding import PartitionSpec as P

EPS = 1e-05
F32 = jnp.float32
BF16 = jnp.bfloat16


def divisor(total, limit, step=1):
    return max(d for d in range(step, total + 1, step) if total % d == 0 and (d <= limit or d == step))


def centering(width):
    row = lax.broadcasted_iota(jnp.int32, (2 * width, 2 * width), 0)
    col = lax.broadcasted_iota(jnp.int32, (2 * width, 2 * width), 1)
    share = jnp.where((row < width) == (col < width), 1.0 / width, 0.0)
    center = jnp.where(row == col, 1.0, 0.0) - share
    return center.astype(BF16), share.astype(BF16)


def normed(x, center, share):
    half = x.shape[0] // 2
    wide = jnp.concatenate([x[:half], x[half:]], axis=1)
    d = jnp.dot(wide, center, preferred_element_type=F32)
    var = jnp.dot((d * d).astype(BF16), share, preferred_element_type=F32)
    return (d * lax.rsqrt(var + EPS)).astype(BF16)


def gated(n, both):
    width = both.shape[1] // 2
    y = jnp.dot(n, both, preferred_element_type=F32)
    value = y[:, width:]
    return value + value * jnp.tanh(y[:, :width])


def pair_weights(gate_ref, weight_ref):
    half = jnp.asarray(0.5, BF16)
    return jnp.concatenate([gate_ref[...] * half, weight_ref[...] * half], axis=1)


def right_kernel(length_ref, pair_ref, gate_ref, weight_ref, out_ref):
    rows, cols, width = pair_ref.shape
    live = length_ref[0]
    first_k = lax.axis_index("col") * cols
    first_j = lax.axis_index("row") * (rows * pl.num_programs(0)) + pl.program_id(0) * rows
    center, share = centering(width)
    both = pair_weights(gate_ref, weight_ref)
    n = normed(pair_ref[...].reshape(rows * cols, width), center, share)
    k = first_k + lax.broadcasted_iota(jnp.int32, (cols, width), 0)
    for side in range(2):
        edge = gated(n[:, side * width : (side + 1) * width], both).reshape(rows // 2, cols, width)
        for r in range(rows // 2):
            j = side * (rows // 2) + r
            reach = jnp.where(first_j + j < live, live, 0)
            out_ref[j] = jnp.where(k < reach, edge[r], 0.0).astype(BF16)


def fold(parts):
    place = lax.broadcasted_iota(jnp.int32, parts[0].shape, 0)
    for step in (1, 2, 4):
        here = (place & step) == 0
        parts = [
            jnp.where(here, a, b) + pltpu.roll(jnp.where(here, b, a), 8 - step, 0)
            for a, b in zip(parts[0::2], parts[1::2])
        ]
    return parts[0]


def tri_kernel(
    length_ref, slab_ref, right_ref, gate_ref, weight_ref, out_gate_ref, send_ref, keep_ref, left_ref, norm_ref,
    *, group,
):
    slabs, depth, width = slab_ref.shape
    block = right_ref.shape[0]
    k_step, j_step = pl.program_id(0), pl.program_id(1)
    half_steps = pl.num_programs(1) // 2
    half_rows = block * half_steps
    side = lax.axis_index("col")
    half_cols = depth * pl.num_programs(0)

    @pl.when(j_step == 0)
    def _():
        center, share = centering(width)
        both = pair_weights(gate_ref, weight_ref)
        n = normed(slab_ref[...].reshape(slabs * depth, width), center, share)
        first_k = side * half_cols + k_step * depth
        k = first_k + lax.broadcasted_iota(jnp.int32, (depth, width), 0)
        live = length_ref[0]
        for part in range(2):
            own = n[:, part * width : (part + 1) * width]
            edge = gated(own, both).reshape(slabs // 2, depth, width)
            norm_ref[pl.ds(part * (slabs // 2 * depth), slabs // 2 * depth), :] = own.astype(F32)
            for i in range(slabs // 2):
                left_ref[part * (slabs // 2) + i] = jnp.where(k < live, edge[i], 0.0).astype(BF16).astype(F32)

    first_j = lax.rem(lax.axis_index("row") * (2 * half_rows), half_cols)

    @pl.when((j_step == 0) & (k_step == first_j // depth))
    def _():
        start = lax.rem(first_j, depth)

        def gates(place, dest_ref):
            rows = [
                norm_ref[pl.ds(start + place * half_rows + j, slabs, stride=depth), :] for j in range(half_rows)
            ]
            rows = jnp.concatenate(rows, axis=0).astype(BF16)
            y = jnp.dot(rows, out_gate_ref[...] * jnp.asarray(0.5, BF16), preferred_element_type=F32)
            dest_ref[1] = (0.5 + 0.5 * jnp.tanh(y)).astype(BF16).astype(F32)

        gates(1 - side, send_ref)
        gates(side, keep_ref)

    def contract(dest_ref, first_row):
        def some_rows(turn, _):
            for i0 in range(0, slabs, 8):
                sums = [[None] * 8 for _ in range(group)]
                for k0 in range(0, depth, 16):
                    edges = [right_ref[turn * group + j, pl.ds(k0, 16), :].astype(F32) for j in range(group)]
                    for i in range(8):
                        left = left_ref[i0 + i, pl.ds(k0, 16), :]
                        for j in range(group):
                            term = left * edges[j]
                            term = term[:8] + term[8:]
                            sums[j][i] = term if k0 == 0 else sums[j][i] + term
                for j in range(group):
                    row = (first_row + turn * group + j) * slabs + i0
                    dest = dest_ref.at[0, pl.ds(pl.multiple_of(row, 8), 8), :]
                    total = fold(sums[j])
                    dest[...] = jnp.where(k_step == 0, total, total + dest[...])
            return 0

        lax.fori_loop(0, block // group, some_rows, 0)

    @pl.when(j_step < half_steps)
    def _():
        contract(send_ref, j_step * block)

    @pl.when(j_step >= half_steps)
    def _():
        contract(keep_ref, (j_step - half_steps) * block)


def last_kernel(keep_ref, got_ref, weight_ref, out_ref, done_ref, *, owner_side):
    slabs, cols, width = out_ref.shape
    tri = keep_ref[0] + got_ref[0]
    d = tri - jnp.mean(tri, axis=-1, keepdims=True)
    var = jnp.mean(d * d, axis=-1, keepdims=True)
    n = (d * lax.rsqrt(var + EPS)).astype(BF16)
    projected = jnp.dot(n, weight_ref[...], preferred_element_type=F32)
    mine = owner_side(lax.axis_index("row")) == lax.axis_index("col")
    done_ref[...] = projected * jnp.where(mine, keep_ref[1], got_ref[1])
    for i in range(slabs):
        out_ref[i] = done_ref[pl.ds(i, cols, stride=slabs), :].astype(BF16)


def gathered(half, axis):
    count = lax.axis_size(axis)
    spread = jnp.broadcast_to(half[None], (count,) + half.shape)
    return lax.all_to_all(spread, axis, split_axis=0, concat_axis=0, tiled=True)


def shards(pair_rep, slab_rep, length, weight_a, gate_a, weight_b, gate_b, weight_gate, weight_out):
    rows_dev, half_cols, width = pair_rep.shape
    hidden = weight_a.shape[1]
    count = lax.axis_size("row")
    side = lax.axis_index("col")
    half_rows = rows_dev // 2
    smem = pl.BlockSpec(memory_space=pltpu.SMEM)
    vmem = pl.BlockSpec(memory_space=pltpu.VMEM)

    half = lax.dynamic_slice_in_dim(slab_rep, side * half_cols, half_cols, 1)
    slab = gathered(half, "row").reshape(-1, half_cols, width)
    slabs = slab.shape[0]

    rows_step = divisor(rows_dev, max(2, 1728 // half_cols), 2)
    whole_weight = pl.BlockSpec((width, hidden), lambda *_: (0, 0))
    right = pl.pallas_call(
        right_kernel,
        out_shape=jax.ShapeDtypeStruct((rows_dev, half_cols, hidden), BF16),
        grid=(rows_dev // rows_step,),
        in_specs=[
            smem,
            pl.BlockSpec((rows_step, half_cols, width), lambda s: (s, 0, 0)),
            whole_weight,
            whole_weight,
        ],
        out_specs=pl.BlockSpec((rows_step, half_cols, hidden), lambda s: (s, 0, 0)),
        compiler_params=pltpu.CompilerParams(vmem_limit_bytes=40 << 20),
        cost_estimate=pl.CostEstimate(
            flops=2 * rows_dev * half_cols * width * hidden * 6,
            bytes_accessed=4 * rows_dev * half_cols * width,
            transcendentals=2 * rows_dev * half_cols * width,
        ),
        name="right",
    )(length, pair_rep, gate_b, weight_b)

    depth = divisor(half_cols, 144, rows_dev)
    j_block = half_rows
    group = 3
    tri_shape = jax.ShapeDtypeStruct((2, half_rows * slabs, hidden), F32)
    tri_spec = pl.BlockSpec((2, half_rows * slabs, hidden), lambda k, j: (0, 0, 0))
    half_steps = half_rows // j_block

    def right_block(k, j):
        flip = 1 - lax.axis_index("col")
        return (lax.rem(j + flip * half_steps, 2 * half_steps), k, 0)

    send, keep = pl.pallas_call(
        functools.partial(tri_kernel, group=group),
        out_shape=(tri_shape, tri_shape),
        grid=(half_cols // depth, 2 * half_steps),
        in_specs=[
            smem,
            pl.BlockSpec((slabs, depth, width), lambda k, j: (0, k, 0)),
            pl.BlockSpec((j_block, depth, hidden), right_block),
            whole_weight,
            whole_weight,
            whole_weight,
        ],
        out_specs=(tri_spec, tri_spec),
        scratch_shapes=[
            pltpu.VMEM((slabs, depth, hidden), F32),
            pltpu.VMEM((slabs * depth, width), F32),
        ],
        compiler_params=pltpu.CompilerParams(vmem_limit_bytes=48 << 20),
        cost_estimate=pl.CostEstimate(
            flops=2 * rows_dev * half_cols * slabs * hidden,
            bytes_accessed=2 * rows_dev * half_cols * width,
            transcendentals=slabs * half_cols * width,
        ),
        name="tri",
    )(length, slab, right, gate_a, weight_a, weight_gate)

    got = lax.ppermute(send, "col", [(0, 1), (1, 0)])

    return pl.pallas_call(
        functools.partial(last_kernel, owner_side=lambda row: (row * rows_dev) // half_cols),
        out_shape=jax.ShapeDtypeStruct((slabs, half_rows, width), BF16),
        in_specs=[vmem, vmem, vmem],
        out_specs=vmem,
        scratch_shapes=[pltpu.VMEM((half_rows * slabs, width), F32)],
        compiler_params=pltpu.CompilerParams(vmem_limit_bytes=32 << 20),
        name="last",
    )(keep, got, weight_out)


def solution(mesh):
    placed = (
        P(("groups", "row"), "col", None),
        P(("groups", "row"), None, None),
        P("groups"),
        P(),
        P(),
        P(),
        P(),
        P(),
        P(),
    )
    return jax.shard_map(
        shards,
        mesh=mesh,
        in_specs=placed,
        out_specs=P("groups", ("row", "col"), None),
        check_vma=False,
    )
```

time: 89.2 us -> 24 us (0.27)
  waiting for transfers between devices: 45.7 us -> 5.21 us
  between operations: 14.3 us -> 0.71 us
  other arithmetic: 13 us -> 0 us
  matrix products: 6.82 us -> 0 us
  Pallas kernels: 0 us -> 5.21 us
  local copies, waits for them, and re-layouts: 2.24 us -> 5.11 us
  starting transfers between devices: 6.35 us -> 7.32 us
    ppermute x7 -> x1, waiting for transfers between devices: 42 us -> 1.36 us  [shards(): got = lax.ppermute(send, 'col', [(0, 1), (1, 0)])]
    reduce_sum x6 -> x0, other arithmetic: 8.47 us -> none  [the longest x3 4.39 us: layer_norm(): spread = jnp.mean((values - center) ** 2, axis=-1, keepdims=True)]
    dot_general x6 -> x0, matrix products: 6.82 us -> none  [the longest x1 3.33 us: shards(): jnp.dot(pair_norm, gate_b, preferred_element_type=jnp.float32)]
    pallas_call x0 -> x3, Pallas kernels: none -> 5.21 us  [the longest x1 2.65 us: shards(): pl.pallas_call(functools.partial(tri_kernel, group=group), out_shape=(tri...]
    all_to_all x1, starting transfers between devices: 3.35 us -> 7.25 us  [gathered(): return lax.all_to_all(spread, axis, split_axis=0, concat_axis=0, tiled=True)]
    unnamed x16, local copies, waits for them, and re-layouts: 0.68 us -> 3.73 us
    ppermute x7 -> x1, starting transfers between devices: 3 us -> 0.07 us  [shards(): got = lax.ppermute(send, 'col', [(0, 1), (1, 0)])]
    dot_general x8 -> x0, other arithmetic: 2.36 us -> none  [contract(): jnp.einsum('ikc,jkc->ijc', edge_rows, right, preferred_element_type=jnp.f...]
  transfers between devices with their start and end apart: 9 -> 2, of which waited for: 9 -> 2; matrix products, arithmetic and copies ran while one was open for 8% -> 0% of each run, Pallas kernels for 0% -> 10%
where the time goes in v1:
time: 24 us; the launch traced here: 23.6 us
  starting transfers between devices  7.32 us (30%)
  Pallas kernels  5.21 us (22%)
  waiting for transfers between devices  5.21 us (22%)
  local copies, waits for them, and re-layouts  5.11 us (21%)
  between operations  0.71 us (3%)
    all_to_all x1, starting transfers between devices, gathered(): return lax.all_to_all(spread, axis, split_axis=0, concat_axis=0, tiled=True)  7.25 us
    all_to_all x1, waiting for transfers between devices, gathered(): return lax.all_to_all(spread, axis, split_axis=0, concat_axis=0, tiled=True)  3.86 us
    unnamed x16, local copies, waits for them, and re-layouts  3.73 us
    pallas_call x1, Pallas kernels, shards(): pl.pallas_call(functools.partial(tri_kernel, group=group), out_shape=(tri...  2.65 us
    pallas_call x1, Pallas kernels, shards(): pl.pallas_call(right_kernel, out_shape=jax.ShapeDtypeStruct((rows_dev, ha...  2.24 us
    ppermute x1, waiting for transfers between devices, shards(): got = lax.ppermute(send, 'col', [(0, 1), (1, 0)])  1.36 us
    broadcast_in_dim x2, local copies, waits for them, and re-layouts, gathered(): spread = jnp.broadcast_to(half[None], (count,) + half.shape)  0.75 us
    pallas_call x1, local copies, waits for them, and re-layouts, shards(): pl.pallas_call(functools.partial(last_kernel, owner_side=lambda row: row...  0.62 us
  transfers between devices with their start and end apart: 2, of which 2 were waited for; matrix products, arithmetic and copies ran while one was open for 0% of the time, Pallas kernels for 10%

profile of v1, /device:TPU:0, one launch (start us, length us, event | category | flops | bytes accessed | tf_op | source)
XLA Modules:
  0.0 23.6 jit_solution(11850160564481213793)
XLA Ops:
  0.0 0.0 copy-start
  0.0 0.9 %copy-done = bf16[1,288,128]{2,1,0:T(8,128)(2,1)S(1)} copy-done((bf16[1,288,128]{2,1,0:T(8,128)(2,1)S(1)}, bf16[1,288,128]{2,1,0:T(8,128)(2,1)}, u32[]{:S(2)}) %copy-start) | copy-done | bytes 73752
  0.9 0.7 %broadcast_in_dim.9 = bf16[8,1,144,128]{3,2,1,0:T(8,128)(2,1)} broadcast(bf16[144,128]{1,0:T(8,128)(2,1)S(1)} %dynamic-slice_bitcast_fusion), dimensions={2,3} | broadcast | bytes 331776 | tf_op jit(solution)/shard_map/broadcast_in_dim | solution.py:164
  1.6 7.3 %all-to-all-start = ((bf16[8,1,144,128]{3,2,1,0:T(8,128)(2,1)}), bf16[8,1,144,128]{3,2,1,0:T(8,128)(2,1)S(1)}, u32[]{:S(2)}, u32[]{:S(2)}) async-start(bf16[8,1,144,128]{3,2,1,0:T(8,128)(2,1)} %broadcast_in_dim.9), calls=%async_computation | async-start | bytes 589824 | tf_op jit(solution)/shard_map/all_to_all | solution.py:165
  9.5 0.0 copy-start.5
  9.6 1.3 %copy-done.5 = bf16[36,144,128]{2,1,0:T(8,128)(2,1)S(1)} copy-done((bf16[36,144,128]{2,1,0:T(8,128)(2,1)S(1)}, bf16[36,144,128]{2,1,0:T(8,128)(2,1)}, u32[]{:S(2)}) %copy-start.5) | copy-done | bytes 1327128
  10.9 0.0 copy-start.6
  10.9 0.8 %copy-done.6 = bf16[128,128]{1,0:T(8,128)(2,1)S(1)} copy-done((bf16[128,128]{1,0:T(8,128)(2,1)S(1)}, bf16[128,128]{1,0:T(8,128)(2,1)}, u32[]{:S(2)}) %copy-start.6) | copy-done | bytes 32792
  11.6 0.0 copy-start.7
  11.6 0.8 %copy-done.7 = bf16[128,128]{1,0:T(8,128)(2,1)S(1)} copy-done((bf16[128,128]{1,0:T(8,128)(2,1)S(1)}, bf16[128,128]{1,0:T(8,128)(2,1)}, u32[]{:S(2)}) %copy-start.7) | copy-done | bytes 32792
  12.4 0.0 copy-start.1
  12.4 0.0 copy-start.2
  12.4 0.0 copy-start.3
  12.4 2.2 %right.1.right_ref = bf16[36,144,128]{2,1,0:T(8,128)(2,1)S(1)} custom-call(s32[1]{0:T(128)S(6)} %copy.12.length_ref, bf16[36,144,128]{2,1,0:T(8,128)(2,1)S(1)} %copy-done.5, bf16[128,128]{1,0:T(8,128)(2,1)S(1)} %copy-done.6, bf16[128,128]{1,0:T(8,128)(2,1)S(1)} %copy-done.7), custom_call_target="tpu_custom_call" | custom-call | flops 1019215872 | bytes 2654208 | tf_op jit(solution)/shard_map/right/pallas_call | solution.py:183
  14.6 0.0 copy-start.4
  14.7 3.9 %all-to-all-done = bf16[8,1,144,128]{3,2,1,0:T(8,128)(2,1)S(1)} async-done(((bf16[8,1,144,128]{3,2,1,0:T(8,128)(2,1)}), bf16[8,1,144,128]{3,2,1,0:T(8,128)(2,1)S(1)}, u32[]{:S(2)}, u32[]{:S(2)}) %all-to-all-start) | async-done | bytes 294944 | tf_op jit(solution)/shard_map/all_to_all | solution.py:165
  18.5 0.0 copy-done.1
  18.5 0.0 copy-done.2
  18.5 0.0 copy-done.3
  18.5 2.6 %tri.1 = (f32[2,144,128]{2,1,0:T(8,128)S(1)}, f32[2,144,128]{2,1,0:T(8,128)S(1)}) custom-call(s32[1]{0:T(128)S(6)} %copy.12.length_ref, bf16[8,144,128]{2,1,0:T(8,128)(2,1)S(1)} %bitcast.3, bf16[36,144,128]{2,1,0:T(8,128)(2,1)S(1)} %right.1.right_ref, bf16[128,128]{1,0:T(8,128)(2,1)S(1)} %copy-done.1, bf16[128,128]{1,0:T(8,128)(2,1)S(1)} %copy-done.2, ...), custom_call_target="tpu_custom_call" | custom-call | flops 10616832 | bytes 1327104 | tf_op jit(solution)/shard_map/tri/pallas_call | solution.py:214
  21.2 0.1 collective-permute-start
  21.3 1.4 %collective-permute-done.got_ref = f32[2,144,128]{2,1,0:T(8,128)S(1)} collective-permute-done((f32[2,144,128]{2,1,0:T(8,128)S(1)}, f32[2,144,128]{2,1,0:T(8,128)S(1)}, u32[]{:S(2)}, u32[]{:S(2)}) %collective-permute-start) | collective-permute-done | bytes 147488 | tf_op jit(solution)/shard_map/ppermute | solution.py:240
  22.6 0.0 copy-done.4
  22.6 0.3 %last.1 = bf16[8,18,128]{2,1,0:T(8,128)(2,1)S(1)} custom-call(f32[2,144,128]{2,1,0:T(8,128)S(1)} %get-tuple-element.7.keep_ref, f32[2,144,128]{2,1,0:T(8,128)S(1)} %collective-permute-done.got_ref, bf16[128,128]{1,0:T(8,128)(2,1)S(1)} %copy-done.4), custom_call_target="tpu_custom_call" | custom-call | tf_op jit(solution)/shard_map/last/pallas_call | solution.py:242
  22.9 0.6 %copy.11 = bf16[8,18,128]{2,0,1:T(8,128)(2,1)} copy(bf16[8,18,128]{2,1,0:T(8,128)(2,1)S(1)} %last.1) | data formatting | bytes 73728 | tf_op jit(solution)/shard_map/last/pallas_call | solution.py:242
  (1 shorter events, 0.0 us)
Async XLA Ops:
  0.0 0.9 %copy-start = (bf16[1,288,128]{2,1,0:T(8,128)(2,1)S(1)}, bf16[1,288,128]{2,1,0:T(8,128)(2,1)}, u32[]{:S(2)}) copy-start(bf16[1,288,128]{2,1,0:T(8,128)(2,1)} %param.10) | copy-start | bytes 221188
  1.6 16.9 %all-to-all-start = ((bf16[8,1,144,128]{3,2,1,0:T(8,128)(2,1)}), bf16[8,1,144,128]{3,2,1,0:T(8,128)(2,1)S(1)}, u32[]{:S(2)}, u32[]{:S(2)}) async-start(bf16[8,1,144,128]{3,2,1,0:T(8,128)(2,1)} %broadcast_in_dim.9), calls=%async_computation | async-start | bytes 589824 | tf_op jit(solution)/shard_map/all_to_all | solution.py:165
  9.5 1.3 %copy-start.5 = (bf16[36,144,128]{2,1,0:T(8,128)(2,1)S(1)}, bf16[36,144,128]{2,1,0:T(8,128)(2,1)}, u32[]{:S(2)}) copy-start(bf16[36,144,128]{2,1,0:T(8,128)(2,1)} %pair_ref.1) | copy-start | bytes 3981316
  10.9 0.8 %copy-start.6 = (bf16[128,128]{1,0:T(8,128)(2,1)S(1)}, bf16[128,128]{1,0:T(8,128)(2,1)}, u32[]{:S(2)}) copy-start(bf16[128,128]{1,0:T(8,128)(2,1)} %gate_ref.2) | copy-start | bytes 98308
  11.6 0.8 %copy-start.7 = (bf16[128,128]{1,0:T(8,128)(2,1)S(1)}, bf16[128,128]{1,0:T(8,128)(2,1)}, u32[]{:S(2)}) copy-start(bf16[128,128]{1,0:T(8,128)(2,1)} %weight_ref.3) | copy-start | bytes 98308
  12.4 6.1 %copy-start.1 = (bf16[128,128]{1,0:T(8,128)(2,1)S(1)}, bf16[128,128]{1,0:T(8,128)(2,1)}, u32[]{:S(2)}) copy-start(bf16[128,128]{1,0:T(8,128)(2,1)} %gate_ref.3) | copy-start | bytes 98308
  12.4 6.1 %copy-start.2 = (bf16[128,128]{1,0:T(8,128)(2,1)S(1)}, bf16[128,128]{1,0:T(8,128)(2,1)}, u32[]{:S(2)}) copy-start(bf16[128,128]{1,0:T(8,128)(2,1)} %weight_ref.4) | copy-start | bytes 98308
  12.4 6.1 %copy-start.3 = (bf16[128,128]{1,0:T(8,128)(2,1)S(1)}, bf16[128,128]{1,0:T(8,128)(2,1)}, u32[]{:S(2)}) copy-start(bf16[128,128]{1,0:T(8,128)(2,1)} %out_gate_ref.1) | copy-start | bytes 98308
  14.6 8.0 %copy-start.4 = (bf16[128,128]{1,0:T(8,128)(2,1)S(1)}, bf16[128,128]{1,0:T(8,128)(2,1)}, u32[]{:S(2)}) copy-start(bf16[128,128]{1,0:T(8,128)(2,1)} %weight_ref.5) | copy-start | bytes 98308
  21.2 1.4 %collective-permute-start = (f32[2,144,128]{2,1,0:T(8,128)S(1)}, f32[2,144,128]{2,1,0:T(8,128)S(1)}, u32[]{:S(2)}, u32[]{:S(2)}) collective-permute-start(f32[2,144,128]{2,1,0:T(8,128)S(1)} %get-tuple-element.8), channel_id=1, source_target_pairs={{0,1},{1,0},{2,3},{3,2},{4,5},{5,4},{6,7},{7,6},{8,9},{9,8},{10,11... | collective-permute-start | bytes 442376 | tf_op jit(solution)/shard_map/ppermute | solution.py:240

commit v2 on v1

--- a/solution.py
+++ b/solution.py
@@ -24,9 +24,8 @@
     return center.astype(BF16), share.astype(BF16)
 
 
-def normed(x, center, share):
-    half = x.shape[0] // 2
-    wide = jnp.concatenate([x[:half], x[half:]], axis=1)
+def normed(first, second, center, share):
+    wide = jnp.concatenate([first, second], axis=1)
     d = jnp.dot(wide, center, preferred_element_type=F32)
     var = jnp.dot((d * d).astype(BF16), share, preferred_element_type=F32)
     return (d * lax.rsqrt(var + EPS)).astype(BF16)
@@ -51,7 +50,8 @@
     first_j = lax.axis_index("row") * (rows * pl.num_programs(0)) + pl.program_id(0) * rows
     center, share = centering(width)
     both = pair_weights(gate_ref, weight_ref)
-    n = normed(pair_ref[...].reshape(rows * cols, width), center, share)
+    x = pair_ref[...].reshape(2, rows * cols // 2, width)
+    n = normed(x[0], x[1], center, share)
     k = first_k + lax.broadcasted_iota(jnp.int32, (cols, width), 0)
     for side in range(2):
         edge = gated(n[:, side * width : (side + 1) * width], both).reshape(rows // 2, cols, width)
@@ -72,11 +72,10 @@
     return parts[0]
 
 
-def tri_kernel(
-    length_ref, slab_ref, right_ref, gate_ref, weight_ref, out_gate_ref, send_ref, keep_ref, left_ref, norm_ref,
-    *, group,
-):
-    slabs, depth, width = slab_ref.shape
+def tri_kernel(length_ref, right_ref, gate_ref, weight_ref, out_gate_ref, *refs, group):
+    slab_refs, (send_ref, keep_ref, left_ref, norm_ref) = refs[:-4], refs[-4:]
+    slabs = len(slab_refs)
+    _, depth, width = slab_refs[0].shape
     block = right_ref.shape[0]
     k_step, j_step = pl.program_id(0), pl.program_id(1)
     half_steps = pl.num_programs(1) // 2
@@ -88,16 +87,17 @@
     def _():
         center, share = centering(width)
         both = pair_weights(gate_ref, weight_ref)
-        n = normed(slab_ref[...].reshape(slabs * depth, width), center, share)
         first_k = side * half_cols + k_step * depth
         k = first_k + lax.broadcasted_iota(jnp.int32, (depth, width), 0)
         live = length_ref[0]
-        for part in range(2):
-            own = n[:, part * width : (part + 1) * width]
-            edge = gated(own, both).reshape(slabs // 2, depth, width)
-            norm_ref[pl.ds(part * (slabs // 2 * depth), slabs // 2 * depth), :] = own.astype(F32)
-            for i in range(slabs // 2):
-                left_ref[part * (slabs // 2) + i] = jnp.where(k < live, edge[i], 0.0).astype(BF16).astype(F32)
+        place = lax.axis_index("row")
+        for m in range(0, slabs, 2):
+            pair = normed(slab_refs[m][0], slab_refs[m + 1][0], center, share)
+            for part in range(2):
+                i = jnp.bitwise_xor(place, m + part)
+                n = pair[:, part * width : (part + 1) * width]
+                norm_ref[pl.ds(pl.multiple_of(i * depth, 16), depth), :] = n.astype(F32)
+                left_ref[i] = jnp.where(k < live, gated(n, both), 0.0).astype(BF16).astype(F32)
 
     first_j = lax.rem(lax.axis_index("row") * (2 * half_rows), half_cols)
 
@@ -146,23 +146,15 @@
         contract(keep_ref, (j_step - half_steps) * block)
 
 
-def last_kernel(keep_ref, got_ref, weight_ref, out_ref, done_ref, *, owner_side):
-    slabs, cols, width = out_ref.shape
+def last_kernel(keep_ref, got_ref, weight_ref, out_ref, *, owner_side):
     tri = keep_ref[0] + got_ref[0]
     d = tri - jnp.mean(tri, axis=-1, keepdims=True)
     var = jnp.mean(d * d, axis=-1, keepdims=True)
     n = (d * lax.rsqrt(var + EPS)).astype(BF16)
     projected = jnp.dot(n, weight_ref[...], preferred_element_type=F32)
     mine = owner_side(lax.axis_index("row")) == lax.axis_index("col")
-    done_ref[...] = projected * jnp.where(mine, keep_ref[1], got_ref[1])
-    for i in range(slabs):
-        out_ref[i] = done_ref[pl.ds(i, cols, stride=slabs), :].astype(BF16)
-
-
-def gathered(half, axis):
-    count = lax.axis_size(axis)
-    spread = jnp.broadcast_to(half[None], (count,) + half.shape)
-    return lax.all_to_all(spread, axis, split_axis=0, concat_axis=0, tiled=True)
+    update = projected * jnp.where(mine, keep_ref[1], got_ref[1])
+    out_ref[...] = update.astype(BF16).reshape(out_ref.shape)
 
 
 def shards(pair_rep, slab_rep, length, weight_a, gate_a, weight_b, gate_b, weight_gate, weight_out):
@@ -174,9 +166,9 @@
     smem = pl.BlockSpec(memory_space=pltpu.SMEM)
     vmem = pl.BlockSpec(memory_space=pltpu.VMEM)
 
+    slabs = count
     half = lax.dynamic_slice_in_dim(slab_rep, side * half_cols, half_cols, 1)
-    slab = gathered(half, "row").reshape(-1, half_cols, width)
-    slabs = slab.shape[0]
+    slab = [half] + [lax.ppermute(half, "row", [(r, r ^ m) for r in range(count)]) for m in range(1, count)]
 
     rows_step = divisor(rows_dev, max(2, 1728 // half_cols), 2)
     whole_weight = pl.BlockSpec((width, hidden), lambda *_: (0, 0))
@@ -217,12 +209,12 @@
         grid=(half_cols // depth, 2 * half_steps),
         in_specs=[
             smem,
-            pl.BlockSpec((slabs, depth, width), lambda k, j: (0, k, 0)),
             pl.BlockSpec((j_block, depth, hidden), right_block),
             whole_weight,
             whole_weight,
             whole_weight,
-        ],
+        ]
+        + [pl.BlockSpec((1, depth, width), lambda k, j: (0, k, 0))] * slabs,
         out_specs=(tri_spec, tri_spec),
         scratch_shapes=[
             pltpu.VMEM((slabs, depth, hidden), F32),
@@ -235,19 +227,19 @@
             transcendentals=slabs * half_cols * width,
         ),
         name="tri",
-    )(length, slab, right, gate_a, weight_a, weight_gate)
+    )(length, right, gate_a, weight_a, weight_gate, *slab)
 
     got = lax.ppermute(send, "col", [(0, 1), (1, 0)])
 
-    return pl.pallas_call(
+    update = pl.pallas_call(
         functools.partial(last_kernel, owner_side=lambda row: (row * rows_dev) // half_cols),
-        out_shape=jax.ShapeDtypeStruct((slabs, half_rows, width), BF16),
+        out_shape=jax.ShapeDtypeStruct((half_rows, slabs, width), BF16),
         in_specs=[vmem, vmem, vmem],
         out_specs=vmem,
-        scratch_shapes=[pltpu.VMEM((half_rows * slabs, width), F32)],
         compiler_params=pltpu.CompilerParams(vmem_limit_bytes=32 << 20),
         name="last",
     )(keep, got, weight_out)
+    return jnp.transpose(update, (1, 0, 2))
 
 
 def solution(mesh):

time: 24 us -> 25.4 us (1.058)
  starting transfers between devices: 7.32 us -> 12.5 us
  waiting for transfers between devices: 5.21 us -> 1.38 us
  Pallas kernels: 5.21 us -> 6.6 us
  local copies, waits for them, and re-layouts: 5.11 us -> 3.75 us
    ppermute x0 -> x7, starting transfers between devices: none -> 12.5 us  [shards(): lax.ppermute(half, 'row', [(r, r ^ m) for r in range(count)])]
    all_to_all x1 -> x0, starting transfers between devices: 7.25 us -> none  [gathered(): return lax.all_to_all(spread, axis, split_axis=0, concat_axis=0, tiled=True)]
    all_to_all x1 -> x0, waiting for transfers between devices: 3.86 us -> none  [gathered(): return lax.all_to_all(spread, axis, split_axis=0, concat_axis=0, tiled=True)]
    pallas_call x1, Pallas kernels: 2.65 us -> 3.43 us  [shards(): pl.pallas_call(functools.partial(tri_kernel, group=group), out_shape=(tri...]
    broadcast_in_dim x2 -> x0, local copies, waits for them, and re-layouts: 0.75 us -> none  [gathered(): spread = jnp.broadcast_to(half[None], (count,) + half.shape)]
    pallas_call x1 -> x0, local copies, waits for them, and re-layouts: 0.62 us -> none  [shards(): pl.pallas_call(functools.partial(last_kernel, owner_side=lambda row: row...]
    pallas_call x1, Pallas kernels: 0.32 us -> 0.93 us  [shards(): pl.pallas_call(functools.partial(last_kernel, owner_side=lambda row: row...]
  transfers between devices with their start and end apart: 2 -> 8, of which waited for: 2 -> 1; matrix products, arithmetic and copies ran while one was open for 0% -> 0% of each run, Pallas kernels for 10% -> 9%
where the time goes in v2:
time: 25.4 us; the launch traced here: 25 us
  starting transfers between devices  12.5 us (49%)
  Pallas kernels  6.6 us (26%)
  local copies, waits for them, and re-layouts  3.75 us (15%)
  waiting for transfers between devices  1.38 us (5%)
  between operations  0.79 us (3%)
    ppermute x7, starting transfers between devices, shards(): lax.ppermute(half, 'row', [(r, r ^ m) for r in range(count)])  12.5 us
    unnamed x16, local copies, waits for them, and re-layouts  3.75 us
    pallas_call x1, Pallas kernels, shards(): pl.pallas_call(functools.partial(tri_kernel, group=group), out_shape=(tri...  3.43 us
    pallas_call x1, Pallas kernels, shards(): pl.pallas_call(right_kernel, out_shape=jax.ShapeDtypeStruct((rows_dev, ha...  2.24 us
    ppermute x1, waiting for transfers between devices, shards(): got = lax.ppermute(send, 'col', [(0, 1), (1, 0)])  1.36 us
    pallas_call x1, Pallas kernels, shards(): pl.pallas_call(functools.partial(last_kernel, owner_side=lambda row: row...  0.93 us
  transfers between devices with their start and end apart: 8, of which 1 were waited for; matrix products, arithmetic and copies ran while one was open for 0% of the time, Pallas kernels for 9%

profile of v2, /device:TPU:0, one launch (start us, length us, event | category | flops | bytes accessed | tf_op | source)
XLA Modules:
  0.0 25.0 jit_solution(8489440356484315563)
XLA Ops:
  0.0 0.0 copy-start
  0.0 0.9 %copy-done = bf16[1,288,128]{2,1,0:T(8,128)(2,1)S(1)} copy-done((bf16[1,288,128]{2,1,0:T(8,128)(2,1)S(1)}, bf16[1,288,128]{2,1,0:T(8,128)(2,1)}, u32[]{:S(2)}) %copy-start) | copy-done | bytes 73752
  0.9 6.0 %collective-permute-start.6 = (bf16[1,144,128]{2,1,0:T(8,128)(2,1)S(1)}, bf16[1,144,128]{2,1,0:T(8,128)(2,1)S(1)}, u32[]{:S(2)}, u32[]{:S(2)}) collective-permute-start(bf16[1,144,128]{2,1,0:T(8,128)(2,1)S(1)} %constant_dynamic-slice_fusion.refs_0_), channel_id=1, source_target_pairs={{0,14},{2,12},{4,10},{6,8},{8,6},{10,4},{12,2},{14,0},{1,15},{3,13... | collective-permute-start | bytes 110600 | tf_op jit(solution)/shard_map/ppermute | solution.py:171
  6.9 0.2 collective-permute-start.5
  7.1 0.8 %collective-permute-start.4 = (bf16[1,144,128]{2,1,0:T(8,128)(2,1)S(1)}, bf16[1,144,128]{2,1,0:T(8,128)(2,1)S(1)}, u32[]{:S(2)}, u32[]{:S(2)}) collective-permute-start(bf16[1,144,128]{2,1,0:T(8,128)(2,1)S(1)} %constant_dynamic-slice_fusion.refs_0_), channel_id=1, source_target_pairs={{0,10},{2,8},{4,14},{6,12},{8,2},{10,0},{12,6},{14,4},{1,11},{3,9}... | collective-permute-start | bytes 110600 | tf_op jit(solution)/shard_map/ppermute | solution.py:171
  7.9 1.9 %collective-permute-start.3 = (bf16[1,144,128]{2,1,0:T(8,128)(2,1)S(1)}, bf16[1,144,128]{2,1,0:T(8,128)(2,1)S(1)}, u32[]{:S(2)}, u32[]{:S(2)}) collective-permute-start(bf16[1,144,128]{2,1,0:T(8,128)(2,1)S(1)} %constant_dynamic-slice_fusion.refs_0_), channel_id=1, source_target_pairs={{0,8},{2,10},{4,12},{6,14},{8,0},{10,2},{12,4},{14,6},{1,9},{3,11}... | collective-permute-start | bytes 110600 | tf_op jit(solution)/shard_map/ppermute | solution.py:171
  9.8 2.4 %collective-permute-start.2 = (bf16[1,144,128]{2,1,0:T(8,128)(2,1)S(1)}, bf16[1,144,128]{2,1,0:T(8,128)(2,1)S(1)}, u32[]{:S(2)}, u32[]{:S(2)}) collective-permute-start(bf16[1,144,128]{2,1,0:T(8,128)(2,1)S(1)} %constant_dynamic-slice_fusion.refs_0_), channel_id=1, source_target_pairs={{0,6},{2,4},{4,2},{6,0},{8,14},{10,12},{12,10},{14,8},{1,7},{3,5},... | collective-permute-start | bytes 110600 | tf_op jit(solution)/shard_map/ppermute | solution.py:171
  12.8 0.0 copy-start.1
  12.8 0.0 copy-start.2
  12.8 0.0 copy-start.3
  12.8 0.0 collective-permute-done.6.refs_7_
  12.9 0.8 %collective-permute-start.1 = (bf16[1,144,128]{2,1,0:T(8,128)(2,1)S(1)}, bf16[1,144,128]{2,1,0:T(8,128)(2,1)S(1)}, u32[]{:S(2)}, u32[]{:S(2)}) collective-permute-start(bf16[1,144,128]{2,1,0:T(8,128)(2,1)S(1)} %constant_dynamic-slice_fusion.refs_0_), channel_id=1, source_target_pairs={{0,4},{2,6},{4,0},{6,2},{8,12},{10,14},{12,8},{14,10},{1,5},{3,7},... | collective-permute-start | bytes 110600 | tf_op jit(solution)/shard_map/ppermute | solution.py:171
  13.7 0.0 collective-permute-done.5.refs_6_
  13.7 0.3 %collective-permute-start = (bf16[1,144,128]{2,1,0:T(8,128)(2,1)S(1)}, bf16[1,144,128]{2,1,0:T(8,128)(2,1)S(1)}, u32[]{:S(2)}, u32[]{:S(2)}) collective-permute-start(bf16[1,144,128]{2,1,0:T(8,128)(2,1)S(1)} %constant_dynamic-slice_fusion.refs_0_), channel_id=1, source_target_pairs={{0,2},{2,0},{4,6},{6,4},{8,10},{10,8},{12,14},{14,12},{1,3},{3,1},... | collective-permute-start | bytes 110600 | tf_op jit(solution)/shard_map/ppermute | solution.py:171
  14.1 0.0 copy-start.5
  14.1 1.3 %copy-done.5 = bf16[36,144,128]{2,1,0:T(8,128)(2,1)S(1)} copy-done((bf16[36,144,128]{2,1,0:T(8,128)(2,1)S(1)}, bf16[36,144,128]{2,1,0:T(8,128)(2,1)}, u32[]{:S(2)}) %copy-start.5) | copy-done | bytes 1327128
  15.4 0.0 copy-start.6
  15.4 0.8 %copy-done.6 = bf16[128,128]{1,0:T(8,128)(2,1)S(1)} copy-done((bf16[128,128]{1,0:T(8,128)(2,1)S(1)}, bf16[128,128]{1,0:T(8,128)(2,1)}, u32[]{:S(2)}) %copy-start.6) | copy-done | bytes 32792
  16.1 0.0 copy-start.7
  16.1 0.8 %copy-done.7 = bf16[128,128]{1,0:T(8,128)(2,1)S(1)} copy-done((bf16[128,128]{1,0:T(8,128)(2,1)S(1)}, bf16[128,128]{1,0:T(8,128)(2,1)}, u32[]{:S(2)}) %copy-start.7) | copy-done | bytes 32792
  16.9 2.2 %right.1.right_ref = bf16[36,144,128]{2,1,0:T(8,128)(2,1)S(1)} custom-call(s32[1]{0:T(128)S(6)} %copy.10.length_ref, bf16[36,144,128]{2,1,0:T(8,128)(2,1)S(1)} %copy-done.5, bf16[128,128]{1,0:T(8,128)(2,1)S(1)} %copy-done.6, bf16[128,128]{1,0:T(8,128)(2,1)S(1)} %copy-done.7), custom_call_target="tpu_custom_call" | custom-call | flops 1019215872 | bytes 2654208 | tf_op jit(solution)/shard_map/right/pallas_call | solution.py:175
  19.1 0.0 copy-start.4
  19.2 0.0 collective-permute-done.4.refs_5_
  19.2 0.0 collective-permute-done.3.refs_4_
  19.2 0.0 collective-permute-done.2.refs_3_
  19.2 0.0 collective-permute-done.1.refs_2_
  19.2 0.0 collective-permute-done.refs_1_
  19.2 0.0 copy-done.1
  19.2 0.0 copy-done.2
  19.2 0.0 copy-done.3
  19.2 3.4 %tri.1 = (f32[2,144,128]{2,1,0:T(8,128)S(1)}, f32[2,144,128]{2,1,0:T(8,128)S(1)}) custom-call(s32[1]{0:T(128)S(6)} %copy.10.length_ref, bf16[36,144,128]{2,1,0:T(8,128)(2,1)S(1)} %right.1.right_ref, bf16[128,128]{1,0:T(8,128)(2,1)S(1)} %copy-done.1, bf16[128,128]{1,0:T(8,128)(2,1)S(1)} %copy-done.2, bf16[128,128]{1,0:T(8,128)(2,1)S(1)} %copy-done.3, ...), custom_call_target="tpu_custom_call" | custom-call | flops 10616832 | bytes 1327104 | tf_op jit(solution)/shard_map/tri/pallas_call | solution.py:206
  22.7 0.1 collective-permute-start.7
  22.8 1.4 %collective-permute-done.7.got_ref = f32[2,144,128]{2,1,0:T(8,128)S(1)} collective-permute-done((f32[2,144,128]{2,1,0:T(8,128)S(1)}, f32[2,144,128]{2,1,0:T(8,128)S(1)}, u32[]{:S(2)}, u32[]{:S(2)}) %collective-permute-start.7) | collective-permute-done | bytes 147488 | tf_op jit(solution)/shard_map/ppermute | solution.py:232
  24.1 0.0 copy-done.4
  24.1 0.9 %last.1 = bf16[18,8,128]{2,1,0:T(8,128)(2,1)} custom-call(f32[2,144,128]{2,1,0:T(8,128)S(1)} %get-tuple-element.7.keep_ref, f32[2,144,128]{2,1,0:T(8,128)S(1)} %collective-permute-done.7.got_ref, bf16[128,128]{1,0:T(8,128)(2,1)S(1)} %copy-done.4), custom_call_target="tpu_custom_call" | custom-call | tf_op jit(solution)/shard_map/last/pallas_call | solution.py:234
  (1 shorter events, 0.0 us)
Async XLA Ops:
  0.0 0.9 %copy-start = (bf16[1,288,128]{2,1,0:T(8,128)(2,1)S(1)}, bf16[1,288,128]{2,1,0:T(8,128)(2,1)}, u32[]{:S(2)}) copy-start(bf16[1,288,128]{2,1,0:T(8,128)(2,1)} %param.10) | copy-start | bytes 221188
  0.9 12.0 %collective-permute-start.6 = (bf16[1,144,128]{2,1,0:T(8,128)(2,1)S(1)}, bf16[1,144,128]{2,1,0:T(8,128)(2,1)S(1)}, u32[]{:S(2)}, u32[]{:S(2)}) collective-permute-start(bf16[1,144,128]{2,1,0:T(8,128)(2,1)S(1)} %constant_dynamic-slice_fusion.refs_0_), channel_id=1, source_target_pairs={{0,14},{2,12},{4,10},{6,8},{8,6},{10,4},{12,2},{14,0},{1,15},{3,13... | collective-permute-start | bytes 110600 | tf_op jit(solution)/shard_map/ppermute | solution.py:171
  6.9 6.8 %collective-permute-start.5 = (bf16[1,144,128]{2,1,0:T(8,128)(2,1)S(1)}, bf16[1,144,128]{2,1,0:T(8,128)(2,1)S(1)}, u32[]{:S(2)}, u32[]{:S(2)}) collective-permute-start(bf16[1,144,128]{2,1,0:T(8,128)(2,1)S(1)} %constant_dynamic-slice_fusion.refs_0_), channel_id=1, source_target_pairs={{0,12},{2,14},{4,8},{6,10},{8,4},{10,6},{12,0},{14,2},{1,13},{3,15... | collective-permute-start | bytes 110600 | tf_op jit(solution)/shard_map/ppermute | solution.py:171
  7.1 12.1 %collective-permute-start.4 = (bf16[1,144,128]{2,1,0:T(8,128)(2,1)S(1)}, bf16[1,144,128]{2,1,0:T(8,128)(2,1)S(1)}, u32[]{:S(2)}, u32[]{:S(2)}) collective-permute-start(bf16[1,144,128]{2,1,0:T(8,128)(2,1)S(1)} %constant_dynamic-slice_fusion.refs_0_), channel_id=1, source_target_pairs={{0,10},{2,8},{4,14},{6,12},{8,2},{10,0},{12,6},{14,4},{1,11},{3,9}... | collective-permute-start | bytes 110600 | tf_op jit(solution)/shard_map/ppermute | solution.py:171
  7.9 11.3 %collective-permute-start.3 = (bf16[1,144,128]{2,1,0:T(8,128)(2,1)S(1)}, bf16[1,144,128]{2,1,0:T(8,128)(2,1)S(1)}, u32[]{:S(2)}, u32[]{:S(2)}) collective-permute-start(bf16[1,144,128]{2,1,0:T(8,128)(2,1)S(1)} %constant_dynamic-slice_fusion.refs_0_), channel_id=1, source_target_pairs={{0,8},{2,10},{4,12},{6,14},{8,0},{10,2},{12,4},{14,6},{1,9},{3,11}... | collective-permute-start | bytes 110600 | tf_op jit(solution)/shard_map/ppermute | solution.py:171
  9.8 9.4 %collective-permute-start.2 = (bf16[1,144,128]{2,1,0:T(8,128)(2,1)S(1)}, bf16[1,144,128]{2,1,0:T(8,128)(2,1)S(1)}, u32[]{:S(2)}, u32[]{:S(2)}) collective-permute-start(bf16[1,144,128]{2,1,0:T(8,128)(2,1)S(1)} %constant_dynamic-slice_fusion.refs_0_), channel_id=1, source_target_pairs={{0,6},{2,4},{4,2},{6,0},{8,14},{10,12},{12,10},{14,8},{1,7},{3,5},... | collective-permute-start | bytes 110600 | tf_op jit(solution)/shard_map/ppermute | solution.py:171
  12.8 6.4 %copy-start.1 = (bf16[128,128]{1,0:T(8,128)(2,1)S(1)}, bf16[128,128]{1,0:T(8,128)(2,1)}, u32[]{:S(2)}) copy-start(bf16[128,128]{1,0:T(8,128)(2,1)} %gate_ref.3) | copy-start | bytes 98308
  12.8 6.4 %copy-start.2 = (bf16[128,128]{1,0:T(8,128)(2,1)S(1)}, bf16[128,128]{1,0:T(8,128)(2,1)}, u32[]{:S(2)}) copy-start(bf16[128,128]{1,0:T(8,128)(2,1)} %weight_ref.4) | copy-start | bytes 98308
  12.8 6.4 %copy-start.3 = (bf16[128,128]{1,0:T(8,128)(2,1)S(1)}, bf16[128,128]{1,0:T(8,128)(2,1)}, u32[]{:S(2)}) copy-start(bf16[128,128]{1,0:T(8,128)(2,1)} %out_gate_ref.1) | copy-start | bytes 98308
  12.9 6.3 %collective-permute-start.1 = (bf16[1,144,128]{2,1,0:T(8,128)(2,1)S(1)}, bf16[1,144,128]{2,1,0:T(8,128)(2,1)S(1)}, u32[]{:S(2)}, u32[]{:S(2)}) collective-permute-start(bf16[1,144,128]{2,1,0:T(8,128)(2,1)S(1)} %constant_dynamic-slice_fusion.refs_0_), channel_id=1, source_target_pairs={{0,4},{2,6},{4,0},{6,2},{8,12},{10,14},{12,8},{14,10},{1,5},{3,7},... | collective-permute-start | bytes 110600 | tf_op jit(solution)/shard_map/ppermute | solution.py:171
  13.7 5.5 %collective-permute-start = (bf16[1,144,128]{2,1,0:T(8,128)(2,1)S(1)}, bf16[1,144,128]{2,1,0:T(8,128)(2,1)S(1)}, u32[]{:S(2)}, u32[]{:S(2)}) collective-permute-start(bf16[1,144,128]{2,1,0:T(8,128)(2,1)S(1)} %constant_dynamic-slice_fusion.refs_0_), channel_id=1, source_target_pairs={{0,2},{2,0},{4,6},{6,4},{8,10},{10,8},{12,14},{14,12},{1,3},{3,1},... | collective-permute-start | bytes 110600 | tf_op jit(solution)/shard_map/ppermute | solution.py:171
  14.1 1.3 %copy-start.5 = (bf16[36,144,128]{2,1,0:T(8,128)(2,1)S(1)}, bf16[36,144,128]{2,1,0:T(8,128)(2,1)}, u32[]{:S(2)}) copy-start(bf16[36,144,128]{2,1,0:T(8,128)(2,1)} %pair_ref.1) | copy-start | bytes 3981316
  15.4 0.8 %copy-start.6 = (bf16[128,128]{1,0:T(8,128)(2,1)S(1)}, bf16[128,128]{1,0:T(8,128)(2,1)}, u32[]{:S(2)}) copy-start(bf16[128,128]{1,0:T(8,128)(2,1)} %gate_ref.2) | copy-start | bytes 98308
  16.1 0.8 %copy-start.7 = (bf16[128,128]{1,0:T(8,128)(2,1)S(1)}, bf16[128,128]{1,0:T(8,128)(2,1)}, u32[]{:S(2)}) copy-start(bf16[128,128]{1,0:T(8,128)(2,1)} %weight_ref.3) | copy-start | bytes 98308
  19.1 5.0 %copy-start.4 = (bf16[128,128]{1,0:T(8,128)(2,1)S(1)}, bf16[128,128]{1,0:T(8,128)(2,1)}, u32[]{:S(2)}) copy-start(bf16[128,128]{1,0:T(8,128)(2,1)} %weight_ref.5) | copy-start | bytes 98308
  22.7 1.4 %collective-permute-start.7 = (f32[2,144,128]{2,1,0:T(8,128)S(1)}, f32[2,144,128]{2,1,0:T(8,128)S(1)}, u32[]{:S(2)}, u32[]{:S(2)}) collective-permute-start(f32[2,144,128]{2,1,0:T(8,128)S(1)} %get-tuple-element.8), channel_id=1, source_target_pairs={{0,1},{1,0},{2,3},{3,2},{4,5},{5,4},{6,7},{7,6},{8,9},{9,8},{10,11... | collective-permute-start | bytes 442376 | tf_op jit(solution)/shard_map/ppermute | solution.py:232

commit v3 on v2

v3 whole, which is shorter than its diff:
```python
import functools

import jax
import jax.numpy as jnp
from jax import lax
from jax.experimental import pallas as pl
from jax.experimental.pallas import tpu as pltpu
from jax.sharding import PartitionSpec as P

EPS = 1e-05
F32 = jnp.float32
BF16 = jnp.bfloat16
QUAD = 4
GATE_ROWS = 40


def divisor(total, limit, step=1):
    return max(d for d in range(step, total + 1, step) if total % d == 0 and (d <= limit or d == step))


def doubling(count):
    bits = [1 << b for b in reversed(range(count.bit_length() - 1))]
    return bits, bits[-1:] + bits[:-1]


def slots(steps):
    held = [0]
    for step in steps:
        held = held + [m ^ step for m in held]
    return held


def centering(width):
    row = lax.broadcasted_iota(jnp.int32, (2 * width, 2 * width), 0)
    col = lax.broadcasted_iota(jnp.int32, (2 * width, 2 * width), 1)
    share = jnp.where((row < width) == (col < width), 1.0 / width, 0.0)
    center = jnp.where(row == col, 1.0, 0.0) - share
    return center.astype(BF16), share.astype(BF16)


def normed(first, second, center, share):
    wide = jnp.concatenate([first, second], axis=1)
    d = jnp.dot(wide, center, preferred_element_type=F32)
    var = jnp.dot((d * d).astype(BF16), share, preferred_element_type=F32)
    return (d * lax.rsqrt(var + EPS)).astype(BF16)


def gated(n, both):
    width = both.shape[1] // 2
    y = jnp.dot(n, both, preferred_element_type=F32)
    value = y[:, width:]
    return value + value * jnp.tanh(y[:, :width])


def pair_weights(gate_ref, weight_ref):
    half = jnp.asarray(0.5, BF16)
    return jnp.concatenate([gate_ref[...] * half, weight_ref[...] * half], axis=1)


def right_kernel(length_ref, pair_ref, gate_ref, weight_ref, out_ref, *, flip):
    rows, cols, width = pair_ref.shape
    half_rows = rows * pl.num_programs(0)
    live = length_ref[0]
    side = lax.axis_index("col")
    j_half = 1 - side if flip else side
    first_k = side * cols
    first_j = lax.axis_index("row") * 2 * half_rows + j_half * half_rows + pl.program_id(0) * rows
    center, share = centering(width)
    both = pair_weights(gate_ref, weight_ref)
    x = pair_ref[...].reshape(2, rows * cols // 2, width)
    n = normed(x[0], x[1], center, share)
    k = first_k + lax.broadcasted_iota(jnp.int32, (cols, width), 0)
    for part in range(2):
        edge = gated(n[:, part * width : (part + 1) * width], both).reshape(rows // 2, cols, width)
        for r in range(rows // 2):
            j = part * (rows // 2) + r
            reach = jnp.where(first_j + j < live, live, 0)
            out_ref[j] = jnp.where(k < reach, edge[r], 0.0).astype(BF16)


def fold(parts):
    place = lax.broadcasted_iota(jnp.int32, parts[0].shape, 0)
    for step in (1, 2, 4):
        here = (place & step) == 0
        parts = [
            jnp.where(here, a, b) + pltpu.roll(jnp.where(here, b, a), 8 - step, 0)
            for a, b in zip(parts[0::2], parts[1::2])
        ]
    return parts[0]


def project(length_ref, slab_ref, gate_ref, weight_ref, out_gate_ref, left_ref, gates_ref, norm_ref, half_rows):
    slabs, depth, width = slab_ref.shape
    k_step = pl.program_id(0)
    half_cols = depth * pl.num_programs(0)
    center, share = centering(width)
    both = pair_weights(gate_ref, weight_ref)
    first_k = lax.axis_index("col") * half_cols + k_step * depth
    live = first_k + lax.broadcasted_iota(jnp.int32, (depth, width), 0) < length_ref[0]
    first_j = lax.rem(lax.axis_index("row") * (2 * half_rows), half_cols)
    start = lax.rem(first_j, depth)

    def pair(s):
        n = normed(slab_ref[s], slab_ref[s + 1], center, share)
        for part in range(2):
            norm_ref[pl.ds(part * (depth + GATE_ROWS), depth), :] = n[:, part * width : (part + 1) * width].astype(F32)
            edge = gated(n[:, part * width : (part + 1) * width], both)
            left_ref[s + part] = jnp.where(live, edge, 0.0).astype(BF16).astype(left_ref.dtype)

        @pl.when(k_step == first_j // depth)
        def _():
            own = [norm_ref[pl.ds(start + part * (depth + GATE_ROWS), GATE_ROWS), :] for part in range(2)]
            rows = jnp.concatenate(own, axis=0).astype(BF16)
            y = jnp.dot(rows, out_gate_ref[...] * jnp.asarray(0.5, BF16), preferred_element_type=F32)
            gate = (0.5 + 0.5 * jnp.tanh(y)).astype(BF16).astype(F32)
            gates_ref[pl.ds(pl.multiple_of(s * GATE_ROWS, 8), 2 * GATE_ROWS), :] = gate

    if slabs <= 8:
        for s in range(0, slabs, 2):
            pair(s)
    else:
        pl.loop(0, slabs, step=2)(pair)


def contract(left_ref, right_ref, sums_ref):
    slabs, depth, _ = left_ref.shape
    rows = right_ref.shape[0]
    group = divisor(rows, 6, 2)

    def tile(turn, _):
        q = turn // (rows // group)
        j0 = lax.rem(turn, rows // group) * group
        sums = [[None] * QUAD for _ in range(group)]
        for k0 in range(0, depth, 16):
            edges = [right_ref[j0 + j, pl.ds(k0, 16), :].astype(F32) for j in range(group)]
            for n in range(QUAD):
                left = left_ref[q * QUAD + n, pl.ds(k0, 16), :].astype(F32)
                for j in range(group):
                    term = left * edges[j]
                    term = term[:8] + term[8:]
                    sums[j][n] = term if k0 == 0 else sums[j][n] + term
        for j in range(0, group, 2):
            dest = sums_ref.at[q, pl.ds(pl.multiple_of((j0 + j) * QUAD, 8), 8), :]
            total = fold(sums[j] + sums[j + 1])
            dest[...] = jnp.where(pl.program_id(0) == 0, total, total + dest[...])
        return 0

    lax.fori_loop(0, slabs // QUAD * (rows // group), tile, 0)


def assemble(dest_ref, sums_ref, gates_ref, steps, last, j_half):
    half_rows = sums_ref.shape[1] // QUAD
    count = dest_ref.shape[1] // half_rows
    side, place = lax.axis_index("col"), lax.axis_index("row")
    for n, (m0, m1) in enumerate(zip(*(slots(s[:-1]) for s in steps))):
        if last:
            m0, m1 = m0 ^ steps[0][-1], m1 ^ steps[1][-1]
        i = jnp.bitwise_xor(place, jnp.where(side == 0, m0, m1))
        rows = pl.ds(i, half_rows, stride=count)
        dest_ref[0, rows, :] = sums_ref[n // QUAD, pl.ds(n % QUAD, half_rows, stride=QUAD), :]
        dest_ref[1, rows, :] = gates_ref[pl.ds(n * GATE_ROWS + j_half * half_rows, half_rows), :]


def near_kernel(
    length_ref, mate_ref, own_ref, slab_ref, gate_ref, weight_ref, out_gate_ref,
    mate_sums_ref, own_sums_ref, gates_ref, left_ref, norm_ref,
):
    project(
        length_ref, slab_ref, gate_ref, weight_ref, out_gate_ref, left_ref, gates_ref, norm_ref, mate_ref.shape[0]
    )
    contract(left_ref, mate_ref, mate_sums_ref)
    contract(left_ref, own_ref, own_sums_ref)


def send_kernel(
    length_ref, mate_ref, slab_ref, gate_ref, weight_ref, out_gate_ref, near_sums_ref, near_gates_ref,
    send_ref, left_ref, gates_ref, sums_ref, norm_ref, *, steps,
):
    project(
        length_ref, slab_ref, gate_ref, weight_ref, out_gate_ref, left_ref, gates_ref, norm_ref, mate_ref.shape[0]
    )
    contract(left_ref, mate_ref, sums_ref)

    @pl.when(pl.program_id(0) == pl.num_programs(0) - 1)
    def _():
        flip = 1 - lax.axis_index("col")
        assemble(send_ref, near_sums_ref, near_gates_ref, steps, False, flip)
        assemble(send_ref, sums_ref, gates_ref, steps, True, flip)


def keep_kernel(
    own_ref, left_ref, gates_ref, near_sums_ref, near_gates_ref, keep_ref, sums_ref, *, steps
):
    contract(left_ref, own_ref, sums_ref)

    @pl.when(pl.program_id(0) == pl.num_programs(0) - 1)
    def _():
        side = lax.axis_index("col")
        assemble(keep_ref, near_sums_ref, near_gates_ref, steps, False, side)
        assemble(keep_ref, sums_ref, gates_ref, steps, True, side)


def last_kernel(keep_ref, got_ref, weight_ref, out_ref, *, half_cols):
    rows_dev = 2 * out_ref.shape[0]
    tri = keep_ref[0] + got_ref[0]
    d = tri - jnp.mean(tri, axis=-1, keepdims=True)
    var = jnp.mean(d * d, axis=-1, keepdims=True)
    n = (d * lax.rsqrt(var + EPS)).astype(BF16)
    projected = jnp.dot(n, weight_ref[...], preferred_element_type=F32)
    mine = lax.axis_index("row") * rows_dev // half_cols == lax.axis_index("col")
    update = projected * jnp.where(mine, keep_ref[1], got_ref[1])
    out_ref[...] = update.astype(BF16).reshape(out_ref.shape)


def shards(pair_rep, slab_rep, length, weight_a, gate_a, weight_b, gate_b, weight_gate, weight_out):
    rows_dev, half_cols, width = pair_rep.shape
    hidden = weight_a.shape[1]
    count = lax.axis_size("row")
    side = lax.axis_index("col")
    half_rows = rows_dev // 2
    steps = doubling(count)
    depth = divisor(half_cols, 144, rows_dev)
    blocks = half_cols // depth
    near = count // 2
    smem = pl.BlockSpec(memory_space=pltpu.SMEM)
    vmem = pl.BlockSpec(memory_space=pltpu.VMEM)
    params = pltpu.CompilerParams(vmem_limit_bytes=48 << 20)

    def whole(*shape):
        return pl.BlockSpec(shape, lambda *_: (0,) * len(shape))

    def deep(*shape):
        return pl.BlockSpec(shape, lambda k: (0, k, 0))

    def passed(x, step):
        pairs = []
        for row in range(count):
            for core in range(2):
                pairs.append((row * 2 + core, (row ^ steps[core][step]) * 2 + core))
        return lax.ppermute(x, ("row", "col"), pairs)

    def right_half(pair, flip):
        rows_step = divisor(half_rows, max(2, 1728 // half_cols), 2)
        turns = half_rows // rows_step

        def block(s):
            return ((1 - lax.axis_index("col") if flip else lax.axis_index("col")) * turns + s, 0, 0)

        return pl.pallas_call(
            functools.partial(right_kernel, flip=flip),
            out_shape=jax.ShapeDtypeStruct((half_rows, half_cols, hidden), BF16),
            grid=(turns,),
            in_specs=[
                smem,
                pl.BlockSpec((rows_step, half_cols, width), block),
                whole(width, hidden),
                whole(width, hidden),
            ],
            out_specs=pl.BlockSpec((rows_step, half_cols, hidden), lambda s: (s, 0, 0)),
            compiler_params=pltpu.CompilerParams(vmem_limit_bytes=60 << 20),
            cost_estimate=pl.CostEstimate(
                flops=2 * half_rows * half_cols * width * hidden * 6,
                bytes_accessed=4 * half_rows * half_cols * width,
                transcendentals=2 * half_rows * half_cols * width,
            ),
            name="right_mate" if flip else "right_own",
        )(length, pair, gate_b, weight_b)

    sums = jax.ShapeDtypeStruct((near // QUAD, half_rows * QUAD, hidden), F32)
    gates = jax.ShapeDtypeStruct((near * GATE_ROWS, width), F32)
    swapped = jax.ShapeDtypeStruct((2, half_rows * count, hidden), F32)
    norm = pltpu.VMEM((2 * (depth + GATE_ROWS), width), F32)
    cost = pl.CostEstimate(
        flops=2 * rows_dev * half_cols * near * hidden,
        bytes_accessed=2 * rows_dev * half_cols * width,
        transcendentals=near * half_cols * width,
    )

    held = lax.dynamic_slice_in_dim(slab_rep, side * half_cols, half_cols, 1)
    right = []
    got = None
    for step in range(len(steps[0])):
        if step > 0:
            held = jnp.concatenate([held, got], axis=0)
        if len(right) < step and len(right) < 2:
            made, held = lax.optimization_barrier((right_half(pair_rep, not right), held))
            right.append(made)
        got = passed(held, step)
    right_mate, right_own = right

    near_mate, near_own, near_gates = pl.pallas_call(
        near_kernel,
        out_shape=(sums, sums, gates),
        grid=(blocks,),
        in_specs=[
            smem,
            deep(half_rows, depth, hidden),
            deep(half_rows, depth, hidden),
            deep(near, depth, width),
            whole(width, hidden),
            whole(width, hidden),
            whole(width, width),
        ],
        out_specs=(whole(*sums.shape), whole(*sums.shape), whole(*gates.shape)),
        scratch_shapes=[pltpu.VMEM((near, depth, hidden), F32), norm],
        compiler_params=params,
        cost_estimate=cost,
        name="near",
    )(length, right_mate, right_own, held, gate_a, weight_a, weight_gate)

    send, left, far_gates = pl.pallas_call(
        functools.partial(send_kernel, steps=steps),
        out_shape=(swapped, jax.ShapeDtypeStruct((near, half_cols, hidden), BF16), gates),
        grid=(blocks,),
        in_specs=[
            smem,
            deep(half_rows, depth, hidden),
            deep(near, depth, width),
            whole(width, hidden),
            whole(width, hidden),
            whole(width, width),
            whole(*sums.shape),
            whole(*gates.shape),
        ],
        out_specs=(whole(*swapped.shape), deep(near, depth, hidden), whole(*gates.shape)),
        scratch_shapes=[pltpu.VMEM(sums.shape, F32), norm],
        compiler_params=params,
        name="send",
    )(length, right_mate, got, gate_a, weight_a, weight_gate, near_mate, near_gates)

    swap = lax.ppermute(send, "col", [(0, 1), (1, 0)])

    keep = pl.pallas_call(
        functools.partial(keep_kernel, steps=steps),
        out_shape=swapped,
        grid=(blocks,),
        in_specs=[
            deep(half_rows, depth, hidden),
            deep(near, depth, hidden),
            whole(*gates.shape),
            whole(*sums.shape),
            whole(*gates.shape),
        ],
        out_specs=whole(*swapped.shape),
        scratch_shapes=[pltpu.VMEM(sums.shape, F32)],
        compiler_params=params,
        cost_estimate=cost,
        name="keep",
    )(right_own, left, far_gates, near_own, near_gates)

    update = pl.pallas_call(
        functools.partial(last_kernel, half_cols=half_cols),
        out_shape=jax.ShapeDtypeStruct((half_rows, count, width), BF16),
        in_specs=[vmem, vmem, vmem],
        out_specs=vmem,
        compiler_params=pltpu.CompilerParams(vmem_limit_bytes=32 << 20),
        name="last",
    )(keep, swap, weight_out)
    return jnp.transpose(update, (1, 0, 2))


def solution(mesh):
    placed = (
        P(("groups", "row"), "col", None),
        P(("groups", "row"), None, None),
        P("groups"),
        P(),
        P(),
        P(),
        P(),
        P(),
        P(),
    )
    return jax.shard_map(
        shards,
        mesh=mesh,
        in_specs=placed,
        out_specs=P("groups", ("row", "col"), None),
        check_vma=False,
    )
```

time: 25.4 us -> 24.4 us (0.961)
  Pallas kernels: 6.6 us -> 12.8 us
  starting transfers between devices: 12.5 us -> 7.3 us
  local copies, waits for them, and re-layouts: 3.75 us -> 1.99 us
    pallas_call x3 -> x6, Pallas kernels: 6.6 us -> 12.8 us  [the longest x2 7.48 us: right_half(): pl.pallas_call(functools.partial(right_kernel, flip=flip), out_shape=jax....]
    ppermute x8 -> x4, starting transfers between devices: 12.5 us -> 7.3 us  [the longest x3 7.23 us: passed(): return lax.ppermute(x, ('row', 'col'), pairs)]
    unnamed x16 -> x14, local copies, waits for them, and re-layouts: 3.75 us -> 1.99 us
    ppermute x8 -> x4, waiting for transfers between devices: 1.38 us -> 1.24 us  [the longest x1 0.83 us: shards(): swap = lax.ppermute(send, 'col', [(0, 1), (1, 0)])]
  transfers between devices with their start and end apart: 8 -> 4, of which waited for: 1 -> 2; matrix products, arithmetic and copies ran while one was open for 0% -> 0% of each run, Pallas kernels for 9% -> 42%
where the time goes in v3:
time: 24.4 us; the launch traced here: 24.1 us
  Pallas kernels  12.8 us (52%)
  starting transfers between devices  7.3 us (30%)
  local copies, waits for them, and re-layouts  1.99 us (8%)
  waiting for transfers between devices  1.24 us (5%)
  between operations  0.74 us (3%)
    pallas_call x2, Pallas kernels, right_half(): pl.pallas_call(functools.partial(right_kernel, flip=flip), out_shape=jax....  7.48 us
    ppermute x3, starting transfers between devices, passed(): return lax.ppermute(x, ('row', 'col'), pairs)  7.23 us
    pallas_call x1, Pallas kernels, shards(): pl.pallas_call(near_kernel, out_shape=(sums, sums, gates), grid=(blocks,)...  2.13 us
    unnamed x14, local copies, waits for them, and re-layouts  1.99 us
    pallas_call x1, Pallas kernels, shards(): pl.pallas_call(functools.partial(send_kernel, steps=steps), out_shape=(sw...  1.73 us
    pallas_call x1, Pallas kernels, shards(): pl.pallas_call(functools.partial(last_kernel, half_cols=half_cols), out_s...  0.93 us
    ppermute x1, waiting for transfers between devices, shards(): swap = lax.ppermute(send, 'col', [(0, 1), (1, 0)])  0.83 us
    pallas_call x1, Pallas kernels, shards(): pl.pallas_call(functools.partial(keep_kernel, steps=steps), out_shape=swa...  0.52 us
  transfers between devices with their start and end apart: 4, of which 2 were waited for; matrix products, arithmetic and copies ran while one was open for 0% of the time, Pallas kernels for 42%

profile of v3, /device:TPU:0, one launch (start us, length us, event | category | flops | bytes accessed | tf_op | source)
XLA Modules:
  0.0 24.1 jit_solution(6488165565177676061)
XLA Ops:
  0.0 0.0 copy-start
  0.0 0.9 %copy-done = bf16[1,288,128]{2,1,0:T(8,128)(2,1)S(1)} copy-done((bf16[1,288,128]{2,1,0:T(8,128)(2,1)S(1)}, bf16[1,288,128]{2,1,0:T(8,128)(2,1)}, u32[]{:S(2)}) %copy-start) | copy-done | bytes 73752
  0.9 4.0 %collective-permute-start = (bf16[1,144,128]{2,1,0:T(8,128)(2,1)S(1)}, bf16[1,144,128]{2,1,0:T(8,128)(2,1)S(1)}, u32[]{:S(2)}, u32[]{:S(2)}) collective-permute-start(bf16[1,144,128]{2,1,0:T(8,128)(2,1)S(1)} %constant_dynamic-slice_fusion), channel_id=1, source_target_pairs={{0,8},{1,3},{2,10},{3,1},{4,12},{5,7},{6,14},{7,5},{8,0},{9,11},{1... | collective-permute-start | bytes 110600 | tf_op jit(solution)/shard_map/ppermute | solution.py:240
  5.6 3.8 %right_mate.1.mate_ref = bf16[18,144,128]{2,1,0:T(8,128)(2,1)} custom-call(s32[1]{0:T(128)S(6)} %copy.10.length_ref, bf16[36,144,128]{2,1,0:T(8,128)(2,1)} %pair_ref.3, bf16[128,128]{1,0:T(8,128)(2,1)} %gate_ref.5, bf16[128,128]{1,0:T(8,128)(2,1)} %weight_ref.6), custom_call_target="tpu_custom_call" | custom-call | flops 509607936 | bytes 1327104 | tf_op jit(solution)/shard_map/right_mate/pallas_call | solution.py:249
  9.3 0.0 copy-start.1
  9.3 0.0 copy-start.3
  9.3 0.0 copy-start.4
  9.3 0.0 copy-start.5
  9.4 0.0 collective-permute-done
  9.4 1.6 %collective-permute-start.1 = (bf16[2,144,128]{2,1,0:T(8,128)(2,1)S(1)}, bf16[2,144,128]{2,1,0:T(8,128)(2,1)S(1)}, u32[]{:S(2)}, u32[]{:S(2)}) collective-permute-start(bf16[2,144,128]{2,1,0:T(8,128)(2,1)S(1)} %pad_maximum_fusion.1), channel_id=1, source_target_pairs={{0,4},{1,9},{2,6},{3,11},{4,0},{5,13},{6,2},{7,15},{8,12},{9,1},{1... | collective-permute-start | bytes 221192 | tf_op jit(solution)/shard_map/ppermute | solution.py:240
  11.0 3.7 %right_own.1.own_ref = bf16[18,144,128]{2,1,0:T(8,128)(2,1)} custom-call(s32[1]{0:T(128)S(6)} %copy.10.length_ref, bf16[36,144,128]{2,1,0:T(8,128)(2,1)} %pair_ref.3, bf16[128,128]{1,0:T(8,128)(2,1)} %gate_ref.5, bf16[128,128]{1,0:T(8,128)(2,1)} %weight_ref.6), custom_call_target="tpu_custom_call" | custom-call | flops 509607936 | bytes 1327104 | tf_op jit(solution)/shard_map/right_own/pallas_call | solution.py:249
  14.8 0.0 collective-permute-done.1
  14.8 1.5 %collective-permute-start.2 = (bf16[4,144,128]{2,1,0:T(8,128)(2,1)S(1)}, bf16[4,144,128]{2,1,0:T(8,128)(2,1)S(1)}, u32[]{:S(2)}, u32[]{:S(2)}) collective-permute-start(bf16[4,144,128]{2,1,0:T(8,128)(2,1)S(1)} %pad_maximum_fusion.slab_ref), channel_id=1, source_target_pairs={{0,2},{1,5},{2,0},{3,7},{4,6},{5,1},{6,4},{7,3},{8,10},{9,13},{10,... | collective-permute-start | bytes 442376 | tf_op jit(solution)/shard_map/ppermute | solution.py:240
  16.3 0.0 copy-done.1
  16.3 0.0 copy-done.3
  16.3 0.0 copy-done.4
  16.3 0.0 copy-done.5
  16.3 0.0 copy-start.2
  16.3 1.1 %copy-done.2 = bf16[18,144,128]{2,1,0:T(8,128)(2,1)S(1)} copy-done((bf16[18,144,128]{2,1,0:T(8,128)(2,1)S(1)}, bf16[18,144,128]{2,1,0:T(8,128)(2,1)}, u32[]{:S(2)}) %copy-start.2) | copy-done | bytes 663576
  17.4 2.1 %near.1 = (f32[1,72,128]{2,1,0:T(8,128)S(1)}, f32[1,72,128]{2,1,0:T(8,128)S(1)}, f32[160,128]{1,0:T(8,128)S(1)}) custom-call(s32[1]{0:T(128)S(6)} %copy.10.length_ref, bf16[18,144,128]{2,1,0:T(8,128)(2,1)S(1)} %copy-done.1, bf16[18,144,128]{2,1,0:T(8,128)(2,1)S(1)} %copy-done.2, bf16[4,144,128]{2,1,0:T(8,128)(2,1)S(1)} %pad_maximum_fusion.slab_ref, ...), custom_call_target="tpu_custom_call" | custom-call | flops 5308416 | bytes 1327104 | tf_op jit(solution)/shard_map/near/pallas_call | solution.py:291
  19.6 0.0 copy-start.6
  19.6 0.4 %collective-permute-done.2.slab_ref = bf16[4,144,128]{2,1,0:T(8,128)(2,1)S(1)} collective-permute-done((bf16[4,144,128]{2,1,0:T(8,128)(2,1)S(1)}, bf16[4,144,128]{2,1,0:T(8,128)(2,1)S(1)}, u32[]{:S(2)}, u32[]{:S(2)}) %collective-permute-start.2) | collective-permute-done | bytes 147488 | tf_op jit(solution)/shard_map/ppermute | solution.py:240
  20.0 1.7 %send.1 = (f32[2,144,128]{2,1,0:T(8,128)S(1)}, bf16[4,144,128]{2,1,0:T(8,128)(2,1)S(1)}, f32[160,128]{1,0:T(8,128)S(1)}) custom-call(s32[1]{0:T(128)S(6)} %copy.10.length_ref, bf16[18,144,128]{2,1,0:T(8,128)(2,1)S(1)} %copy-done.1, bf16[4,144,128]{2,1,0:T(8,128)(2,1)S(1)} %collective-permute-done.2.slab_ref, bf16[128,128]{1,0:T(8,128)(2,1)S(1)} %copy-done.3, ...), custom_call_target="tpu_custom_call" | custom-call | tf_op jit(solution)/shard_map/send/pallas_call | solution.py:311
  21.7 0.1 collective-permute-start.3
  21.8 0.5 %keep.1.keep_ref = f32[2,144,128]{2,1,0:T(8,128)S(1)} custom-call(bf16[18,144,128]{2,1,0:T(8,128)(2,1)S(1)} %copy-done.2, bf16[4,144,128]{2,1,0:T(8,128)(2,1)S(1)} %get-tuple-element.21.left_ref, f32[160,128]{1,0:T(8,128)S(1)} %get-tuple-element.22.gates_ref, f32[1,72,128]{2,1,0:T(8,128)S(1)} %get-tuple-element.23.near_sums_ref, ...), custom_call_target="tpu_custom_call" | custom-call | flops 5308416 | bytes 1327104 | tf_op jit(solution)/shard_map/keep/pallas_call | solution.py:333
  22.3 0.8 %collective-permute-done.3.got_ref = f32[2,144,128]{2,1,0:T(8,128)S(1)} collective-permute-done((f32[2,144,128]{2,1,0:T(8,128)S(1)}, f32[2,144,128]{2,1,0:T(8,128)S(1)}, u32[]{:S(2)}, u32[]{:S(2)}) %collective-permute-start.3) | collective-permute-done | bytes 147488 | tf_op jit(solution)/shard_map/ppermute | solution.py:331
  23.2 0.0 copy-done.6
  23.2 0.9 %last.1 = bf16[18,8,128]{2,1,0:T(8,128)(2,1)} custom-call(f32[2,144,128]{2,1,0:T(8,128)S(1)} %keep.1.keep_ref, f32[2,144,128]{2,1,0:T(8,128)S(1)} %collective-permute-done.3.got_ref, bf16[128,128]{1,0:T(8,128)(2,1)S(1)} %copy-done.6), custom_call_target="tpu_custom_call" | custom-call | tf_op jit(solution)/shard_map/last/pallas_call | solution.py:351
  (3 shorter events, 0.0 us)
Async XLA Ops:
  0.0 0.9 %copy-start = (bf16[1,288,128]{2,1,0:T(8,128)(2,1)S(1)}, bf16[1,288,128]{2,1,0:T(8,128)(2,1)}, u32[]{:S(2)}) copy-start(bf16[1,288,128]{2,1,0:T(8,128)(2,1)} %param.10) | copy-start | bytes 221188
  0.9 8.5 %collective-permute-start = (bf16[1,144,128]{2,1,0:T(8,128)(2,1)S(1)}, bf16[1,144,128]{2,1,0:T(8,128)(2,1)S(1)}, u32[]{:S(2)}, u32[]{:S(2)}) collective-permute-start(bf16[1,144,128]{2,1,0:T(8,128)(2,1)S(1)} %constant_dynamic-slice_fusion), channel_id=1, source_target_pairs={{0,8},{1,3},{2,10},{3,1},{4,12},{5,7},{6,14},{7,5},{8,0},{9,11},{1... | collective-permute-start | bytes 110600 | tf_op jit(solution)/shard_map/ppermute | solution.py:240
  9.3 7.0 %copy-start.1 = (bf16[18,144,128]{2,1,0:T(8,128)(2,1)S(1)}, bf16[18,144,128]{2,1,0:T(8,128)(2,1)}, u32[]{:S(2)}) copy-start(bf16[18,144,128]{2,1,0:T(8,128)(2,1)} %right_mate.1.mate_ref) | copy-start | bytes 1990660
  9.3 7.0 %copy-start.3 = (bf16[128,128]{1,0:T(8,128)(2,1)S(1)}, bf16[128,128]{1,0:T(8,128)(2,1)}, u32[]{:S(2)}) copy-start(bf16[128,128]{1,0:T(8,128)(2,1)} %gate_ref.7) | copy-start | bytes 98308
  9.3 7.0 %copy-start.4 = (bf16[128,128]{1,0:T(8,128)(2,1)S(1)}, bf16[128,128]{1,0:T(8,128)(2,1)}, u32[]{:S(2)}) copy-start(bf16[128,128]{1,0:T(8,128)(2,1)} %weight_ref.8) | copy-start | bytes 98308
  9.3 7.0 %copy-start.5 = (bf16[128,128]{1,0:T(8,128)(2,1)S(1)}, bf16[128,128]{1,0:T(8,128)(2,1)}, u32[]{:S(2)}) copy-start(bf16[128,128]{1,0:T(8,128)(2,1)} %out_gate_ref.3) | copy-start | bytes 98308
  9.4 5.4 %collective-permute-start.1 = (bf16[2,144,128]{2,1,0:T(8,128)(2,1)S(1)}, bf16[2,144,128]{2,1,0:T(8,128)(2,1)S(1)}, u32[]{:S(2)}, u32[]{:S(2)}) collective-permute-start(bf16[2,144,128]{2,1,0:T(8,128)(2,1)S(1)} %pad_maximum_fusion.1), channel_id=1, source_target_pairs={{0,4},{1,9},{2,6},{3,11},{4,0},{5,13},{6,2},{7,15},{8,12},{9,1},{1... | collective-permute-start | bytes 221192 | tf_op jit(solution)/shard_map/ppermute | solution.py:240
  14.8 5.2 %collective-permute-start.2 = (bf16[4,144,128]{2,1,0:T(8,128)(2,1)S(1)}, bf16[4,144,128]{2,1,0:T(8,128)(2,1)S(1)}, u32[]{:S(2)}, u32[]{:S(2)}) collective-permute-start(bf16[4,144,128]{2,1,0:T(8,128)(2,1)S(1)} %pad_maximum_fusion.slab_ref), channel_id=1, source_target_pairs={{0,2},{1,5},{2,0},{3,7},{4,6},{5,1},{6,4},{7,3},{8,10},{9,13},{10,... | collective-permute-start | bytes 442376 | tf_op jit(solution)/shard_map/ppermute | solution.py:240
  16.3 1.1 %copy-start.2 = (bf16[18,144,128]{2,1,0:T(8,128)(2,1)S(1)}, bf16[18,144,128]{2,1,0:T(8,128)(2,1)}, u32[]{:S(2)}) copy-start(bf16[18,144,128]{2,1,0:T(8,128)(2,1)} %right_own.1.own_ref) | copy-start | bytes 1990660
  19.6 3.6 %copy-start.6 = (bf16[128,128]{1,0:T(8,128)(2,1)S(1)}, bf16[128,128]{1,0:T(8,128)(2,1)}, u32[]{:S(2)}) copy-start(bf16[128,128]{1,0:T(8,128)(2,1)} %weight_ref.9) | copy-start | bytes 98308
  21.7 1.4 %collective-permute-start.3 = (f32[2,144,128]{2,1,0:T(8,128)S(1)}, f32[2,144,128]{2,1,0:T(8,128)S(1)}, u32[]{:S(2)}, u32[]{:S(2)}) collective-permute-start(f32[2,144,128]{2,1,0:T(8,128)S(1)} %get-tuple-element.24), channel_id=1, source_target_pairs={{0,1},{1,0},{2,3},{3,2},{4,5},{5,4},{6,7},{7,6},{8,9},{9,8},{10,11... | collective-permute-start | bytes 442376 | tf_op jit(solution)/shard_map/ppermute | solution.py:331

commit v4 on v3

--- a/solution.py
+++ b/solution.py
@@ -52,30 +52,69 @@
     return value + value * jnp.tanh(y[:, :width])
 
 
-def pair_weights(gate_ref, weight_ref):
+def right_rows(pair_ref, out_ref, both, live, j_half, chunk, wait):
+    half_rows, cols, width = pair_ref.shape
+    first_j = (lax.axis_index("row") * 2 + j_half) * half_rows
+    center, share = centering(width)
+    k = lax.axis_index("col") * cols + lax.broadcasted_iota(jnp.int32, (cols, width), 0)
+
+    def some(turn, _):
+        wait(turn)
+        j0 = turn * chunk
+        x = pair_ref[pl.ds(j0, chunk)].reshape(2, chunk * cols // 2, width)
+        n = normed(x[0], x[1], center, share)
+        for part in range(2):
+            edge = gated(n[:, part * width : (part + 1) * width], both).reshape(chunk // 2, cols, width)
+            for r in range(chunk // 2):
+                j = j0 + part * (chunk // 2) + r
+                reach = jnp.where(first_j + j < live, live, 0)
+                out_ref[j] = jnp.where(k < reach, edge[r], 0.0).astype(BF16)
+        return 0
+
+    lax.fori_loop(0, half_rows // chunk, some, 0)
+
+
+def mate_kernel(
+    length_ref, pair_ref, weight_a_ref, gate_a_ref, weight_b_ref, gate_b_ref, weight_gate_ref, weight_out_ref,
+    right_ref, own_ref, live_ref, both_a_ref, both_b_ref, out_gate_ref, last_ref,
+    mate_ref, raw_ref, count_ref, sems, chunk_sems, *, chunk,
+):
+    half_rows, cols, width = mate_ref.shape
+    side = lax.axis_index("col")
+    turns = half_rows // chunk
+    sources = [length_ref, weight_b_ref, gate_b_ref, weight_a_ref, gate_a_ref, weight_gate_ref, weight_out_ref]
+    places = [count_ref] + [raw_ref.at[n] for n in range(5)] + [last_ref]
+    small = [pltpu.make_async_copy(src, dst, sems.at[n]) for n, (src, dst) in enumerate(zip(sources, places))]
+
+    def piece(turn):
+        rows = pl.ds((1 - side) * half_rows + turn * chunk, chunk)
+        return pltpu.make_async_copy(pair_ref.at[rows], mate_ref.at[pl.ds(turn * chunk, chunk)], chunk_sems.at[turn])
+
+    own = pltpu.make_async_copy(pair_ref.at[pl.ds(side * half_rows, half_rows)], own_ref, sems.at[len(small)])
+    for copy in small[:3]:
+        copy.start()
+    for turn in range(turns):
+        piece(turn).start()
+    for copy in small[3:]:
+        copy.start()
+    own.start()
+    for copy in small[:3]:
+        copy.wait()
     half = jnp.asarray(0.5, BF16)
-    return jnp.concatenate([gate_ref[...] * half, weight_ref[...] * half], axis=1)
-
-
-def right_kernel(length_ref, pair_ref, gate_ref, weight_ref, out_ref, *, flip):
-    rows, cols, width = pair_ref.shape
-    half_rows = rows * pl.num_programs(0)
-    live = length_ref[0]
-    side = lax.axis_index("col")
-    j_half = 1 - side if flip else side
-    first_k = side * cols
-    first_j = lax.axis_index("row") * 2 * half_rows + j_half * half_rows + pl.program_id(0) * rows
-    center, share = centering(width)
-    both = pair_weights(gate_ref, weight_ref)
-    x = pair_ref[...].reshape(2, rows * cols // 2, width)
-    n = normed(x[0], x[1], center, share)
-    k = first_k + lax.broadcasted_iota(jnp.int32, (cols, width), 0)
-    for part in range(2):
-        edge = gated(n[:, part * width : (part + 1) * width], both).reshape(rows // 2, cols, width)
-        for r in range(rows // 2):
-            j = part * (rows // 2) + r
-            reach = jnp.where(first_j + j < live, live, 0)
-            out_ref[j] = jnp.where(k < reach, edge[r], 0.0).astype(BF16)
+    both_b_ref[...] = jnp.concatenate([raw_ref[1] * half, raw_ref[0] * half], axis=1)
+    live = count_ref[0]
+    live_ref[...] = jnp.full(live_ref.shape, live, jnp.int32)
+    right_rows(mate_ref, right_ref, both_b_ref[...], live, 1 - side, chunk, lambda turn: piece(turn).wait())
+    for copy in small[3:]:
+        copy.wait()
+    both_a_ref[...] = jnp.concatenate([raw_ref[3] * half, raw_ref[2] * half], axis=1)
+    out_gate_ref[...] = raw_ref[4] * half
+    own.wait()
+
+
+def own_kernel(live_ref, pair_ref, both_ref, out_ref, *, chunk):
+    live = live_ref[0, 0]
+    right_rows(pair_ref, out_ref, both_ref[...], live, lax.axis_index("col"), chunk, lambda turn: None)
 
 
 def fold(parts):
@@ -89,37 +128,40 @@
     return parts[0]
 
 
-def project(length_ref, slab_ref, gate_ref, weight_ref, out_gate_ref, left_ref, gates_ref, norm_ref, half_rows):
+def project(live_ref, slab_ref, both_ref, out_gate_ref, left_ref, gates_ref, norm_ref, half_rows):
     slabs, depth, width = slab_ref.shape
     k_step = pl.program_id(0)
     half_cols = depth * pl.num_programs(0)
     center, share = centering(width)
-    both = pair_weights(gate_ref, weight_ref)
+    both = both_ref[...]
     first_k = lax.axis_index("col") * half_cols + k_step * depth
-    live = first_k + lax.broadcasted_iota(jnp.int32, (depth, width), 0) < length_ref[0]
+    live = first_k + lax.broadcasted_iota(jnp.int32, (depth, width), 0) < live_ref[0:1, :]
     first_j = lax.rem(lax.axis_index("row") * (2 * half_rows), half_cols)
     start = lax.rem(first_j, depth)
 
-    def pair(s):
-        n = normed(slab_ref[s], slab_ref[s + 1], center, share)
+    def quad(q):
+        s = q * QUAD
+        x = slab_ref[pl.ds(s, QUAD)].reshape(2, 2 * depth, width)
+        n = normed(x[0], x[1], center, share)
         for part in range(2):
-            norm_ref[pl.ds(part * (depth + GATE_ROWS), depth), :] = n[:, part * width : (part + 1) * width].astype(F32)
-            edge = gated(n[:, part * width : (part + 1) * width], both)
-            left_ref[s + part] = jnp.where(live, edge, 0.0).astype(BF16).astype(left_ref.dtype)
+            own = n[:, part * width : (part + 1) * width]
+            edge = gated(own, both)
+            for r in range(2):
+                here = slice(r * depth, (r + 1) * depth)
+                left_ref[s + 2 * part + r] = jnp.where(live, edge[here], 0.0).astype(BF16).astype(F32)
+                norm_ref[2 * part + r, pl.ds(0, depth), :] = own[here].astype(F32)
 
         @pl.when(k_step == first_j // depth)
         def _():
-            own = [norm_ref[pl.ds(start + part * (depth + GATE_ROWS), GATE_ROWS), :] for part in range(2)]
-            rows = jnp.concatenate(own, axis=0).astype(BF16)
-            y = jnp.dot(rows, out_gate_ref[...] * jnp.asarray(0.5, BF16), preferred_element_type=F32)
+            rows = jnp.concatenate([norm_ref[n, pl.ds(start, GATE_ROWS), :] for n in range(QUAD)], axis=0)
+            y = jnp.dot(rows.astype(BF16), out_gate_ref[...], preferred_element_type=F32)
             gate = (0.5 + 0.5 * jnp.tanh(y)).astype(BF16).astype(F32)
-            gates_ref[pl.ds(pl.multiple_of(s * GATE_ROWS, 8), 2 * GATE_ROWS), :] = gate
-
-    if slabs <= 8:
-        for s in range(0, slabs, 2):
-            pair(s)
+            gates_ref[pl.ds(pl.multiple_of(s * GATE_ROWS, 8), QUAD * GATE_ROWS), :] = gate
+
+    if slabs == QUAD:
+        quad(0)
     else:
-        pl.loop(0, slabs, step=2)(pair)
+        pl.loop(0, slabs // QUAD)(quad)
 
 
 def contract(left_ref, right_ref, sums_ref):
@@ -162,23 +204,20 @@
 
 
 def near_kernel(
-    length_ref, mate_ref, own_ref, slab_ref, gate_ref, weight_ref, out_gate_ref,
+    live_ref, mate_ref, own_ref, slab_ref, both_ref, out_gate_ref,
     mate_sums_ref, own_sums_ref, gates_ref, left_ref, norm_ref,
 ):
-    project(
-        length_ref, slab_ref, gate_ref, weight_ref, out_gate_ref, left_ref, gates_ref, norm_ref, mate_ref.shape[0]
-    )
+    project(live_ref, slab_ref, both_ref, out_gate_ref, left_ref, gates_ref, norm_ref, mate_ref.shape[0])
     contract(left_ref, mate_ref, mate_sums_ref)
     contract(left_ref, own_ref, own_sums_ref)
 
 
 def send_kernel(
-    length_ref, mate_ref, slab_ref, gate_ref, weight_ref, out_gate_ref, near_sums_ref, near_gates_ref,
-    send_ref, left_ref, gates_ref, sums_ref, norm_ref, *, steps,
+    live_ref, mate_ref, slab_ref, both_ref, out_gate_ref, near_sums_ref, near_gates_ref,
+    send_ref, left_out_ref, gates_ref, left_ref, sums_ref, norm_ref, *, steps,
 ):
-    project(
-        length_ref, slab_ref, gate_ref, weight_ref, out_gate_ref, left_ref, gates_ref, norm_ref, mate_ref.shape[0]
-    )
+    project(live_ref, slab_ref, both_ref, out_gate_ref, left_ref, gates_ref, norm_ref, mate_ref.shape[0])
+    left_out_ref[...] = left_ref[...].astype(BF16)
     contract(left_ref, mate_ref, sums_ref)
 
     @pl.when(pl.program_id(0) == pl.num_programs(0) - 1)
@@ -222,9 +261,9 @@
     depth = divisor(half_cols, 144, rows_dev)
     blocks = half_cols // depth
     near = count // 2
-    smem = pl.BlockSpec(memory_space=pltpu.SMEM)
+    hbm = pl.BlockSpec(memory_space=pltpu.HBM)
     vmem = pl.BlockSpec(memory_space=pltpu.VMEM)
-    params = pltpu.CompilerParams(vmem_limit_bytes=48 << 20)
+    params = pltpu.CompilerParams(vmem_limit_bytes=40 << 20)
 
     def whole(*shape):
         return pl.BlockSpec(shape, lambda *_: (0,) * len(shape))
@@ -239,37 +278,52 @@
                 pairs.append((row * 2 + core, (row ^ steps[core][step]) * 2 + core))
         return lax.ppermute(x, ("row", "col"), pairs)
 
-    def right_half(pair, flip):
-        rows_step = divisor(half_rows, max(2, 1728 // half_cols), 2)
-        turns = half_rows // rows_step
-
-        def block(s):
-            return ((1 - lax.axis_index("col") if flip else lax.axis_index("col")) * turns + s, 0, 0)
-
-        return pl.pallas_call(
-            functools.partial(right_kernel, flip=flip),
-            out_shape=jax.ShapeDtypeStruct((half_rows, half_cols, hidden), BF16),
-            grid=(turns,),
-            in_specs=[
-                smem,
-                pl.BlockSpec((rows_step, half_cols, width), block),
-                whole(width, hidden),
-                whole(width, hidden),
-            ],
-            out_specs=pl.BlockSpec((rows_step, half_cols, hidden), lambda s: (s, 0, 0)),
-            compiler_params=pltpu.CompilerParams(vmem_limit_bytes=60 << 20),
-            cost_estimate=pl.CostEstimate(
-                flops=2 * half_rows * half_cols * width * hidden * 6,
-                bytes_accessed=4 * half_rows * half_cols * width,
-                transcendentals=2 * half_rows * half_cols * width,
-            ),
-            name="right_mate" if flip else "right_own",
-        )(length, pair, gate_b, weight_b)
+    chunk = divisor(half_rows, max(2, 1728 // half_cols), 2)
+    half_right = jax.ShapeDtypeStruct((half_rows, half_cols, hidden), BF16)
+    half_pair = jax.ShapeDtypeStruct((half_rows, half_cols, width), BF16)
+    right_cost = pl.CostEstimate(
+        flops=2 * half_rows * half_cols * width * hidden * 6,
+        bytes_accessed=4 * half_rows * half_cols * width,
+        transcendentals=2 * half_rows * half_cols * width,
+    )
+    mate_call = pl.pallas_call(
+        functools.partial(mate_kernel, chunk=chunk),
+        out_shape=(
+            half_right,
+            half_pair,
+            jax.ShapeDtypeStruct((8, width), jnp.int32),
+            jax.ShapeDtypeStruct((width, 2 * hidden), BF16),
+            jax.ShapeDtypeStruct((width, 2 * hidden), BF16),
+            jax.ShapeDtypeStruct((width, width), BF16),
+            jax.ShapeDtypeStruct((hidden, width), BF16),
+        ),
+        in_specs=[hbm] * 8,
+        out_specs=[vmem] * 7,
+        scratch_shapes=[
+            pltpu.VMEM(half_pair.shape, BF16),
+            pltpu.VMEM((5, width, hidden), BF16),
+            pltpu.SMEM((1,), jnp.int32),
+            pltpu.SemaphoreType.DMA((8,)),
+            pltpu.SemaphoreType.DMA((half_rows // chunk,)),
+        ],
+        compiler_params=pltpu.CompilerParams(vmem_limit_bytes=58 << 20),
+        cost_estimate=right_cost,
+        name="right_mate",
+    )
+    own_call = pl.pallas_call(
+        functools.partial(own_kernel, chunk=chunk),
+        out_shape=half_right,
+        in_specs=[vmem] * 3,
+        out_specs=vmem,
+        compiler_params=params,
+        cost_estimate=right_cost,
+        name="right_own",
+    )
 
     sums = jax.ShapeDtypeStruct((near // QUAD, half_rows * QUAD, hidden), F32)
     gates = jax.ShapeDtypeStruct((near * GATE_ROWS, width), F32)
     swapped = jax.ShapeDtypeStruct((2, half_rows * count, hidden), F32)
-    norm = pltpu.VMEM((2 * (depth + GATE_ROWS), width), F32)
+    norm = pltpu.VMEM((QUAD, depth + GATE_ROWS, width), F32)
     cost = pl.CostEstimate(
         flops=2 * rows_dev * half_cols * near * hidden,
         bytes_accessed=2 * rows_dev * half_cols * width,
@@ -277,28 +331,27 @@
     )
 
     held = lax.dynamic_slice_in_dim(slab_rep, side * half_cols, half_cols, 1)
-    right = []
-    got = None
-    for step in range(len(steps[0])):
-        if step > 0:
-            held = jnp.concatenate([held, got], axis=0)
-        if len(right) < step and len(right) < 2:
-            made, held = lax.optimization_barrier((right_half(pair_rep, not right), held))
-            right.append(made)
+    got = passed(held, 0)
+    for step in range(1, len(steps[0])):
+        held = jnp.concatenate([held, got], axis=0)
+        if step == 1:
+            made = mate_call(length, pair_rep, weight_a, gate_a, weight_b, gate_b, weight_gate, weight_out)
+            made, held = lax.optimization_barrier((made, held))
+            right_mate, pair_own, live, both_a, both_b, out_gate, last_weight = made
+        if step == 2:
+            right_own, held = lax.optimization_barrier((own_call(live, pair_own, both_b), held))
         got = passed(held, step)
-    right_mate, right_own = right
 
     near_mate, near_own, near_gates = pl.pallas_call(
         near_kernel,
         out_shape=(sums, sums, gates),
         grid=(blocks,),
         in_specs=[
-            smem,
+            whole(*live.shape),
             deep(half_rows, depth, hidden),
             deep(half_rows, depth, hidden),
             deep(near, depth, width),
-            whole(width, hidden),
-            whole(width, hidden),
+            whole(width, 2 * hidden),
             whole(width, width),
         ],
         out_specs=(whole(*sums.shape), whole(*sums.shape), whole(*gates.shape)),
@@ -306,27 +359,26 @@
         compiler_params=params,
         cost_estimate=cost,
         name="near",
-    )(length, right_mate, right_own, held, gate_a, weight_a, weight_gate)
+    )(live, right_mate, right_own, held, both_a, out_gate)
 
     send, left, far_gates = pl.pallas_call(
         functools.partial(send_kernel, steps=steps),
         out_shape=(swapped, jax.ShapeDtypeStruct((near, half_cols, hidden), BF16), gates),
         grid=(blocks,),
         in_specs=[
-            smem,
+            whole(*live.shape),
             deep(half_rows, depth, hidden),
             deep(near, depth, width),
-            whole(width, hidden),
-            whole(width, hidden),
+            whole(width, 2 * hidden),
             whole(width, width),
             whole(*sums.shape),
             whole(*gates.shape),
         ],
         out_specs=(whole(*swapped.shape), deep(near, depth, hidden), whole(*gates.shape)),
-        scratch_shapes=[pltpu.VMEM(sums.shape, F32), norm],
+        scratch_shapes=[pltpu.VMEM((near, depth, hidden), F32), pltpu.VMEM(sums.shape, F32), norm],
         compiler_params=params,
         name="send",
-    )(length, right_mate, got, gate_a, weight_a, weight_gate, near_mate, near_gates)
+    )(live, right_mate, got, both_a, out_gate, near_mate, near_gates)
 
     swap = lax.ppermute(send, "col", [(0, 1), (1, 0)])
 
@@ -355,7 +407,7 @@
         out_specs=vmem,
         compiler_params=pltpu.CompilerParams(vmem_limit_bytes=32 << 20),
         name="last",
-    )(keep, swap, weight_out)
+    )(keep, swap, last_weight)
     return jnp.transpose(update, (1, 0, 2))
 
 

time: 24.4 us -> 24.5 us (level)
  Pallas kernels: 12.8 us -> 9.67 us
  waiting for transfers between devices: 1.24 us -> 2.86 us
  local copies, waits for them, and re-layouts: 1.99 us -> 3.5 us
    pallas_call x2, Pallas kernels: 7.48 us -> 5.5 us  [the longest x1 3.87 us: shards(): mate_call(length, pair_rep, weight_a, gate_a, weight_b, gate_b, weight_ga...]
    ppermute x3, waiting for transfers between devices: 0.41 us -> 2.03 us  [passed(): return lax.ppermute(x, ('row', 'col'), pairs)]
    unnamed x14 -> x16, local copies, waits for them, and re-layouts: 1.99 us -> 3.5 us
    pallas_call x1, Pallas kernels: 1.73 us -> 1.15 us  [shards(): pl.pallas_call(functools.partial(send_kernel, steps=steps), out_shape=(sw...]
    pallas_call x1, Pallas kernels: 2.13 us -> 1.57 us  [shards(): pl.pallas_call(near_kernel, out_shape=(sums, sums, gates), grid=(blocks,)...]
  transfers between devices with their start and end apart: 4 -> 4, of which waited for: 2 -> 2; matrix products, arithmetic and copies ran while one was open for 0% -> 0% of each run, Pallas kernels for 42% -> 31%
where the time goes in v4:
time: 24.5 us; the launch traced here: 24.2 us
  Pallas kernels  9.67 us (39%)
  starting transfers between devices  7.33 us (30%)
  local copies, waits for them, and re-layouts  3.5 us (14%)
  waiting for transfers between devices  2.86 us (12%)
  between operations  0.77 us (3%)
    ppermute x3, starting transfers between devices, passed(): return lax.ppermute(x, ('row', 'col'), pairs)  7.26 us
    pallas_call x1, Pallas kernels, shards(): mate_call(length, pair_rep, weight_a, gate_a, weight_b, gate_b, weight_ga...  3.87 us
    unnamed x16, local copies, waits for them, and re-layouts  3.5 us
    ppermute x3, waiting for transfers between devices, passed(): return lax.ppermute(x, ('row', 'col'), pairs)  2.03 us
    pallas_call x1, Pallas kernels, shards(): own_call(live, pair_own, both_b)  1.63 us
    pallas_call x1, Pallas kernels, shards(): pl.pallas_call(near_kernel, out_shape=(sums, sums, gates), grid=(blocks,)...  1.57 us
    pallas_call x1, Pallas kernels, shards(): pl.pallas_call(functools.partial(send_kernel, steps=steps), out_shape=(sw...  1.15 us
    pallas_call x1, Pallas kernels, shards(): pl.pallas_call(functools.partial(last_kernel, half_cols=half_cols), out_s...  0.93 us
  transfers between devices with their start and end apart: 4, of which 2 were waited for; matrix products, arithmetic and copies ran while one was open for 0% of the time, Pallas kernels for 31%

profile of v4, /device:TPU:0, one launch (start us, length us, event | category | flops | bytes accessed | tf_op | source)
XLA Modules:
  0.0 24.2 jit_solution(13531087049947729296)
XLA Ops:
  0.0 0.0 copy-start
  0.0 0.9 %copy-done = bf16[1,288,128]{2,1,0:T(8,128)(2,1)S(1)} copy-done((bf16[1,288,128]{2,1,0:T(8,128)(2,1)S(1)}, bf16[1,288,128]{2,1,0:T(8,128)(2,1)}, u32[]{:S(2)}) %copy-start) | copy-done | bytes 73752
  0.9 4.0 %collective-permute-start = (bf16[1,144,128]{2,1,0:T(8,128)(2,1)S(1)}, bf16[1,144,128]{2,1,0:T(8,128)(2,1)S(1)}, u32[]{:S(2)}, u32[]{:S(2)}) collective-permute-start(bf16[1,144,128]{2,1,0:T(8,128)(2,1)S(1)} %constant_dynamic-slice_fusion), channel_id=1, source_target_pairs={{0,8},{1,3},{2,10},{3,1},{4,12},{5,7},{6,14},{7,5},{8,0},{9,11},{1... | collective-permute-start | bytes 110600 | tf_op jit(solution)/shard_map/ppermute | solution.py:279
  5.6 3.9 %right_mate.1 = (bf16[18,144,128]{2,1,0:T(8,128)(2,1)}, bf16[18,144,128]{2,1,0:T(8,128)(2,1)}, s32[8,128]{1,0:T(8,128)}, bf16[128,256]{1,0:T(8,128)(2,1)}, bf16[...) custom-call(s32[1]{0:T(128)S(6)} %copy.10.length_ref, bf16[36,144,128]{2,1,0:T(8,128)(2,1)} %pair_ref.1, ...), custom_call_target="tpu_custom_call" | custom-call | flops 509607936 | bytes 1327104 | tf_op jit(solution)/shard_map/right_mate/pallas_call | solution.py:338
  9.5 0.0 copy-start.1
  9.5 0.0 copy-start.2
  9.5 0.0 copy-start.3
  9.5 0.0 collective-permute-done
  9.5 1.6 %collective-permute-start.1 = (bf16[2,144,128]{2,1,0:T(8,128)(2,1)S(1)}, bf16[2,144,128]{2,1,0:T(8,128)(2,1)S(1)}, u32[]{:S(2)}, u32[]{:S(2)}) collective-permute-start(bf16[2,144,128]{2,1,0:T(8,128)(2,1)S(1)} %pad_maximum_fusion.1), channel_id=1, source_target_pairs={{0,4},{1,9},{2,6},{3,11},{4,0},{5,13},{6,2},{7,15},{8,12},{9,1},{1... | collective-permute-start | bytes 221192 | tf_op jit(solution)/shard_map/ppermute | solution.py:279
  11.1 0.0 copy-start.5
  11.2 0.7 %copy-done.5 = s32[8,128]{1,0:T(8,128)S(1)} copy-done((s32[8,128]{1,0:T(8,128)S(1)}, s32[8,128]{1,0:T(8,128)}, u32[]{:S(2)}) %copy-start.5) | copy-done | bytes 4120
  11.8 0.0 copy-start.6
  11.8 1.1 %copy-done.6 = bf16[18,144,128]{2,1,0:T(8,128)(2,1)S(1)} copy-done((bf16[18,144,128]{2,1,0:T(8,128)(2,1)S(1)}, bf16[18,144,128]{2,1,0:T(8,128)(2,1)}, u32[]{:S(2)}) %copy-start.6) | copy-done | bytes 663576
  12.9 0.0 copy-start.7
  12.9 0.8 %copy-done.7 = bf16[128,256]{1,0:T(8,128)(2,1)S(1)} copy-done((bf16[128,256]{1,0:T(8,128)(2,1)S(1)}, bf16[128,256]{1,0:T(8,128)(2,1)}, u32[]{:S(2)}) %copy-start.7) | copy-done | bytes 65560
  13.7 1.6 %right_own.1.own_ref = bf16[18,144,128]{2,1,0:T(8,128)(2,1)S(1)} custom-call(s32[8,128]{1,0:T(8,128)S(1)} %copy-done.5, bf16[18,144,128]{2,1,0:T(8,128)(2,1)S(1)} %copy-done.6, bf16[128,256]{1,0:T(8,128)(2,1)S(1)} %copy-done.7), custom_call_target="tpu_custom_call" | custom-call | flops 509607936 | bytes 1327104 | tf_op jit(solution)/shard_map/right_own/pallas_call | solution.py:342
  15.4 0.0 collective-permute-done.1
  15.4 1.6 %collective-permute-start.2 = (bf16[4,144,128]{2,1,0:T(8,128)(2,1)S(1)}, bf16[4,144,128]{2,1,0:T(8,128)(2,1)S(1)}, u32[]{:S(2)}, u32[]{:S(2)}) collective-permute-start(bf16[4,144,128]{2,1,0:T(8,128)(2,1)S(1)} %pad_maximum_fusion.slab_ref), channel_id=1, source_target_pairs={{0,2},{1,5},{2,0},{3,7},{4,6},{5,1},{6,4},{7,3},{8,10},{9,13},{10,... | collective-permute-start | bytes 442376 | tf_op jit(solution)/shard_map/ppermute | solution.py:279
  17.0 0.0 copy-done.1
  17.0 0.0 copy-done.2
  17.0 0.0 copy-done.3
  17.0 1.6 %near.1 = (f32[1,72,128]{2,1,0:T(8,128)S(1)}, f32[1,72,128]{2,1,0:T(8,128)S(1)}, f32[160,128]{1,0:T(8,128)S(1)}) custom-call(s32[8,128]{1,0:T(8,128)S(1)} %copy-done.5, bf16[18,144,128]{2,1,0:T(8,128)(2,1)S(1)} %copy-done.1, bf16[18,144,128]{2,1,0:T(8,128)(2,1)S(1)} %right_own.1.own_ref, bf16[4,144,128]{2,1,0:T(8,128)(2,1)S(1)} %pad_maximum_fusion.slab_ref, ...), custom_call_target="tpu_custom_call" | custom-call | flops 5308416 | bytes 1327104 | tf_op jit(solution)/shard_map/near/pallas_call | solution.py:345
  18.6 0.0 copy-start.4
  18.6 2.0 %collective-permute-done.2.slab_ref = bf16[4,144,128]{2,1,0:T(8,128)(2,1)S(1)} collective-permute-done((bf16[4,144,128]{2,1,0:T(8,128)(2,1)S(1)}, bf16[4,144,128]{2,1,0:T(8,128)(2,1)S(1)}, u32[]{:S(2)}, u32[]{:S(2)}) %collective-permute-start.2) | collective-permute-done | bytes 147488 | tf_op jit(solution)/shard_map/ppermute | solution.py:279
  20.6 1.2 %send.1 = (f32[2,144,128]{2,1,0:T(8,128)S(1)}, bf16[4,144,128]{2,1,0:T(8,128)(2,1)S(1)}, f32[160,128]{1,0:T(8,128)S(1)}) custom-call(s32[8,128]{1,0:T(8,128)S(1)} %copy-done.5, bf16[18,144,128]{2,1,0:T(8,128)(2,1)S(1)} %copy-done.1, bf16[4,144,128]{2,1,0:T(8,128)(2,1)S(1)} %collective-permute-done.2.slab_ref, bf16[128,256]{1,0:T(8,128)(2,1)S(1)} %copy-done.2, ...), custom_call_target="tpu_custom_call" | custom-call | tf_op jit(solution)/shard_map/send/pallas_call | solution.py:364
  21.8 0.1 collective-permute-start.3
  21.9 0.5 %keep.1.keep_ref = f32[2,144,128]{2,1,0:T(8,128)S(1)} custom-call(bf16[18,144,128]{2,1,0:T(8,128)(2,1)S(1)} %right_own.1.own_ref, bf16[4,144,128]{2,1,0:T(8,128)(2,1)S(1)} %get-tuple-element.46.left_ref, f32[160,128]{1,0:T(8,128)S(1)} %get-tuple-element.47.gates_ref, f32[1,72,128]{2,1,0:T(8,128)S(1)} %get-tuple-element.48.near_sums_ref, ...), custom_call_target="tpu_custom_call" | custom-call | flops 5308416 | bytes 1327104 | tf_op jit(solution)/shard_map/keep/pallas_call | solution.py:385
  22.4 0.8 %collective-permute-done.3.got_ref = f32[2,144,128]{2,1,0:T(8,128)S(1)} collective-permute-done((f32[2,144,128]{2,1,0:T(8,128)S(1)}, f32[2,144,128]{2,1,0:T(8,128)S(1)}, u32[]{:S(2)}, u32[]{:S(2)}) %collective-permute-start.3) | collective-permute-done | bytes 147488 | tf_op jit(solution)/shard_map/ppermute | solution.py:383
  23.2 0.0 copy-done.4
  23.2 0.9 %last.1 = bf16[18,8,128]{2,1,0:T(8,128)(2,1)} custom-call(f32[2,144,128]{2,1,0:T(8,128)S(1)} %keep.1.keep_ref, f32[2,144,128]{2,1,0:T(8,128)S(1)} %collective-permute-done.3.got_ref, bf16[128,128]{1,0:T(8,128)(2,1)S(1)} %copy-done.4), custom_call_target="tpu_custom_call" | custom-call | tf_op jit(solution)/shard_map/last/pallas_call | solution.py:403
  (3 shorter events, 0.0 us)
Async XLA Ops:
  0.0 0.9 %copy-start = (bf16[1,288,128]{2,1,0:T(8,128)(2,1)S(1)}, bf16[1,288,128]{2,1,0:T(8,128)(2,1)}, u32[]{:S(2)}) copy-start(bf16[1,288,128]{2,1,0:T(8,128)(2,1)} %param.10) | copy-start | bytes 221188
  0.9 8.6 %collective-permute-start = (bf16[1,144,128]{2,1,0:T(8,128)(2,1)S(1)}, bf16[1,144,128]{2,1,0:T(8,128)(2,1)S(1)}, u32[]{:S(2)}, u32[]{:S(2)}) collective-permute-start(bf16[1,144,128]{2,1,0:T(8,128)(2,1)S(1)} %constant_dynamic-slice_fusion), channel_id=1, source_target_pairs={{0,8},{1,3},{2,10},{3,1},{4,12},{5,7},{6,14},{7,5},{8,0},{9,11},{1... | collective-permute-start | bytes 110600 | tf_op jit(solution)/shard_map/ppermute | solution.py:279
  9.5 7.6 %copy-start.1 = (bf16[18,144,128]{2,1,0:T(8,128)(2,1)S(1)}, bf16[18,144,128]{2,1,0:T(8,128)(2,1)}, u32[]{:S(2)}) copy-start(bf16[18,144,128]{2,1,0:T(8,128)(2,1)} %get-tuple-element.40.mate_ref) | copy-start | bytes 1990660
  9.5 7.5 %copy-start.2 = (bf16[128,256]{1,0:T(8,128)(2,1)S(1)}, bf16[128,256]{1,0:T(8,128)(2,1)}, u32[]{:S(2)}) copy-start(bf16[128,256]{1,0:T(8,128)(2,1)} %get-tuple-element.42.both_ref) | copy-start | bytes 196612
  9.5 7.5 %copy-start.3 = (bf16[128,128]{1,0:T(8,128)(2,1)S(1)}, bf16[128,128]{1,0:T(8,128)(2,1)}, u32[]{:S(2)}) copy-start(bf16[128,128]{1,0:T(8,128)(2,1)} %get-tuple-element.43.out_gate_ref) | copy-start | bytes 98308
  9.5 5.9 %collective-permute-start.1 = (bf16[2,144,128]{2,1,0:T(8,128)(2,1)S(1)}, bf16[2,144,128]{2,1,0:T(8,128)(2,1)S(1)}, u32[]{:S(2)}, u32[]{:S(2)}) collective-permute-start(bf16[2,144,128]{2,1,0:T(8,128)(2,1)S(1)} %pad_maximum_fusion.1), channel_id=1, source_target_pairs={{0,4},{1,9},{2,6},{3,11},{4,0},{5,13},{6,2},{7,15},{8,12},{9,1},{1... | collective-permute-start | bytes 221192 | tf_op jit(solution)/shard_map/ppermute | solution.py:279
  11.1 0.7 %copy-start.5 = (s32[8,128]{1,0:T(8,128)S(1)}, s32[8,128]{1,0:T(8,128)}, u32[]{:S(2)}) copy-start(s32[8,128]{1,0:T(8,128)} %get-tuple-element.35.live_ref) | copy-start | bytes 12292
  11.8 1.1 %copy-start.6 = (bf16[18,144,128]{2,1,0:T(8,128)(2,1)S(1)}, bf16[18,144,128]{2,1,0:T(8,128)(2,1)}, u32[]{:S(2)}) copy-start(bf16[18,144,128]{2,1,0:T(8,128)(2,1)} %get-tuple-element.36.pair_ref) | copy-start | bytes 1990660
  12.9 0.8 %copy-start.7 = (bf16[128,256]{1,0:T(8,128)(2,1)S(1)}, bf16[128,256]{1,0:T(8,128)(2,1)}, u32[]{:S(2)}) copy-start(bf16[128,256]{1,0:T(8,128)(2,1)} %get-tuple-element.37.both_ref) | copy-start | bytes 196612
  15.4 5.2 %collective-permute-start.2 = (bf16[4,144,128]{2,1,0:T(8,128)(2,1)S(1)}, bf16[4,144,128]{2,1,0:T(8,128)(2,1)S(1)}, u32[]{:S(2)}, u32[]{:S(2)}) collective-permute-start(bf16[4,144,128]{2,1,0:T(8,128)(2,1)S(1)} %pad_maximum_fusion.slab_ref), channel_id=1, source_target_pairs={{0,2},{1,5},{2,0},{3,7},{4,6},{5,1},{6,4},{7,3},{8,10},{9,13},{10,... | collective-permute-start | bytes 442376 | tf_op jit(solution)/shard_map/ppermute | solution.py:279
  18.6 4.6 %copy-start.4 = (bf16[128,128]{1,0:T(8,128)(2,1)S(1)}, bf16[128,128]{1,0:T(8,128)(2,1)}, u32[]{:S(2)}) copy-start(bf16[128,128]{1,0:T(8,128)(2,1)} %get-tuple-element.50.weight_ref) | copy-start | bytes 98308
  21.8 1.4 %collective-permute-start.3 = (f32[2,144,128]{2,1,0:T(8,128)S(1)}, f32[2,144,128]{2,1,0:T(8,128)S(1)}, u32[]{:S(2)}, u32[]{:S(2)}) collective-permute-start(f32[2,144,128]{2,1,0:T(8,128)S(1)} %get-tuple-element.49), channel_id=1, source_target_pairs={{0,1},{1,0},{2,3},{3,2},{4,5},{5,4},{6,7},{7,6},{8,9},{9,8},{10,11... | collective-permute-start | bytes 442376 | tf_op jit(solution)/shard_map/ppermute | solution.py:383

commit v5 on v4

v5 whole, which is shorter than its diff:
```python
import functools

import jax
import jax.numpy as jnp
from jax import lax
from jax.experimental import pallas as pl
from jax.experimental.pallas import tpu as pltpu
from jax.sharding import PartitionSpec as P

EPS = 1e-05
F32 = jnp.float32
BF16 = jnp.bfloat16
QUAD = 4
GATE_ROWS = 40


def divisor(total, limit, step=1):
    return max(d for d in range(step, total + 1, step) if total % d == 0 and (d <= limit or d == step))


def doubling(count):
    bits = [1 << b for b in reversed(range(count.bit_length() - 1))]
    return bits, bits[-1:] + bits[:-1]


def slots(steps):
    held = [0]
    for step in steps:
        held = held + [m ^ step for m in held]
    return held


def centering(width):
    row = lax.broadcasted_iota(jnp.int32, (2 * width, 2 * width), 0)
    col = lax.broadcasted_iota(jnp.int32, (2 * width, 2 * width), 1)
    share = jnp.where((row < width) == (col < width), 1.0 / width, 0.0)
    center = jnp.where(row == col, 1.0, 0.0) - share
    return center.astype(BF16), share.astype(BF16)


def normed(first, second, center, share):
    wide = jnp.concatenate([first, second], axis=1)
    d = jnp.dot(wide, center, preferred_element_type=F32)
    var = jnp.dot((d * d).astype(BF16), share, preferred_element_type=F32)
    return (d * lax.rsqrt(var + EPS)).astype(BF16)


def gated(n, both):
    width = both.shape[1] // 2
    y = jnp.dot(n, both, preferred_element_type=F32)
    value = y[:, width:]
    return value + value * jnp.tanh(y[:, :width])


def right_kernel(
    length_ref, pair_ref, weight_ref, gate_ref, out_ref, x_ref, y_ref, w_ref, count_ref, small_sems, in_sems, out_sems,
    *, chunk,
):
    rows, cols, width = pair_ref.shape
    turns = rows // chunk

    def piece(turn, src, dst, sems):
        here = pl.ds(turn * chunk, chunk)
        return pltpu.make_async_copy(src.at[here], dst.at[here], sems.at[turn])

    small = [
        pltpu.make_async_copy(src, dst, small_sems.at[n])
        for n, (src, dst) in enumerate(
            ((length_ref, count_ref), (gate_ref, w_ref.at[0]), (weight_ref, w_ref.at[1]))
        )
    ]
    for copy in small:
        copy.start()
    for turn in range(turns):
        piece(turn, pair_ref, x_ref, in_sems).start()
    for copy in small:
        copy.wait()
    half = jnp.asarray(0.5, BF16)
    both = jnp.concatenate([w_ref[0] * half, w_ref[1] * half], axis=1)
    live = count_ref[0]
    first_j = lax.axis_index("row") * rows
    center, share = centering(width)
    k = lax.axis_index("col") * cols + lax.broadcasted_iota(jnp.int32, (cols, width), 0)

    def some(turn, _):
        piece(turn, pair_ref, x_ref, in_sems).wait()
        j0 = turn * chunk
        x = x_ref[pl.ds(j0, chunk)].reshape(2, chunk * cols // 2, width)
        n = normed(x[0], x[1], center, share)
        for part in range(2):
            edge = gated(n[:, part * width : (part + 1) * width], both).reshape(chunk // 2, cols, width)
            for r in range(chunk // 2):
                j = j0 + part * (chunk // 2) + r
                reach = jnp.where(first_j + j < live, live, 0)
                y_ref[j] = jnp.where(k < reach, edge[r], 0.0).astype(BF16)
        piece(turn, y_ref, out_ref, out_sems).start()
        return 0

    lax.fori_loop(0, turns, some, 0)
    for turn in range(turns):
        piece(turn, y_ref, out_ref, out_sems).wait()


def fold(parts):
    place = lax.broadcasted_iota(jnp.int32, parts[0].shape, 0)
    for step in (1, 2, 4):
        here = (place & step) == 0
        parts = [
            jnp.where(here, a, b) + pltpu.roll(jnp.where(here, b, a), 8 - step, 0)
            for a, b in zip(parts[0::2], parts[1::2])
        ]
    return parts[0]


def block_of(blocks):
    return 0 if blocks == 1 else pl.program_id(0)


def project(length_ref, slab_ref, gate_ref, weight_ref, out_gate_ref, left_ref, gates_ref, norm_ref, half_rows, blocks):
    slabs, depth, width = slab_ref.shape
    k_step = block_of(blocks)
    half_cols = depth * blocks
    half = jnp.asarray(0.5, BF16)
    center, share = centering(width)
    both = jnp.concatenate([gate_ref[...] * half, weight_ref[...] * half], axis=1)
    first_k = lax.axis_index("col") * half_cols + k_step * depth
    live = first_k + lax.broadcasted_iota(jnp.int32, (depth, width), 0) < length_ref[0]
    first_j = lax.rem(lax.axis_index("row") * (2 * half_rows), half_cols)
    start = lax.rem(first_j, depth)

    def quad(q):
        s = q * QUAD
        x = slab_ref[pl.ds(s, QUAD)].reshape(2, 2 * depth, width)
        n = normed(x[0], x[1], center, share)
        for part in range(2):
            own = n[:, part * width : (part + 1) * width]
            edge = gated(own, both)
            for r in range(2):
                here = slice(r * depth, (r + 1) * depth)
                left_ref[s + 2 * part + r] = jnp.where(live, edge[here], 0.0).astype(BF16).astype(F32)
                norm_ref[2 * part + r, pl.ds(0, depth), :] = own[here].astype(F32)

        def gates():
            rows = jnp.concatenate([norm_ref[n, pl.ds(start, GATE_ROWS), :] for n in range(QUAD)], axis=0)
            y = jnp.dot(rows.astype(BF16), out_gate_ref[...] * half, preferred_element_type=F32)
            gate = (0.5 + 0.5 * jnp.tanh(y)).astype(BF16).astype(F32)
            gates_ref[pl.ds(pl.multiple_of(s * GATE_ROWS, 8), QUAD * GATE_ROWS), :] = gate

        if blocks == 1:
            gates()
        else:
            pl.when(k_step == first_j // depth)(gates)

    if slabs == QUAD:
        quad(0)
    else:
        pl.loop(0, slabs // QUAD)(quad)


def contract(left_ref, right_ref, j_half, sums_ref, blocks):
    slabs, depth, _ = left_ref.shape
    rows = right_ref.shape[0] // 2
    group = divisor(rows, 6, 2)

    def tile(turn, _):
        q = turn // (rows // group)
        j0 = lax.rem(turn, rows // group) * group
        first = j_half * rows + j0
        sums = [[None] * QUAD for _ in range(group)]
        for k0 in range(0, depth, 16):
            edges = [right_ref[first + j, pl.ds(k0, 16), :].astype(F32) for j in range(group)]
            for n in range(QUAD):
                left = left_ref[q * QUAD + n, pl.ds(k0, 16), :].astype(F32)
                for j in range(group):
                    term = left * edges[j]
                    term = term[:8] + term[8:]
                    sums[j][n] = term if k0 == 0 else sums[j][n] + term
        for j in range(0, group, 2):
            dest = sums_ref.at[q, pl.ds(pl.multiple_of((j0 + j) * QUAD, 8), 8), :]
            total = fold(sums[j] + sums[j + 1])
            dest[...] = total if blocks == 1 else jnp.where(block_of(blocks) == 0, total, total + dest[...])
        return 0

    lax.fori_loop(0, slabs // QUAD * (rows // group), tile, 0)


def assemble(dest_ref, sums_ref, gates_ref, places, j_half):
    half_rows = sums_ref.shape[1] // QUAD
    count = dest_ref.shape[1] // half_rows
    side, place = lax.axis_index("col"), lax.axis_index("row")
    for n, (m0, m1) in enumerate(zip(*places)):
        i = jnp.bitwise_xor(place, jnp.where(side == 0, m0, m1))
        rows = pl.ds(i, half_rows, stride=count)
        dest_ref[0, rows, :] = sums_ref[n // QUAD, pl.ds(n % QUAD, half_rows, stride=QUAD), :]
        dest_ref[1, rows, :] = gates_ref[pl.ds(n * GATE_ROWS + j_half * half_rows, half_rows), :]


def near_kernel(
    length_ref, right_ref, slab_ref, gate_ref, weight_ref, out_gate_ref,
    mate_sums_ref, own_sums_ref, gates_ref, left_ref, norm_ref, *, blocks,
):
    side = lax.axis_index("col")
    project(
        length_ref, slab_ref, gate_ref, weight_ref, out_gate_ref, left_ref, gates_ref, norm_ref,
        right_ref.shape[0] // 2, blocks,
    )
    contract(left_ref, right_ref, 1 - side, mate_sums_ref, blocks)
    contract(left_ref, right_ref, side, own_sums_ref, blocks)


def send_kernel(
    length_ref, right_ref, slab_ref, gate_ref, weight_ref, out_gate_ref, near_sums_ref, near_gates_ref,
    send_ref, left_out_ref, gates_ref, left_ref, sums_ref, norm_ref, *, blocks, near_places, far_places,
):
    flip = 1 - lax.axis_index("col")
    project(
        length_ref, slab_ref, gate_ref, weight_ref, out_gate_ref, left_ref, gates_ref, norm_ref,
        right_ref.shape[0] // 2, blocks,
    )
    left_out_ref[...] = left_ref[...].astype(BF16)
    contract(left_ref, right_ref, flip, sums_ref, blocks)

    def rest():
        assemble(send_ref, near_sums_ref, near_gates_ref, near_places, flip)
        assemble(send_ref, sums_ref, gates_ref, far_places, flip)

    if blocks == 1:
        rest()
    else:
        pl.when(pl.program_id(0) == blocks - 1)(rest)


def keep_kernel(
    right_ref, left_ref, gates_ref, near_sums_ref, near_gates_ref, keep_ref, sums_ref,
    *, blocks, near_places, far_places,
):
    side = lax.axis_index("col")
    contract(left_ref, right_ref, side, sums_ref, blocks)

    def rest():
        assemble(keep_ref, near_sums_ref, near_gates_ref, near_places, side)
        assemble(keep_ref, sums_ref, gates_ref, far_places, side)

    if blocks == 1:
        rest()
    else:
        pl.when(pl.program_id(0) == blocks - 1)(rest)


def last_kernel(keep_ref, got_ref, weight_ref, out_ref, *, half_cols):
    rows_dev = 2 * out_ref.shape[0]
    tri = keep_ref[0] + got_ref[0]
    d = tri - jnp.mean(tri, axis=-1, keepdims=True)
    var = jnp.mean(d * d, axis=-1, keepdims=True)
    n = (d * lax.rsqrt(var + EPS)).astype(BF16)
    projected = jnp.dot(n, weight_ref[...], preferred_element_type=F32)
    mine = lax.axis_index("row") * rows_dev // half_cols == lax.axis_index("col")
    update = projected * jnp.where(mine, keep_ref[1], got_ref[1])
    out_ref[...] = update.astype(BF16).reshape(out_ref.shape)


def passed(x, to):
    count = lax.axis_size("row")
    pairs = []
    for row in range(count):
        for core in range(2):
            if (target := to(row, core)) is not None:
                pairs.append((row * 2 + core, target[0] * 2 + target[1]))
    return lax.ppermute(x, ("row", "col"), pairs)


def doubled(half, count, between):
    steps = doubling(count)
    held, got = half, None
    for step in range(len(steps[0])):
        if step > 0:
            held = jnp.concatenate([held, got], axis=0)
        if step == 1:
            held, made = between(held)
        got = passed(held, lambda row, core: (row ^ steps[core][step], core))
    near = [slots(s[:-1]) for s in steps]
    far = [[m ^ s[-1] for m in held_by] for held_by, s in zip(near, steps)]
    return held, got, near, far, made


def direct(slab, half, between):
    half_cols = half.shape[1]
    side = lax.axis_index("col")

    def out(m):
        return passed(slab, lambda row, core: (row ^ m, 1) if core == 0 else None)

    far = [out(m) for m in (4, 5, 6, 7)]
    beside = out(1)
    both, made = between(jnp.concatenate([slab, beside], axis=0))
    pair = passed(both, lambda row, core: (row ^ 2, 0) if core == 1 else None)
    over = jnp.concatenate([beside[:, :half_cols]] * 2, axis=0)
    over = jnp.where(side == 0, pair[:, half_cols:], over)
    over = passed(over, lambda row, core: (row, 1 - core))
    near0 = jnp.concatenate([half, over[:1], pair[:, :half_cols]], axis=0)
    near1 = jnp.concatenate([half, beside[:, half_cols:], over], axis=0)
    near = jnp.where(side == 0, near0, near1)
    _, far = lax.optimization_barrier((near, far))
    crossed = jnp.concatenate([x[:, :half_cols] for x in far], axis=0)
    crossed = passed(crossed, lambda row, core: (row, 0) if core == 1 else None)
    far = jnp.where(side == 0, crossed, jnp.concatenate([x[:, half_cols:] for x in far], axis=0))
    return near, far, [[0, 1, 2, 3]] * 2, [[4, 5, 6, 7]] * 2, made


def shards(pair_rep, slab_rep, length, weight_a, gate_a, weight_b, gate_b, weight_gate, weight_out):
    rows_dev, half_cols, width = pair_rep.shape
    hidden = weight_a.shape[1]
    count = lax.axis_size("row")
    side = lax.axis_index("col")
    half_rows = rows_dev // 2
    depth = divisor(half_cols, 144, rows_dev)
    blocks = half_cols // depth
    grid = () if blocks == 1 else (blocks,)
    near = count // 2
    hbm = pl.BlockSpec(memory_space=pltpu.HBM)
    smem = pl.BlockSpec(memory_space=pltpu.SMEM)
    vmem = pl.BlockSpec(memory_space=pltpu.VMEM)
    params = pltpu.CompilerParams(vmem_limit_bytes=40 << 20)

    def whole(*shape):
        return vmem if blocks == 1 else pl.BlockSpec(shape, lambda *_: (0,) * len(shape))

    def deep(rows):
        return vmem if blocks == 1 else pl.BlockSpec((rows, depth, width), lambda k: (0, k, 0))

    chunk = divisor(rows_dev, max(2, 1728 // half_cols), 2)
    turns = rows_dev // chunk
    right_call = pl.pallas_call(
        functools.partial(right_kernel, chunk=chunk),
        out_shape=jax.ShapeDtypeStruct((rows_dev, half_cols, hidden), BF16),
        in_specs=[hbm] * 4,
        out_specs=hbm,
        scratch_shapes=[
            pltpu.VMEM((rows_dev, half_cols, width), BF16),
            pltpu.VMEM((rows_dev, half_cols, hidden), BF16),
            pltpu.VMEM((2, width, hidden), BF16),
            pltpu.SMEM((1,), jnp.int32),
            pltpu.SemaphoreType.DMA((3,)),
            pltpu.SemaphoreType.DMA((turns,)),
            pltpu.SemaphoreType.DMA((turns,)),
        ],
        compiler_params=pltpu.CompilerParams(vmem_limit_bytes=58 << 20),
        cost_estimate=pl.CostEstimate(
            flops=2 * rows_dev * half_cols * width * hidden * 6,
            bytes_accessed=4 * rows_dev * half_cols * width,
            transcendentals=2 * rows_dev * half_cols * width,
        ),
        name="right",
    )

    def between(held):
        made, held = lax.optimization_barrier((right_call(length, pair_rep, weight_b, gate_b), held))
        return held, made

    half = lax.dynamic_slice_in_dim(slab_rep, side * half_cols, half_cols, 1)
    gather = functools.partial(direct, slab_rep) if count == 8 else functools.partial(doubled, count=count)
    near_slabs, far_slabs, near_places, far_places, right = gather(half, between=between)

    sums = jax.ShapeDtypeStruct((near // QUAD, half_rows * QUAD, hidden), F32)
    gates = jax.ShapeDtypeStruct((near * GATE_ROWS, width), F32)
    swapped = jax.ShapeDtypeStruct((2, half_rows * count, hidden), F32)
    norm = pltpu.VMEM((QUAD, depth + GATE_ROWS, width), F32)
    left_f32 = pltpu.VMEM((near, depth, hidden), F32)
    cost = pl.CostEstimate(
        flops=2 * rows_dev * half_cols * near * hidden,
        bytes_accessed=2 * rows_dev * half_cols * width,
        transcendentals=near * half_cols * width,
    )
    weights = [whole(width, hidden), whole(width, hidden), whole(width, width)]

    near_mate, near_own, near_gates = pl.pallas_call(
        functools.partial(near_kernel, blocks=blocks),
        out_shape=(sums, sums, gates),
        grid=grid,
        in_specs=[smem, deep(rows_dev), deep(near)] + weights,
        out_specs=(whole(*sums.shape), whole(*sums.shape), whole(*gates.shape)),
        scratch_shapes=[left_f32, norm],
        compiler_params=params,
        cost_estimate=cost,
        name="near",
    )(length, right, near_slabs, gate_a, weight_a, weight_gate)

    send, left, far_gates = pl.pallas_call(
        functools.partial(send_kernel, blocks=blocks, near_places=near_places, far_places=far_places),
        out_shape=(swapped, jax.ShapeDtypeStruct((near, half_cols, hidden), BF16), gates),
        grid=grid,
        in_specs=[smem, deep(rows_dev), deep(near)] + weights + [whole(*sums.shape), whole(*gates.shape)],
        out_specs=(whole(*swapped.shape), deep(near), whole(*gates.shape)),
        scratch_shapes=[left_f32, pltpu.VMEM(sums.shape, F32), norm],
        compiler_params=params,
        name="send",
    )(length, right, far_slabs, gate_a, weight_a, weight_gate, near_mate, near_gates)

    swap = passed(send, lambda row, core: (row, 1 - core))

    keep = pl.pallas_call(
        functools.partial(keep_kernel, blocks=blocks, near_places=near_places, far_places=far_places),
        out_shape=swapped,
        grid=grid,
        in_specs=[deep(rows_dev), deep(near), whole(*gates.shape), whole(*sums.shape), whole(*gates.shape)],
        out_specs=whole(*swapped.shape),
        scratch_shapes=[pltpu.VMEM(sums.shape, F32)],
        compiler_params=params,
        cost_estimate=cost,
        name="keep",
    )(right, left, far_gates, near_own, near_gates)

    update = pl.pallas_call(
        functools.partial(last_kernel, half_cols=half_cols),
        out_shape=jax.ShapeDtypeStruct((half_rows, count, width), BF16),
        in_specs=[vmem, vmem, vmem],
        out_specs=vmem,
        compiler_params=pltpu.CompilerParams(vmem_limit_bytes=32 << 20),
        name="last",
    )(keep, swap, weight_out)
    return jnp.transpose(update, (1, 0, 2))


def solution(mesh):
    placed = (
        P(("groups", "row"), "col", None),
        P(("groups", "row"), None, None),
        P("groups"),
        P(),
        P(),
        P(),
        P(),
        P(),
        P(),
    )
    return jax.shard_map(
        shards,
        mesh=mesh,
        in_specs=placed,
        out_specs=P("groups", ("row", "col"), None),
        check_vma=False,
    )
```

time: 24.5 us -> 32.9 us (1.34)
  starting transfers between devices: 7.33 us -> 16 us
  waiting for transfers between devices: 2.86 us -> 7.34 us
  local copies, waits for them, and re-layouts: 3.5 us -> 0.08 us
  Pallas kernels: 9.67 us -> 8.12 us
    ppermute x3 -> x9, starting transfers between devices: 7.26 us -> 16 us  [passed(): return lax.ppermute(x, ('row', 'col'), pairs)]
    ppermute x3 -> x9, waiting for transfers between devices: 2.03 us -> 7.34 us  [passed(): return lax.ppermute(x, ('row', 'col'), pairs)]
    unnamed x16 -> x12, local copies, waits for them, and re-layouts: 3.5 us -> 0.03 us
    pallas_call x5 -> x4, Pallas kernels: 8.74 us -> 7.19 us  [the longest x1 4.2 us: between(): right_call(length, pair_rep, weight_b, gate_b)]
    ppermute x1 -> x0, waiting for transfers between devices: 0.83 us -> none  [shards(): swap = lax.ppermute(send, 'col', [(0, 1), (1, 0)])]
  transfers between devices with their start and end apart: 4 -> 9, of which waited for: 2 -> 4; matrix products, arithmetic and copies ran while one was open for 0% -> 0% of each run, Pallas kernels for 31% -> 19%
where the time goes in v5:
time: 32.9 us; the launch traced here: 32.6 us
  starting transfers between devices  16 us (49%)
  Pallas kernels  8.12 us (25%)
  waiting for transfers between devices  7.34 us (22%)
  between operations  0.93 us (3%)
    ppermute x9, starting transfers between devices, passed(): return lax.ppermute(x, ('row', 'col'), pairs)  16 us
    ppermute x9, waiting for transfers between devices, passed(): return lax.ppermute(x, ('row', 'col'), pairs)  7.34 us
    pallas_call x1, Pallas kernels, between(): right_call(length, pair_rep, weight_b, gate_b)  4.2 us
    pallas_call x1, Pallas kernels, shards(): pl.pallas_call(functools.partial(near_kernel, blocks=blocks), out_shape=(...  1.46 us
    pallas_call x1, Pallas kernels, shards(): pl.pallas_call(functools.partial(send_kernel, blocks=blocks, near_places=...  1.01 us
    pallas_call x1, Pallas kernels, shards(): pl.pallas_call(functools.partial(last_kernel, half_cols=half_cols), out_s...  0.93 us
  transfers between devices with their start and end apart: 9, of which 4 were waited for; matrix products, arithmetic and copies ran while one was open for 0% of the time, Pallas kernels for 19%

profile of v5, /device:TPU:0, one launch (start us, length us, event | category | flops | bytes accessed | tf_op | source)
XLA Modules:
  0.0 32.6 jit_solution(16007546436607769724)
XLA Ops:
  0.0 4.3 %collective-permute-start = (bf16[1,288,128]{2,1,0:T(8,128)(2,1)}, bf16[1,288,128]{2,1,0:T(8,128)(2,1)S(1)}, u32[]{:S(2)}, u32[]{:S(2)}) collective-permute-start(bf16[1,288,128]{2,1,0:T(8,128)(2,1)} %param.10), channel_id=1, source_target_pairs={{0,3},{2,1},{4,7},{6,5},{8,11},{10,9},{12,15},{14,13},{16,19},{18,... | collective-permute-start | bytes 221192 | tf_op jit(solution)/shard_map/ppermute | solution.py:269
  4.3 2.4 %collective-permute-start.3 = (bf16[1,288,128]{2,1,0:T(8,128)(2,1)}, bf16[1,288,128]{2,1,0:T(8,128)(2,1)S(1)}, u32[]{:S(2)}, u32[]{:S(2)}) collective-permute-start(bf16[1,288,128]{2,1,0:T(8,128)(2,1)} %param.10), channel_id=1, source_target_pairs={{0,9},{2,11},{4,13},{6,15},{8,1},{10,3},{12,5},{14,7},{16,25},{18,... | collective-permute-start | bytes 221192 | tf_op jit(solution)/shard_map/ppermute | solution.py:269
  6.7 2.2 %collective-permute-start.4 = (bf16[1,288,128]{2,1,0:T(8,128)(2,1)}, bf16[1,288,128]{2,1,0:T(8,128)(2,1)S(1)}, u32[]{:S(2)}, u32[]{:S(2)}) collective-permute-start(bf16[1,288,128]{2,1,0:T(8,128)(2,1)} %param.10), channel_id=1, source_target_pairs={{0,11},{2,9},{4,15},{6,13},{8,3},{10,1},{12,7},{14,5},{16,27},{18,... | collective-permute-start | bytes 221192 | tf_op jit(solution)/shard_map/ppermute | solution.py:269
  8.9 1.4 %collective-permute-start.5 = (bf16[1,288,128]{2,1,0:T(8,128)(2,1)}, bf16[1,288,128]{2,1,0:T(8,128)(2,1)S(1)}, u32[]{:S(2)}, u32[]{:S(2)}) collective-permute-start(bf16[1,288,128]{2,1,0:T(8,128)(2,1)} %param.10), channel_id=1, source_target_pairs={{0,13},{2,15},{4,9},{6,11},{8,5},{10,7},{12,1},{14,3},{16,29},{18,... | collective-permute-start | bytes 221192 | tf_op jit(solution)/shard_map/ppermute | solution.py:269
  10.3 2.2 %collective-permute-start.6 = (bf16[1,288,128]{2,1,0:T(8,128)(2,1)}, bf16[1,288,128]{2,1,0:T(8,128)(2,1)S(1)}, u32[]{:S(2)}, u32[]{:S(2)}) collective-permute-start(bf16[1,288,128]{2,1,0:T(8,128)(2,1)} %param.10), channel_id=1, source_target_pairs={{0,15},{2,13},{4,11},{6,9},{8,7},{10,5},{12,3},{14,1},{16,31},{18,... | collective-permute-start | bytes 221192 | tf_op jit(solution)/shard_map/ppermute | solution.py:269
  13.2 0.0 copy-start.5
  13.2 4.2 %right.1.right_ref = bf16[36,144,128]{2,1,0:T(8,128)(2,1)} custom-call(s32[1]{0:T(128)S(6)} %copy.10.length_ref, bf16[36,144,128]{2,1,0:T(8,128)(2,1)} %pair_ref.1, bf16[128,128]{1,0:T(8,128)(2,1)} %weight_ref.4, bf16[128,128]{1,0:T(8,128)(2,1)} %gate_ref.3), custom_call_target="tpu_custom_call" | custom-call | flops 1019215872 | bytes 2654208 | tf_op jit(solution)/shard_map/right/pallas_call | solution.py:357
  17.4 0.0 copy-start
  17.4 0.0 copy-start.1
  17.4 0.0 copy-start.2
  17.4 0.0 copy-start.3
  17.4 0.0 collective-permute-done
  17.4 0.0 copy-done.5
  17.5 1.4 %collective-permute-start.1 = (bf16[2,288,128]{2,1,0:T(8,128)(2,1)S(1)}, bf16[2,288,128]{2,1,0:T(8,128)(2,1)S(1)}, u32[]{:S(2)}, u32[]{:S(2)}) collective-permute-start(bf16[2,288,128]{2,1,0:T(8,128)(2,1)S(1)} %pad_maximum_fusion.2), channel_id=1, source_target_pairs={{1,4},{3,6},{5,0},{7,2},{9,12},{11,14},{13,8},{15,10},{17,20},{19,... | collective-permute-start | bytes 442376 | tf_op jit(solution)/shard_map/ppermute | solution.py:269
  18.9 5.1 %collective-permute-done.1 = bf16[2,288,128]{2,1,0:T(8,128)(2,1)S(1)} collective-permute-done((bf16[2,288,128]{2,1,0:T(8,128)(2,1)S(1)}, bf16[2,288,128]{2,1,0:T(8,128)(2,1)S(1)}, u32[]{:S(2)}, u32[]{:S(2)}) %collective-permute-start.1) | collective-permute-done | bytes 147488 | tf_op jit(solution)/shard_map/ppermute | solution.py:269
  24.1 0.1 collective-permute-start.2
  24.2 1.2 %collective-permute-done.2 = bf16[2,144,128]{2,1,0:T(8,128)(2,1)S(1)} collective-permute-done((bf16[2,144,128]{2,1,0:T(8,128)(2,1)S(1)}, bf16[2,144,128]{2,1,0:T(8,128)(2,1)S(1)}, u32[]{:S(2)}, u32[]{:S(2)}) %collective-permute-start.2) | collective-permute-done | bytes 73760 | tf_op jit(solution)/shard_map/ppermute | solution.py:269
  25.5 0.0 collective-permute-done.3
  25.5 0.0 collective-permute-done.4
  25.5 0.0 collective-permute-done.5
  25.5 0.0 collective-permute-done.6
  25.6 1.3 %collective-permute-start.7 = (bf16[4,144,128]{2,1,0:T(8,128)(2,1)S(1)}, bf16[4,144,128]{2,1,0:T(8,128)(2,1)S(1)}, u32[]{:S(2)}, u32[]{:S(2)}) collective-permute-start(bf16[4,144,128]{2,1,0:T(8,128)(2,1)S(1)} %pad_maximum_fusion.3), channel_id=1, source_target_pairs={{1,0},{3,2},{5,4},{7,6},{9,8},{11,10},{13,12},{15,14},{17,16},{19,... | collective-permute-start | bytes 442376 | tf_op jit(solution)/shard_map/ppermute | solution.py:269
  26.9 0.0 copy-done
  26.9 0.0 copy-done.1
  26.9 0.0 copy-done.2
  26.9 0.0 copy-done.3
  26.9 1.5 %near.1 = (f32[1,72,128]{2,1,0:T(8,128)S(1)}, f32[1,72,128]{2,1,0:T(8,128)S(1)}, f32[160,128]{1,0:T(8,128)S(1)}) custom-call(s32[1]{0:T(128)S(6)} %copy.10.length_ref, bf16[36,144,128]{2,1,0:T(8,128)(2,1)S(1)} %copy-done, bf16[4,144,128]{2,1,0:T(8,128)(2,1)S(1)} %fusion.1.slab_ref, bf16[128,128]{1,0:T(8,128)(2,1)S(1)} %copy-done.1, ...), custom_call_target="tpu_custom_call" | custom-call | flops 5308416 | bytes 1327104 | tf_op jit(solution)/shard_map/near/pallas_call | solution.py:376
  28.4 0.5 %collective-permute-done.7 = bf16[4,144,128]{2,1,0:T(8,128)(2,1)S(1)} collective-permute-done((bf16[4,144,128]{2,1,0:T(8,128)(2,1)S(1)}, bf16[4,144,128]{2,1,0:T(8,128)(2,1)S(1)}, u32[]{:S(2)}, u32[]{:S(2)}) %collective-permute-start.7) | collective-permute-done | bytes 147488 | tf_op jit(solution)/shard_map/ppermute | solution.py:269
  28.9 1.0 %send.1 = (f32[2,144,128]{2,1,0:T(8,128)S(1)}, bf16[4,144,128]{2,1,0:T(8,128)(2,1)S(1)}, f32[160,128]{1,0:T(8,128)S(1)}) custom-call(s32[1]{0:T(128)S(6)} %copy.10.length_ref, bf16[36,144,128]{2,1,0:T(8,128)(2,1)S(1)} %copy-done, bf16[4,144,128]{2,1,0:T(8,128)(2,1)S(1)} %maximum_select_fusion.slab_ref, bf16[128,128]{1,0:T(8,128)(2,1)S(1)} %copy-done.1, ...), custom_call_target="tpu_custom_call" | custom-call | tf_op jit(solution)/shard_map/send/pallas_call | solution.py:388
  29.9 0.0 copy-start.4
  29.9 0.8 %collective-permute-start.8 = (f32[2,144,128]{2,1,0:T(8,128)S(1)}, f32[2,144,128]{2,1,0:T(8,128)S(1)}, u32[]{:S(2)}, u32[]{:S(2)}) collective-permute-start(f32[2,144,128]{2,1,0:T(8,128)S(1)} %get-tuple-element.28), channel_id=1, source_target_pairs={{0,1},{1,0},{2,3},{3,2},{4,5},{5,4},{6,7},{7,6},{8,9},{9,8},{10,11... | collective-permute-start | bytes 442376 | tf_op jit(solution)/shard_map/ppermute | solution.py:269
  30.7 0.5 %keep.1.keep_ref = f32[2,144,128]{2,1,0:T(8,128)S(1)} custom-call(bf16[36,144,128]{2,1,0:T(8,128)(2,1)S(1)} %copy-done, bf16[4,144,128]{2,1,0:T(8,128)(2,1)S(1)} %get-tuple-element.25.left_ref, f32[160,128]{1,0:T(8,128)S(1)} %get-tuple-element.26.gates_ref, f32[1,72,128]{2,1,0:T(8,128)S(1)} %get-tuple-element.27.near_sums_ref, ...), custom_call_target="tpu_custom_call" | custom-call | flops 5308416 | bytes 1327104 | tf_op jit(solution)/shard_map/keep/pallas_call | solution.py:401
  31.2 0.5 %collective-permute-done.8.got_ref = f32[2,144,128]{2,1,0:T(8,128)S(1)} collective-permute-done((f32[2,144,128]{2,1,0:T(8,128)S(1)}, f32[2,144,128]{2,1,0:T(8,128)S(1)}, u32[]{:S(2)}, u32[]{:S(2)}) %collective-permute-start.8) | collective-permute-done | bytes 147488 | tf_op jit(solution)/shard_map/ppermute | solution.py:269
  31.7 0.0 copy-done.4
  31.7 0.9 %last.1 = bf16[18,8,128]{2,1,0:T(8,128)(2,1)} custom-call(f32[2,144,128]{2,1,0:T(8,128)S(1)} %keep.1.keep_ref, f32[2,144,128]{2,1,0:T(8,128)S(1)} %collective-permute-done.8.got_ref, bf16[128,128]{1,0:T(8,128)(2,1)S(1)} %copy-done.4), custom_call_target="tpu_custom_call" | custom-call | tf_op jit(solution)/shard_map/last/pallas_call | solution.py:413
  (10 shorter events, 0.2 us)
Async XLA Ops:
  0.0 17.4 %collective-permute-start = (bf16[1,288,128]{2,1,0:T(8,128)(2,1)}, bf16[1,288,128]{2,1,0:T(8,128)(2,1)S(1)}, u32[]{:S(2)}, u32[]{:S(2)}) collective-permute-start(bf16[1,288,128]{2,1,0:T(8,128)(2,1)} %param.10), channel_id=1, source_target_pairs={{0,3},{2,1},{4,7},{6,5},{8,11},{10,9},{12,15},{14,13},{16,19},{18,... | collective-permute-start | bytes 221192 | tf_op jit(solution)/shard_map/ppermute | solution.py:269
  4.3 21.2 %collective-permute-start.3 = (bf16[1,288,128]{2,1,0:T(8,128)(2,1)}, bf16[1,288,128]{2,1,0:T(8,128)(2,1)S(1)}, u32[]{:S(2)}, u32[]{:S(2)}) collective-permute-start(bf16[1,288,128]{2,1,0:T(8,128)(2,1)} %param.10), channel_id=1, source_target_pairs={{0,9},{2,11},{4,13},{6,15},{8,1},{10,3},{12,5},{14,7},{16,25},{18,... | collective-permute-start | bytes 221192 | tf_op jit(solution)/shard_map/ppermute | solution.py:269
  6.7 18.8 %collective-permute-start.4 = (bf16[1,288,128]{2,1,0:T(8,128)(2,1)}, bf16[1,288,128]{2,1,0:T(8,128)(2,1)S(1)}, u32[]{:S(2)}, u32[]{:S(2)}) collective-permute-start(bf16[1,288,128]{2,1,0:T(8,128)(2,1)} %param.10), channel_id=1, source_target_pairs={{0,11},{2,9},{4,15},{6,13},{8,3},{10,1},{12,7},{14,5},{16,27},{18,... | collective-permute-start | bytes 221192 | tf_op jit(solution)/shard_map/ppermute | solution.py:269
  8.9 16.6 %collective-permute-start.5 = (bf16[1,288,128]{2,1,0:T(8,128)(2,1)}, bf16[1,288,128]{2,1,0:T(8,128)(2,1)S(1)}, u32[]{:S(2)}, u32[]{:S(2)}) collective-permute-start(bf16[1,288,128]{2,1,0:T(8,128)(2,1)} %param.10), channel_id=1, source_target_pairs={{0,13},{2,15},{4,9},{6,11},{8,5},{10,7},{12,1},{14,3},{16,29},{18,... | collective-permute-start | bytes 221192 | tf_op jit(solution)/shard_map/ppermute | solution.py:269
  10.3 15.2 %collective-permute-start.6 = (bf16[1,288,128]{2,1,0:T(8,128)(2,1)}, bf16[1,288,128]{2,1,0:T(8,128)(2,1)S(1)}, u32[]{:S(2)}, u32[]{:S(2)}) collective-permute-start(bf16[1,288,128]{2,1,0:T(8,128)(2,1)} %param.10), channel_id=1, source_target_pairs={{0,15},{2,13},{4,11},{6,9},{8,7},{10,5},{12,3},{14,1},{16,31},{18,... | collective-permute-start | bytes 221192 | tf_op jit(solution)/shard_map/ppermute | solution.py:269
  13.2 4.3 %copy-start.5 = (bf16[1,288,128]{2,1,0:T(8,128)(2,1)S(1)}, bf16[1,288,128]{2,1,0:T(8,128)(2,1)}, u32[]{:S(2)}) copy-start(bf16[1,288,128]{2,1,0:T(8,128)(2,1)} %param.10) | copy-start | bytes 221188
  17.4 9.5 %copy-start = (bf16[36,144,128]{2,1,0:T(8,128)(2,1)S(1)}, bf16[36,144,128]{2,1,0:T(8,128)(2,1)}, u32[]{:S(2)}) copy-start(bf16[36,144,128]{2,1,0:T(8,128)(2,1)} %right.1.right_ref) | copy-start | bytes 3981316
  17.4 9.5 %copy-start.1 = (bf16[128,128]{1,0:T(8,128)(2,1)S(1)}, bf16[128,128]{1,0:T(8,128)(2,1)}, u32[]{:S(2)}) copy-start(bf16[128,128]{1,0:T(8,128)(2,1)} %gate_ref.5) | copy-start | bytes 98308
  17.4 9.5 %copy-start.2 = (bf16[128,128]{1,0:T(8,128)(2,1)S(1)}, bf16[128,128]{1,0:T(8,128)(2,1)}, u32[]{:S(2)}) copy-start(bf16[128,128]{1,0:T(8,128)(2,1)} %weight_ref.6) | copy-start | bytes 98308
  17.4 9.5 %copy-start.3 = (bf16[128,128]{1,0:T(8,128)(2,1)S(1)}, bf16[128,128]{1,0:T(8,128)(2,1)}, u32[]{:S(2)}) copy-start(bf16[128,128]{1,0:T(8,128)(2,1)} %out_gate_ref.3) | copy-start | bytes 98308
  17.5 6.6 %collective-permute-start.1 = (bf16[2,288,128]{2,1,0:T(8,128)(2,1)S(1)}, bf16[2,288,128]{2,1,0:T(8,128)(2,1)S(1)}, u32[]{:S(2)}, u32[]{:S(2)}) collective-permute-start(bf16[2,288,128]{2,1,0:T(8,128)(2,1)S(1)} %pad_maximum_fusion.2), channel_id=1, source_target_pairs={{1,4},{3,6},{5,0},{7,2},{9,12},{11,14},{13,8},{15,10},{17,20},{19,... | collective-permute-start | bytes 442376 | tf_op jit(solution)/shard_map/ppermute | solution.py:269
  24.1 1.3 %collective-permute-start.2 = (bf16[2,144,128]{2,1,0:T(8,128)(2,1)S(1)}, bf16[2,144,128]{2,1,0:T(8,128)(2,1)S(1)}, u32[]{:S(2)}, u32[]{:S(2)}) collective-permute-start(bf16[2,144,128]{2,1,0:T(8,128)(2,1)S(1)} %get-tuple-element.29), channel_id=1, source_target_pairs={{0,1},{1,0},{2,3},{3,2},{4,5},{5,4},{6,7},{7,6},{8,9},{9,8},{10,11... | collective-permute-start | bytes 221192 | tf_op jit(solution)/shard_map/ppermute | solution.py:269
  25.6 3.3 %collective-permute-start.7 = (bf16[4,144,128]{2,1,0:T(8,128)(2,1)S(1)}, bf16[4,144,128]{2,1,0:T(8,128)(2,1)S(1)}, u32[]{:S(2)}, u32[]{:S(2)}) collective-permute-start(bf16[4,144,128]{2,1,0:T(8,128)(2,1)S(1)} %pad_maximum_fusion.3), channel_id=1, source_target_pairs={{1,0},{3,2},{5,4},{7,6},{9,8},{11,10},{13,12},{15,14},{17,16},{19,... | collective-permute-start | bytes 442376 | tf_op jit(solution)/shard_map/ppermute | solution.py:269
  29.9 1.8 %copy-start.4 = (bf16[128,128]{1,0:T(8,128)(2,1)S(1)}, bf16[128,128]{1,0:T(8,128)(2,1)}, u32[]{:S(2)}) copy-start(bf16[128,128]{1,0:T(8,128)(2,1)} %weight_ref.7) | copy-start | bytes 98308
  29.9 1.8 %collective-permute-start.8 = (f32[2,144,128]{2,1,0:T(8,128)S(1)}, f32[2,144,128]{2,1,0:T(8,128)S(1)}, u32[]{:S(2)}, u32[]{:S(2)}) collective-permute-start(f32[2,144,128]{2,1,0:T(8,128)S(1)} %get-tuple-element.28), channel_id=1, source_target_pairs={{0,1},{1,0},{2,3},{3,2},{4,5},{5,4},{6,7},{7,6},{8,9},{9,8},{10,11... | collective-permute-start | bytes 442376 | tf_op jit(solution)/shard_map/ppermute | solution.py:269

commit v6 on v5

v6 whole, which is shorter than its diff:
```python
import functools

import jax
import jax.numpy as jnp
from jax import lax
from jax.experimental import pallas as pl
from jax.experimental.pallas import tpu as pltpu
from jax.sharding import PartitionSpec as P

EPS = 1e-05
F32 = jnp.float32
BF16 = jnp.bfloat16


def divisor(total, limit, step=1):
    return max(d for d in range(step, total + 1, step) if total % d == 0 and (d <= limit or d == step))


def centering(width):
    row = lax.broadcasted_iota(jnp.int32, (2 * width, 2 * width), 0)
    col = lax.broadcasted_iota(jnp.int32, (2 * width, 2 * width), 1)
    share = jnp.where((row < width) == (col < width), 1.0 / width, 0.0)
    center = jnp.where(row == col, 1.0, 0.0) - share
    return center.astype(BF16), share.astype(BF16)


def normed(first, second, center, share):
    wide = jnp.concatenate([first, second], axis=1)
    d = jnp.dot(wide, center, preferred_element_type=F32)
    var = jnp.dot((d * d).astype(BF16), share, preferred_element_type=F32)
    return (d * lax.rsqrt(var + EPS)).astype(BF16)


def gated(n, both):
    width = both.shape[1] // 2
    y = jnp.dot(n, both, preferred_element_type=F32)
    value = y[:, width:]
    return value + value * jnp.tanh(y[:, :width])


def right_kernel(
    length_ref, pair_ref, weight_ref, gate_ref, out_ref, x_ref, y_ref, w_ref, count_ref, small_sems, in_sems, out_sems,
    *, chunk,
):
    rows, cols, width = pair_ref.shape
    turns = rows // chunk

    def piece(turn, src, dst, sems):
        here = pl.ds(turn * chunk, chunk)
        return pltpu.make_async_copy(src.at[here], dst.at[here], sems.at[turn])

    small = [
        pltpu.make_async_copy(src, dst, small_sems.at[n])
        for n, (src, dst) in enumerate(
            ((length_ref, count_ref), (gate_ref, w_ref.at[0]), (weight_ref, w_ref.at[1]))
        )
    ]
    for copy in small:
        copy.start()
    for turn in range(turns):
        piece(turn, pair_ref, x_ref, in_sems).start()
    for copy in small:
        copy.wait()
    half = jnp.asarray(0.5, BF16)
    both = jnp.concatenate([w_ref[0] * half, w_ref[1] * half], axis=1)
    live = count_ref[0]
    first_j = lax.axis_index("row") * rows
    center, share = centering(width)
    k = lax.axis_index("col") * cols + lax.broadcasted_iota(jnp.int32, (cols, width), 0)

    def some(turn, _):
        piece(turn, pair_ref, x_ref, in_sems).wait()
        j0 = turn * chunk
        x = x_ref[pl.ds(j0, chunk)].reshape(2, chunk * cols // 2, width)
        n = normed(x[0], x[1], center, share)
        for part in range(2):
            edge = gated(n[:, part * width : (part + 1) * width], both).reshape(chunk // 2, cols, width)
            for r in range(chunk // 2):
                j = j0 + part * (chunk // 2) + r
                reach = jnp.where(first_j + j < live, live, 0)
                y_ref[j] = jnp.where(k < reach, edge[r], 0.0).astype(BF16)
        piece(turn, y_ref, out_ref, out_sems).start()
        return 0

    lax.fori_loop(0, turns, some, 0)
    for turn in range(turns):
        piece(turn, y_ref, out_ref, out_sems).wait()


def fold(parts):
    place = lax.broadcasted_iota(jnp.int32, parts[0].shape, 0)
    for step in (1, 2, 4):
        here = (place & step) == 0
        parts = [
            jnp.where(here, a, b) + pltpu.roll(jnp.where(here, b, a), 8 - step, 0)
            for a, b in zip(parts[0::2], parts[1::2])
        ]
    return parts[0]


def block_of(blocks):
    return 0 if blocks == 1 else pl.program_id(0)


def only(condition, blocks, body):
    if blocks == 1:
        body()
    else:
        pl.when(condition)(body)


def contract(left_ref, right_ref, j_half, dest_ref, blocks):
    slabs, depth, _ = left_ref.shape
    rows = right_ref.shape[0] // 2
    group = divisor(rows, 3)

    def tile(turn, _):
        i0 = turn // (rows // group) * 8
        j0 = lax.rem(turn, rows // group) * group
        first = j_half * rows + j0
        sums = [[None] * 8 for _ in range(group)]
        for k0 in range(0, depth, 16):
            edges = [right_ref[first + j, pl.ds(k0, 16), :].astype(F32) for j in range(group)]
            for i in range(8):
                left = left_ref[i0 + i, pl.ds(k0, 16), :].astype(F32)
                for j in range(group):
                    term = left * edges[j]
                    term = term[:8] + term[8:]
                    sums[j][i] = term if k0 == 0 else sums[j][i] + term
        for j in range(group):
            dest = dest_ref.at[0, pl.ds(pl.multiple_of((j0 + j) * slabs + i0, 8), 8), :]
            total = fold(sums[j])
            dest[...] = total if blocks == 1 else jnp.where(block_of(blocks) == 0, total, total + dest[...])
        return 0

    lax.fori_loop(0, slabs // 8 * (rows // group), tile, 0)


def send_kernel(
    length_ref, right_ref, slab_ref, gate_ref, weight_ref, out_gate_ref,
    send_ref, left_ref, own_gates_ref, norm_ref, *, blocks,
):
    slabs, depth, width = slab_ref.shape
    half_rows = right_ref.shape[0] // 2
    half_cols = depth * blocks
    side = lax.axis_index("col")
    half = jnp.asarray(0.5, BF16)
    center, share = centering(width)
    both = jnp.concatenate([gate_ref[...] * half, weight_ref[...] * half], axis=1)
    first_k = side * half_cols + block_of(blocks) * depth
    live = first_k + lax.broadcasted_iota(jnp.int32, (depth, width), 0) < length_ref[0]

    def quad(q):
        s = q * 4
        x = slab_ref[pl.ds(s, 4)].reshape(2, 2 * depth, width)
        n = normed(x[0], x[1], center, share)
        for part in range(2):
            own = n[:, part * width : (part + 1) * width]
            edge = gated(own, both)
            norm_ref[pl.ds(pl.multiple_of((s + 2 * part) * depth, 16), 2 * depth), :] = own.astype(F32)
            for r in range(2):
                kept = jnp.where(live, edge[r * depth : (r + 1) * depth], 0.0)
                left_ref[s + 2 * part + r] = kept.astype(BF16).astype(left_ref.dtype)

    if slabs <= 8:
        for q in range(slabs // 4):
            quad(q)
    else:
        pl.loop(0, slabs // 4)(quad)

    first_j = lax.rem(lax.axis_index("row") * (2 * half_rows), half_cols)
    start = lax.rem(first_j, depth)

    def gates():
        for place, dest in ((1 - side, send_ref.at[1]), (side, own_gates_ref)):
            rows = [
                norm_ref[pl.ds(start + place * half_rows + j, slabs, stride=depth), :] for j in range(half_rows)
            ]
            rows = jnp.concatenate(rows, axis=0).astype(BF16)
            y = jnp.dot(rows, out_gate_ref[...] * half, preferred_element_type=F32)
            dest[...] = (0.5 + 0.5 * jnp.tanh(y)).astype(BF16).astype(F32)

    only(block_of(blocks) == first_j // depth, blocks, gates)
    contract(left_ref, right_ref, 1 - side, send_ref, blocks)


def keep_kernel(right_ref, left_ref, keep_ref, *, blocks):
    contract(left_ref, right_ref, lax.axis_index("col"), keep_ref, blocks)


def last_kernel(keep_ref, own_gates_ref, got_ref, weight_ref, out_ref, *, half_cols):
    rows_dev = 2 * out_ref.shape[0]
    tri = keep_ref[0] + got_ref[0]
    d = tri - jnp.mean(tri, axis=-1, keepdims=True)
    var = jnp.mean(d * d, axis=-1, keepdims=True)
    n = (d * lax.rsqrt(var + EPS)).astype(BF16)
    projected = jnp.dot(n, weight_ref[...], preferred_element_type=F32)
    mine = lax.axis_index("row") * rows_dev // half_cols == lax.axis_index("col")
    update = projected * jnp.where(mine, own_gates_ref[...], got_ref[1])
    out_ref[...] = update.astype(BF16).reshape(out_ref.shape)


def spread_kernel(slab_ref, out_ref):
    count, half_cols, _ = out_ref.shape
    own = slab_ref[0, pl.ds(pl.multiple_of(lax.axis_index("col") * half_cols, 16), half_cols), :]
    for row in range(count):
        out_ref[row] = own


def shards(pair_rep, slab_rep, length, weight_a, gate_a, weight_b, gate_b, weight_gate, weight_out):
    rows_dev, half_cols, width = pair_rep.shape
    hidden = weight_a.shape[1]
    count = lax.axis_size("row")
    half_rows = rows_dev // 2
    depth = divisor(half_cols, 144, rows_dev)
    blocks = half_cols // depth
    grid = () if blocks == 1 else (blocks,)
    hbm = pl.BlockSpec(memory_space=pltpu.HBM)
    smem = pl.BlockSpec(memory_space=pltpu.SMEM)
    vmem = pl.BlockSpec(memory_space=pltpu.VMEM)
    params = pltpu.CompilerParams(vmem_limit_bytes=40 << 20)

    def whole(*shape):
        return vmem if blocks == 1 else pl.BlockSpec(shape, lambda *_: (0,) * len(shape))

    def deep(rows):
        return vmem if blocks == 1 else pl.BlockSpec((rows, depth, width), lambda k: (0, k, 0))

    spread = pl.pallas_call(
        spread_kernel,
        out_shape=jax.ShapeDtypeStruct((count, half_cols, width), BF16),
        in_specs=[vmem],
        out_specs=vmem,
        compiler_params=params,
        name="spread",
    )(slab_rep)
    spread, length = lax.optimization_barrier((spread, length))
    slabs = lax.all_to_all(spread, "row", split_axis=0, concat_axis=0, tiled=True)

    chunk = divisor(rows_dev, max(2, 1728 // half_cols), 2)
    turns = rows_dev // chunk
    right = pl.pallas_call(
        functools.partial(right_kernel, chunk=chunk),
        out_shape=jax.ShapeDtypeStruct((rows_dev, half_cols, hidden), BF16),
        in_specs=[hbm] * 4,
        out_specs=hbm,
        scratch_shapes=[
            pltpu.VMEM((rows_dev, half_cols, width), BF16),
            pltpu.VMEM((rows_dev, half_cols, hidden), BF16),
            pltpu.VMEM((2, width, hidden), BF16),
            pltpu.SMEM((1,), jnp.int32),
            pltpu.SemaphoreType.DMA((3,)),
            pltpu.SemaphoreType.DMA((turns,)),
            pltpu.SemaphoreType.DMA((turns,)),
        ],
        compiler_params=pltpu.CompilerParams(vmem_limit_bytes=58 << 20),
        cost_estimate=pl.CostEstimate(
            flops=2 * rows_dev * half_cols * width * hidden * 6,
            bytes_accessed=4 * rows_dev * half_cols * width,
            transcendentals=2 * rows_dev * half_cols * width,
        ),
        name="right",
    )(length, pair_rep, weight_b, gate_b)

    swapped = jax.ShapeDtypeStruct((2, half_rows * count, hidden), F32)
    kept = jax.ShapeDtypeStruct((1, half_rows * count, hidden), F32)
    gates = jax.ShapeDtypeStruct((half_rows * count, width), F32)
    send, left, own_gates = pl.pallas_call(
        functools.partial(send_kernel, blocks=blocks),
        out_shape=(swapped, jax.ShapeDtypeStruct((count, half_cols, hidden), F32 if blocks == 1 else BF16), gates),
        grid=grid,
        in_specs=[
            smem, deep(rows_dev), deep(count), whole(width, hidden), whole(width, hidden), whole(width, width),
        ],
        out_specs=(whole(*swapped.shape), deep(count), whole(*gates.shape)),
        scratch_shapes=[pltpu.VMEM((count * depth, width), F32)],
        compiler_params=params,
        name="send",
    )(length, right, slabs, gate_a, weight_a, weight_gate)

    got = lax.ppermute(send, "col", [(0, 1), (1, 0)])

    keep = pl.pallas_call(
        functools.partial(keep_kernel, blocks=blocks),
        out_shape=kept,
        grid=grid,
        in_specs=[deep(rows_dev), deep(count)],
        out_specs=whole(*kept.shape),
        compiler_params=params,
        cost_estimate=pl.CostEstimate(
            flops=rows_dev * half_cols * count * hidden,
            bytes_accessed=2 * rows_dev * half_cols * width,
            transcendentals=0,
        ),
        name="keep",
    )(right, left)

    update = pl.pallas_call(
        functools.partial(last_kernel, half_cols=half_cols),
        out_shape=jax.ShapeDtypeStruct((half_rows, count, width), BF16),
        in_specs=[vmem] * 4,
        out_specs=vmem,
        compiler_params=pltpu.CompilerParams(vmem_limit_bytes=32 << 20),
        name="last",
    )(keep, own_gates, got, weight_out)
    return jnp.transpose(update, (1, 0, 2))


def solution(mesh):
    placed = (
        P(("groups", "row"), "col", None),
        P(("groups", "row"), None, None),
        P("groups"),
        P(),
        P(),
        P(),
        P(),
        P(),
        P(),
    )
    return jax.shard_map(
        shards,
        mesh=mesh,
        in_specs=placed,
        out_specs=P("groups", ("row", "col"), None),
        check_vma=False,
    )
```

time: 32.9 us -> 24.4 us (0.74)
  starting transfers between devices: 16 us -> 7.32 us
  waiting for transfers between devices: 7.34 us -> 5.18 us
  local copies, waits for them, and re-layouts: 0.08 us -> 2.22 us
  Pallas kernels: 8.12 us -> 8.6 us
    ppermute x9 -> x1, starting transfers between devices: 16 us -> 0.07 us  [shards(): got = lax.ppermute(send, 'col', [(0, 1), (1, 0)])]
    all_to_all x0 -> x1, starting transfers between devices: none -> 7.25 us  [shards(): lax.all_to_all(spread, 'row', split_axis=0, concat_axis=0, tiled=True)]
    ppermute x9 -> x1, waiting for transfers between devices: 7.34 us -> 0.43 us  [shards(): got = lax.ppermute(send, 'col', [(0, 1), (1, 0)])]
    all_to_all x0 -> x1, waiting for transfers between devices: none -> 4.74 us  [shards(): lax.all_to_all(spread, 'row', split_axis=0, concat_axis=0, tiled=True)]
    unnamed x12, local copies, waits for them, and re-layouts: 0.03 us -> 2.22 us
    pallas_call x4, Pallas kernels: 7.19 us -> 7.67 us  [the longest x1 4.18 us: shards(): pl.pallas_call(functools.partial(right_kernel, chunk=chunk), out_shape=ja...]
  transfers between devices with their start and end apart: 9 -> 2, of which waited for: 4 -> 2; matrix products, arithmetic and copies ran while one was open for 0% -> 0% of each run, Pallas kernels for 19% -> 21%
where the time goes in v6:
time: 24.4 us; the launch traced here: 24 us
  Pallas kernels  8.6 us (35%)
  starting transfers between devices  7.32 us (30%)
  waiting for transfers between devices  5.18 us (21%)
  local copies, waits for them, and re-layouts  2.22 us (9%)
  between operations  0.72 us (3%)
    all_to_all x1, starting transfers between devices, shards(): lax.all_to_all(spread, 'row', split_axis=0, concat_axis=0, tiled=True)  7.25 us
    all_to_all x1, waiting for transfers between devices, shards(): lax.all_to_all(spread, 'row', split_axis=0, concat_axis=0, tiled=True)  4.74 us
    pallas_call x1, Pallas kernels, shards(): pl.pallas_call(functools.partial(right_kernel, chunk=chunk), out_shape=ja...  4.18 us
    unnamed x12, local copies, waits for them, and re-layouts  2.22 us
    pallas_call x1, Pallas kernels, shards(): pl.pallas_call(functools.partial(send_kernel, blocks=blocks), out_shape=(...  1.81 us
    pallas_call x1, Pallas kernels, shards(): pl.pallas_call(functools.partial(last_kernel, half_cols=half_cols), out_s...  0.93 us
    pallas_call x1, Pallas kernels, shards(): pl.pallas_call(functools.partial(keep_kernel, blocks=blocks), out_shape=k...  0.92 us
    pallas_call x1, Pallas kernels, shards(): pl.pallas_call(spread_kernel, out_shape=jax.ShapeDtypeStruct((count, half...  0.76 us
  transfers between devices with their start and end apart: 2, of which 2 were waited for; matrix products, arithmetic and copies ran while one was open for 0% of the time, Pallas kernels for 21%

profile of v6, /device:TPU:0, one launch (start us, length us, event | category | flops | bytes accessed | tf_op | source)
XLA Modules:
  0.0 24.0 jit_solution(17857788829517395972)
XLA Ops:
  0.0 0.0 copy-start.1
  0.0 0.9 %copy-done.1 = bf16[1,288,128]{2,1,0:T(8,128)(2,1)S(1)} copy-done((bf16[1,288,128]{2,1,0:T(8,128)(2,1)S(1)}, bf16[1,288,128]{2,1,0:T(8,128)(2,1)}, u32[]{:S(2)}) %copy-start.1) | copy-done | bytes 73752
  0.9 0.8 %spread.1 = bf16[8,144,128]{2,1,0:T(8,128)(2,1)} custom-call(bf16[1,288,128]{2,1,0:T(8,128)(2,1)S(1)} %copy-done.1), custom_call_target="tpu_custom_call" | custom-call | tf_op jit(solution)/shard_map/spread/pallas_call | solution.py:229
  1.6 7.3 %all-to-all-start = ((bf16[8,144,128]{2,1,0:T(8,128)(2,1)}), bf16[8,144,128]{2,1,0:T(8,128)(2,1)S(1)}, u32[]{:S(2)}, u32[]{:S(2)}) async-start(bf16[8,144,128]{2,1,0:T(8,128)(2,1)} %spread.1), calls=%async_computation | async-start | bytes 589824 | tf_op jit(solution)/shard_map/all_to_all | solution.py:238
  9.6 0.0 copy-start.2
  9.6 0.0 copy-start.3
  9.6 0.0 copy-start.4
  9.6 4.2 %right.1.right_ref = bf16[36,144,128]{2,1,0:T(8,128)(2,1)} custom-call(s32[1]{0:T(128)S(6)} %copy.10.length_ref, bf16[36,144,128]{2,1,0:T(8,128)(2,1)} %pair_ref.1, bf16[128,128]{1,0:T(8,128)(2,1)} %weight_ref.3, bf16[128,128]{1,0:T(8,128)(2,1)} %gate_ref.2), custom_call_target="tpu_custom_call" | custom-call | flops 1019215872 | bytes 2654208 | tf_op jit(solution)/shard_map/right/pallas_call | solution.py:242
  13.8 4.7 %all-to-all-done.slab_ref = bf16[8,144,128]{2,1,0:T(8,128)(2,1)S(1)} async-done(((bf16[8,144,128]{2,1,0:T(8,128)(2,1)}), bf16[8,144,128]{2,1,0:T(8,128)(2,1)S(1)}, u32[]{:S(2)}, u32[]{:S(2)}) %all-to-all-start) | async-done | bytes 294944 | tf_op jit(solution)/shard_map/all_to_all | solution.py:238
  18.5 0.0 copy-done.2
  18.5 0.0 copy-done.3
  18.5 0.0 copy-done.4
  18.5 0.0 copy-start
  18.5 1.3 %copy-done = bf16[36,144,128]{2,1,0:T(8,128)(2,1)S(1)} copy-done((bf16[36,144,128]{2,1,0:T(8,128)(2,1)S(1)}, bf16[36,144,128]{2,1,0:T(8,128)(2,1)}, u32[]{:S(2)}) %copy-start) | copy-done | bytes 1327128
  19.9 1.8 %send.1 = (f32[2,144,128]{2,1,0:T(8,128)S(1)}, f32[8,144,128]{2,1,0:T(8,128)S(1)}, f32[144,128]{1,0:T(8,128)S(1)}) custom-call(s32[1]{0:T(128)S(6)} %copy.10.length_ref, bf16[36,144,128]{2,1,0:T(8,128)(2,1)S(1)} %copy-done, bf16[8,144,128]{2,1,0:T(8,128)(2,1)S(1)} %all-to-all-done.slab_ref, bf16[128,128]{1,0:T(8,128)(2,1)S(1)} %copy-done.2, ...), custom_call_target="tpu_custom_call" | custom-call | tf_op jit(solution)/shard_map/send/pallas_call | solution.py:268
  21.7 0.0 copy-start.5
  21.7 0.1 collective-permute-start
  21.8 0.9 %keep.1.keep_ref = f32[1,144,128]{2,1,0:T(8,128)S(1)} custom-call(bf16[36,144,128]{2,1,0:T(8,128)(2,1)S(1)} %copy-done, f32[8,144,128]{2,1,0:T(8,128)S(1)} %get-tuple-element.12.left_ref), custom_call_target="tpu_custom_call" | custom-call | flops 5308416 | bytes 1327104 | tf_op jit(solution)/shard_map/keep/pallas_call | solution.py:283
  22.7 0.4 %collective-permute-done.got_ref = f32[2,144,128]{2,1,0:T(8,128)S(1)} collective-permute-done((f32[2,144,128]{2,1,0:T(8,128)S(1)}, f32[2,144,128]{2,1,0:T(8,128)S(1)}, u32[]{:S(2)}, u32[]{:S(2)}) %collective-permute-start) | collective-permute-done | bytes 147488 | tf_op jit(solution)/shard_map/ppermute | solution.py:281
  23.1 0.0 copy-done.5
  23.1 0.9 %last.1 = bf16[18,8,128]{2,1,0:T(8,128)(2,1)} custom-call(f32[1,144,128]{2,1,0:T(8,128)S(1)} %keep.1.keep_ref, f32[144,128]{1,0:T(8,128)S(1)} %get-tuple-element.13.own_gates_ref, f32[2,144,128]{2,1,0:T(8,128)S(1)} %collective-permute-done.got_ref, bf16[128,128]{1,0:T(8,128)(2,1)S(1)} %copy-done.5), custom_call_target="tpu_custom_call" | custom-call | tf_op jit(solution)/shard_map/last/pallas_call | solution.py:298
Async XLA Ops:
  0.0 0.9 %copy-start.1 = (bf16[1,288,128]{2,1,0:T(8,128)(2,1)S(1)}, bf16[1,288,128]{2,1,0:T(8,128)(2,1)}, u32[]{:S(2)}) copy-start(bf16[1,288,128]{2,1,0:T(8,128)(2,1)} %slab_ref.1) | copy-start | bytes 221188
  1.6 16.9 %all-to-all-start = ((bf16[8,144,128]{2,1,0:T(8,128)(2,1)}), bf16[8,144,128]{2,1,0:T(8,128)(2,1)S(1)}, u32[]{:S(2)}, u32[]{:S(2)}) async-start(bf16[8,144,128]{2,1,0:T(8,128)(2,1)} %spread.1), calls=%async_computation | async-start | bytes 589824 | tf_op jit(solution)/shard_map/all_to_all | solution.py:238
  9.6 9.0 %copy-start.2 = (bf16[128,128]{1,0:T(8,128)(2,1)S(1)}, bf16[128,128]{1,0:T(8,128)(2,1)}, u32[]{:S(2)}) copy-start(bf16[128,128]{1,0:T(8,128)(2,1)} %gate_ref.3) | copy-start | bytes 98308
  9.6 9.0 %copy-start.3 = (bf16[128,128]{1,0:T(8,128)(2,1)S(1)}, bf16[128,128]{1,0:T(8,128)(2,1)}, u32[]{:S(2)}) copy-start(bf16[128,128]{1,0:T(8,128)(2,1)} %weight_ref.4) | copy-start | bytes 98308
  9.6 9.0 %copy-start.4 = (bf16[128,128]{1,0:T(8,128)(2,1)S(1)}, bf16[128,128]{1,0:T(8,128)(2,1)}, u32[]{:S(2)}) copy-start(bf16[128,128]{1,0:T(8,128)(2,1)} %out_gate_ref.1) | copy-start | bytes 98308
  18.5 1.3 %copy-start = (bf16[36,144,128]{2,1,0:T(8,128)(2,1)S(1)}, bf16[36,144,128]{2,1,0:T(8,128)(2,1)}, u32[]{:S(2)}) copy-start(bf16[36,144,128]{2,1,0:T(8,128)(2,1)} %right.1.right_ref) | copy-start | bytes 3981316
  21.7 1.5 %copy-start.5 = (bf16[128,128]{1,0:T(8,128)(2,1)S(1)}, bf16[128,128]{1,0:T(8,128)(2,1)}, u32[]{:S(2)}) copy-start(bf16[128,128]{1,0:T(8,128)(2,1)} %weight_ref.5) | copy-start | bytes 98308
  21.7 1.4 %collective-permute-start = (f32[2,144,128]{2,1,0:T(8,128)S(1)}, f32[2,144,128]{2,1,0:T(8,128)S(1)}, u32[]{:S(2)}, u32[]{:S(2)}) collective-permute-start(f32[2,144,128]{2,1,0:T(8,128)S(1)} %get-tuple-element.14), channel_id=1, source_target_pairs={{0,1},{1,0},{2,3},{3,2},{4,5},{5,4},{6,7},{7,6},{8,9},{9,8},{10,11... | collective-permute-start | bytes 442376 | tf_op jit(solution)/shard_map/ppermute | solution.py:281

commit v7 on v5

--- a/solution.py
+++ b/solution.py
@@ -52,38 +52,25 @@
     return value + value * jnp.tanh(y[:, :width])
 
 
-def right_kernel(
-    length_ref, pair_ref, weight_ref, gate_ref, out_ref, x_ref, y_ref, w_ref, count_ref, small_sems, in_sems, out_sems,
-    *, chunk,
-):
+def right_kernel(length_ref, weight_ref, gate_ref, pair_ref, out_ref, x_ref, sems, *, chunk):
     rows, cols, width = pair_ref.shape
     turns = rows // chunk
 
-    def piece(turn, src, dst, sems):
+    def piece(turn):
         here = pl.ds(turn * chunk, chunk)
-        return pltpu.make_async_copy(src.at[here], dst.at[here], sems.at[turn])
-
-    small = [
-        pltpu.make_async_copy(src, dst, small_sems.at[n])
-        for n, (src, dst) in enumerate(
-            ((length_ref, count_ref), (gate_ref, w_ref.at[0]), (weight_ref, w_ref.at[1]))
-        )
-    ]
-    for copy in small:
-        copy.start()
+        return pltpu.make_async_copy(pair_ref.at[here], x_ref.at[here], sems.at[turn])
+
     for turn in range(turns):
-        piece(turn, pair_ref, x_ref, in_sems).start()
-    for copy in small:
-        copy.wait()
+        piece(turn).start()
     half = jnp.asarray(0.5, BF16)
-    both = jnp.concatenate([w_ref[0] * half, w_ref[1] * half], axis=1)
-    live = count_ref[0]
+    both = jnp.concatenate([gate_ref[...] * half, weight_ref[...] * half], axis=1)
+    live = length_ref[0]
     first_j = lax.axis_index("row") * rows
     center, share = centering(width)
     k = lax.axis_index("col") * cols + lax.broadcasted_iota(jnp.int32, (cols, width), 0)
 
     def some(turn, _):
-        piece(turn, pair_ref, x_ref, in_sems).wait()
+        piece(turn).wait()
         j0 = turn * chunk
         x = x_ref[pl.ds(j0, chunk)].reshape(2, chunk * cols // 2, width)
         n = normed(x[0], x[1], center, share)
@@ -92,13 +79,10 @@
             for r in range(chunk // 2):
                 j = j0 + part * (chunk // 2) + r
                 reach = jnp.where(first_j + j < live, live, 0)
-                y_ref[j] = jnp.where(k < reach, edge[r], 0.0).astype(BF16)
-        piece(turn, y_ref, out_ref, out_sems).start()
+                out_ref[j] = jnp.where(k < reach, edge[r], 0.0).astype(BF16)
         return 0
 
     lax.fori_loop(0, turns, some, 0)
-    for turn in range(turns):
-        piece(turn, y_ref, out_ref, out_sems).wait()
 
 
 def fold(parts):
@@ -287,24 +271,20 @@
     half_cols = half.shape[1]
     side = lax.axis_index("col")
 
-    def out(m):
-        return passed(slab, lambda row, core: (row ^ m, 1) if core == 0 else None)
-
-    far = [out(m) for m in (4, 5, 6, 7)]
-    beside = out(1)
-    both, made = between(jnp.concatenate([slab, beside], axis=0))
-    pair = passed(both, lambda row, core: (row ^ 2, 0) if core == 1 else None)
-    over = jnp.concatenate([beside[:, :half_cols]] * 2, axis=0)
-    over = jnp.where(side == 0, pair[:, half_cols:], over)
+    def out(*m):
+        return passed(slab, lambda row, core: (row ^ m[core], core))
+
+    def part(x, which):
+        return lax.dynamic_slice_in_dim(x, which * half_cols, half_cols, 1)
+
+    steps = ((3, 2), (5, 4), (7, 6), (1, 1))
+    first, second, third, beside = [out(*m) for m in steps]
+    over = jnp.concatenate([part(x, 1 - side) for x in (first, second, third)], axis=0)
+    over, made = between(over)
     over = passed(over, lambda row, core: (row, 1 - core))
-    near0 = jnp.concatenate([half, over[:1], pair[:, :half_cols]], axis=0)
-    near1 = jnp.concatenate([half, beside[:, half_cols:], over], axis=0)
-    near = jnp.where(side == 0, near0, near1)
-    _, far = lax.optimization_barrier((near, far))
-    crossed = jnp.concatenate([x[:, :half_cols] for x in far], axis=0)
-    crossed = passed(crossed, lambda row, core: (row, 0) if core == 1 else None)
-    far = jnp.where(side == 0, crossed, jnp.concatenate([x[:, half_cols:] for x in far], axis=0))
-    return near, far, [[0, 1, 2, 3]] * 2, [[4, 5, 6, 7]] * 2, made
+    near = jnp.concatenate([half, part(beside, side), part(first, side), part(second, side)], axis=0)
+    far = jnp.concatenate([part(third, side), over], axis=0)
+    return near, far, [[0, 1, 3, 5], [0, 1, 2, 4]], [[7, 2, 4, 6], [6, 3, 5, 7]], made
 
 
 def shards(pair_rep, slab_rep, length, weight_a, gate_a, weight_b, gate_b, weight_gate, weight_out):
@@ -333,18 +313,10 @@
     right_call = pl.pallas_call(
         functools.partial(right_kernel, chunk=chunk),
         out_shape=jax.ShapeDtypeStruct((rows_dev, half_cols, hidden), BF16),
-        in_specs=[hbm] * 4,
-        out_specs=hbm,
-        scratch_shapes=[
-            pltpu.VMEM((rows_dev, half_cols, width), BF16),
-            pltpu.VMEM((rows_dev, half_cols, hidden), BF16),
-            pltpu.VMEM((2, width, hidden), BF16),
-            pltpu.SMEM((1,), jnp.int32),
-            pltpu.SemaphoreType.DMA((3,)),
-            pltpu.SemaphoreType.DMA((turns,)),
-            pltpu.SemaphoreType.DMA((turns,)),
-        ],
-        compiler_params=pltpu.CompilerParams(vmem_limit_bytes=58 << 20),
+        in_specs=[smem, vmem, vmem, hbm],
+        out_specs=vmem,
+        scratch_shapes=[pltpu.VMEM((rows_dev, half_cols, width), BF16), pltpu.SemaphoreType.DMA((turns,))],
+        compiler_params=pltpu.CompilerParams(vmem_limit_bytes=52 << 20),
         cost_estimate=pl.CostEstimate(
             flops=2 * rows_dev * half_cols * width * hidden * 6,
             bytes_accessed=4 * rows_dev * half_cols * width,
@@ -354,7 +326,7 @@
     )
 
     def between(held):
-        made, held = lax.optimization_barrier((right_call(length, pair_rep, weight_b, gate_b), held))
+        made, held = lax.optimization_barrier((right_call(length, weight_b, gate_b, pair_rep), held))
         return held, made
 
     half = lax.dynamic_slice_in_dim(slab_rep, side * half_cols, half_cols, 1)

time: 32.9 us -> 19.9 us (0.60)
  starting transfers between devices: 16 us -> 8.61 us
  waiting for transfers between devices: 7.34 us -> 0.5 us
  local copies, waits for them, and re-layouts: 0.08 us -> 2.38 us
  Pallas kernels: 8.12 us -> 7.17 us
    ppermute x9 -> x6, starting transfers between devices: 16 us -> 8.61 us  [passed(): return lax.ppermute(x, ('row', 'col'), pairs)]
    ppermute x9 -> x6, waiting for transfers between devices: 7.34 us -> 0.5 us  [passed(): return lax.ppermute(x, ('row', 'col'), pairs)]
    unnamed x12, local copies, waits for them, and re-layouts: 0.03 us -> 1.53 us
    pallas_call x1, Pallas kernels: 4.2 us -> 3.27 us  [between(): right_call(length, weight_b, gate_b, pair_rep)]
    dynamic_slice x1, local copies, waits for them, and re-layouts: 0.01 us -> 0.78 us  [shards(): half = lax.dynamic_slice_in_dim(slab_rep, side * half_cols, half_cols, 1)]
  transfers between devices with their start and end apart: 9 -> 6, of which waited for: 4 -> 1; matrix products, arithmetic and copies ran while one was open for 0% -> 5% of each run, Pallas kernels for 19% -> 27%
where the time goes in v7:
time: 19.9 us; the launch traced here: 19.5 us
  starting transfers between devices  8.61 us (43%)
  Pallas kernels  7.17 us (36%)
  local copies, waits for them, and re-layouts  2.38 us (12%)
  between operations  0.81 us (4%)
  waiting for transfers between devices  0.5 us (3%)
    ppermute x6, starting transfers between devices, passed(): return lax.ppermute(x, ('row', 'col'), pairs)  8.61 us
    pallas_call x1, Pallas kernels, between(): right_call(length, weight_b, gate_b, pair_rep)  3.27 us
    unnamed x12, local copies, waits for them, and re-layouts  1.53 us
    pallas_call x1, Pallas kernels, shards(): pl.pallas_call(functools.partial(near_kernel, blocks=blocks), out_shape=(...  1.45 us
    pallas_call x1, Pallas kernels, shards(): pl.pallas_call(functools.partial(send_kernel, blocks=blocks, near_places=...  1.01 us
    pallas_call x1, Pallas kernels, shards(): pl.pallas_call(functools.partial(last_kernel, half_cols=half_cols), out_s...  0.93 us
    dynamic_slice x1, local copies, waits for them, and re-layouts, shards(): half = lax.dynamic_slice_in_dim(slab_rep, side * half_cols, half_cols, 1)  0.78 us
    pallas_call x1, Pallas kernels, shards(): pl.pallas_call(functools.partial(keep_kernel, blocks=blocks, near_places=...  0.51 us
  transfers between devices with their start and end apart: 6, of which 1 were waited for; matrix products, arithmetic and copies ran while one was open for 5% of the time, Pallas kernels for 27%

profile of v7, /device:TPU:0, one launch (start us, length us, event | category | flops | bytes accessed | tf_op | source)
XLA Modules:
  0.0 19.5 jit_solution(202328926792056727)
XLA Ops:
  0.0 6.0 %collective-permute-start.2 = (bf16[1,288,128]{2,1,0:T(8,128)(2,1)}, bf16[1,288,128]{2,1,0:T(8,128)(2,1)S(1)}, u32[]{:S(2)}, u32[]{:S(2)}) collective-permute-start(bf16[1,288,128]{2,1,0:T(8,128)(2,1)} %param.10), channel_id=1, source_target_pairs={{0,14},{1,13},{2,12},{3,15},{4,10},{5,9},{6,8},{7,11},{8,6},{9,5},... | collective-permute-start | bytes 221192 | tf_op jit(solution)/shard_map/ppermute | solution.py:253
  6.0 0.0 collective-permute-start.1
  6.0 1.7 %collective-permute-start = (bf16[1,288,128]{2,1,0:T(8,128)(2,1)}, bf16[1,288,128]{2,1,0:T(8,128)(2,1)S(1)}, u32[]{:S(2)}, u32[]{:S(2)}) collective-permute-start(bf16[1,288,128]{2,1,0:T(8,128)(2,1)} %param.10), channel_id=1, source_target_pairs={{0,6},{1,5},{2,4},{3,7},{4,2},{5,1},{6,0},{7,3},{8,14},{9,13},{10,... | collective-permute-start | bytes 221192 | tf_op jit(solution)/shard_map/ppermute | solution.py:253
  7.7 0.3 %collective-permute-start.4 = (bf16[1,288,128]{2,1,0:T(8,128)(2,1)}, bf16[1,288,128]{2,1,0:T(8,128)(2,1)S(1)}, u32[]{:S(2)}, u32[]{:S(2)}) collective-permute-start(bf16[1,288,128]{2,1,0:T(8,128)(2,1)} %param.10), channel_id=1, source_target_pairs={{0,2},{1,3},{2,0},{3,1},{4,6},{5,7},{6,4},{7,5},{8,10},{9,11},{10,... | collective-permute-start | bytes 221192 | tf_op jit(solution)/shard_map/ppermute | solution.py:253
  8.7 0.8 %constant_dynamic-slice_fusion.3 = bf16[1,144,128]{2,1,0:T(8,128)(2,1)S(1)} fusion(bf16[1,288,128]{2,1,0:T(8,128)(2,1)} %param.10, s32[]{:T(128)S(6)} %select_n.5), kind=kLoop, calls=%fused_computation.6 | loop fusion | bytes 73732 | tf_op jit(solution)/shard_map/dynamic_slice | solution.py:332
  9.4 0.0 copy-start.4
  9.4 0.8 %copy-done.4 = bf16[128,128]{1,0:T(8,128)(2,1)S(1)} copy-done((bf16[128,128]{1,0:T(8,128)(2,1)S(1)}, bf16[128,128]{1,0:T(8,128)(2,1)}, u32[]{:S(2)}) %copy-start.4) | copy-done | bytes 32792
  10.2 0.0 copy-start.5
  10.2 0.8 %copy-done.5 = bf16[128,128]{1,0:T(8,128)(2,1)S(1)} copy-done((bf16[128,128]{1,0:T(8,128)(2,1)S(1)}, bf16[128,128]{1,0:T(8,128)(2,1)}, u32[]{:S(2)}) %copy-start.5) | copy-done | bytes 32792
  11.0 0.0 copy-start
  11.0 0.0 copy-start.1
  11.0 0.0 copy-start.2
  11.0 3.3 %right.1.right_ref = bf16[36,144,128]{2,1,0:T(8,128)(2,1)S(1)} custom-call(s32[1]{0:T(128)S(6)} %copy.10.length_ref, bf16[128,128]{1,0:T(8,128)(2,1)S(1)} %copy-done.4, bf16[128,128]{1,0:T(8,128)(2,1)S(1)} %copy-done.5, bf16[36,144,128]{2,1,0:T(8,128)(2,1)} %pair_ref.1), custom_call_target="tpu_custom_call" | custom-call | flops 1019215872 | bytes 2654208 | tf_op jit(solution)/shard_map/right/pallas_call | solution.py:329
  14.2 0.0 collective-permute-done.2
  14.3 0.0 collective-permute-done.1
  14.3 0.0 collective-permute-done
  14.4 0.1 collective-permute-start.3
  14.4 0.0 collective-permute-done.4
  14.5 0.0 copy-done
  14.5 0.0 copy-done.1
  14.5 0.0 copy-done.2
  14.5 1.4 %near.1 = (f32[1,72,128]{2,1,0:T(8,128)S(1)}, f32[1,72,128]{2,1,0:T(8,128)S(1)}, f32[160,128]{1,0:T(8,128)S(1)}) custom-call(s32[1]{0:T(128)S(6)} %copy.10.length_ref, bf16[36,144,128]{2,1,0:T(8,128)(2,1)S(1)} %right.1.right_ref, bf16[4,144,128]{2,1,0:T(8,128)(2,1)S(1)} %pad_maximum_fusion.1.slab_ref, bf16[128,128]{1,0:T(8,128)(2,1)S(1)} %copy-done, ...), custom_call_target="tpu_custom_call" | custom-call | flops 5308416 | bytes 1327104 | tf_op jit(solution)/shard_map/near/pallas_call | solution.py:348
  16.0 0.0 collective-permute-done.3
  16.0 1.0 %send.1 = (f32[2,144,128]{2,1,0:T(8,128)S(1)}, bf16[4,144,128]{2,1,0:T(8,128)(2,1)S(1)}, f32[160,128]{1,0:T(8,128)S(1)}) custom-call(s32[1]{0:T(128)S(6)} %copy.10.length_ref, bf16[36,144,128]{2,1,0:T(8,128)(2,1)S(1)} %right.1.right_ref, bf16[4,144,128]{2,1,0:T(8,128)(2,1)S(1)} %pad_maximum_fusion.slab_ref, bf16[128,128]{1,0:T(8,128)(2,1)S(1)} %copy-done, ...), custom_call_target="tpu_custom_call" | custom-call | tf_op jit(solution)/shard_map/send/pallas_call | solution.py:360
  17.0 0.0 copy-start.3
  17.1 0.5 %collective-permute-start.5 = (f32[2,144,128]{2,1,0:T(8,128)S(1)}, f32[2,144,128]{2,1,0:T(8,128)S(1)}, u32[]{:S(2)}, u32[]{:S(2)}) collective-permute-start(f32[2,144,128]{2,1,0:T(8,128)S(1)} %get-tuple-element.20), channel_id=1, source_target_pairs={{0,1},{1,0},{2,3},{3,2},{4,5},{5,4},{6,7},{7,6},{8,9},{9,8},{10,11... | collective-permute-start | bytes 442376 | tf_op jit(solution)/shard_map/ppermute | solution.py:253
  17.6 0.5 %keep.1.keep_ref = f32[2,144,128]{2,1,0:T(8,128)S(1)} custom-call(bf16[36,144,128]{2,1,0:T(8,128)(2,1)S(1)} %right.1.right_ref, bf16[4,144,128]{2,1,0:T(8,128)(2,1)S(1)} %get-tuple-element.17.left_ref, f32[160,128]{1,0:T(8,128)S(1)} %get-tuple-element.18.gates_ref, f32[1,72,128]{2,1,0:T(8,128)S(1)} %get-tuple-element.19.near_sums_ref, ...), custom_call_target="tpu_custom_call" | custom-call | flops 5308416 | bytes 1327104 | tf_op jit(solution)/shard_map/keep/pallas_call | solution.py:373
  18.1 0.5 %collective-permute-done.5.got_ref = f32[2,144,128]{2,1,0:T(8,128)S(1)} collective-permute-done((f32[2,144,128]{2,1,0:T(8,128)S(1)}, f32[2,144,128]{2,1,0:T(8,128)S(1)}, u32[]{:S(2)}, u32[]{:S(2)}) %collective-permute-start.5) | collective-permute-done | bytes 147488 | tf_op jit(solution)/shard_map/ppermute | solution.py:253
  18.6 0.0 copy-done.3
  18.6 0.9 %last.1 = bf16[18,8,128]{2,1,0:T(8,128)(2,1)} custom-call(f32[2,144,128]{2,1,0:T(8,128)S(1)} %keep.1.keep_ref, f32[2,144,128]{2,1,0:T(8,128)S(1)} %collective-permute-done.5.got_ref, bf16[128,128]{1,0:T(8,128)(2,1)S(1)} %copy-done.3), custom_call_target="tpu_custom_call" | custom-call | tf_op jit(solution)/shard_map/last/pallas_call | solution.py:385
  (7 shorter events, 0.1 us)
Async XLA Ops:
  0.0 14.2 %collective-permute-start.2 = (bf16[1,288,128]{2,1,0:T(8,128)(2,1)}, bf16[1,288,128]{2,1,0:T(8,128)(2,1)S(1)}, u32[]{:S(2)}, u32[]{:S(2)}) collective-permute-start(bf16[1,288,128]{2,1,0:T(8,128)(2,1)} %param.10), channel_id=1, source_target_pairs={{0,14},{1,13},{2,12},{3,15},{4,10},{5,9},{6,8},{7,11},{8,6},{9,5},... | collective-permute-start | bytes 221192 | tf_op jit(solution)/shard_map/ppermute | solution.py:253
  6.0 8.3 %collective-permute-start.1 = (bf16[1,288,128]{2,1,0:T(8,128)(2,1)}, bf16[1,288,128]{2,1,0:T(8,128)(2,1)S(1)}, u32[]{:S(2)}, u32[]{:S(2)}) collective-permute-start(bf16[1,288,128]{2,1,0:T(8,128)(2,1)} %param.10), channel_id=1, source_target_pairs={{0,10},{1,9},{2,8},{3,11},{4,14},{5,13},{6,12},{7,15},{8,2},{9,1},... | collective-permute-start | bytes 221192 | tf_op jit(solution)/shard_map/ppermute | solution.py:253
  6.0 8.3 %collective-permute-start = (bf16[1,288,128]{2,1,0:T(8,128)(2,1)}, bf16[1,288,128]{2,1,0:T(8,128)(2,1)S(1)}, u32[]{:S(2)}, u32[]{:S(2)}) collective-permute-start(bf16[1,288,128]{2,1,0:T(8,128)(2,1)} %param.10), channel_id=1, source_target_pairs={{0,6},{1,5},{2,4},{3,7},{4,2},{5,1},{6,0},{7,3},{8,14},{9,13},{10,... | collective-permute-start | bytes 221192 | tf_op jit(solution)/shard_map/ppermute | solution.py:253
  7.7 6.8 %collective-permute-start.4 = (bf16[1,288,128]{2,1,0:T(8,128)(2,1)}, bf16[1,288,128]{2,1,0:T(8,128)(2,1)S(1)}, u32[]{:S(2)}, u32[]{:S(2)}) collective-permute-start(bf16[1,288,128]{2,1,0:T(8,128)(2,1)} %param.10), channel_id=1, source_target_pairs={{0,2},{1,3},{2,0},{3,1},{4,6},{5,7},{6,4},{7,5},{8,10},{9,11},{10,... | collective-permute-start | bytes 221192 | tf_op jit(solution)/shard_map/ppermute | solution.py:253
  9.4 0.8 %copy-start.4 = (bf16[128,128]{1,0:T(8,128)(2,1)S(1)}, bf16[128,128]{1,0:T(8,128)(2,1)}, u32[]{:S(2)}) copy-start(bf16[128,128]{1,0:T(8,128)(2,1)} %weight_ref.4) | copy-start | bytes 98308
  10.2 0.8 %copy-start.5 = (bf16[128,128]{1,0:T(8,128)(2,1)S(1)}, bf16[128,128]{1,0:T(8,128)(2,1)}, u32[]{:S(2)}) copy-start(bf16[128,128]{1,0:T(8,128)(2,1)} %gate_ref.3) | copy-start | bytes 98308
  11.0 3.6 %copy-start = (bf16[128,128]{1,0:T(8,128)(2,1)S(1)}, bf16[128,128]{1,0:T(8,128)(2,1)}, u32[]{:S(2)}) copy-start(bf16[128,128]{1,0:T(8,128)(2,1)} %gate_ref.5) | copy-start | bytes 98308
  11.0 3.6 %copy-start.1 = (bf16[128,128]{1,0:T(8,128)(2,1)S(1)}, bf16[128,128]{1,0:T(8,128)(2,1)}, u32[]{:S(2)}) copy-start(bf16[128,128]{1,0:T(8,128)(2,1)} %weight_ref.6) | copy-start | bytes 98308
  11.0 3.6 %copy-start.2 = (bf16[128,128]{1,0:T(8,128)(2,1)S(1)}, bf16[128,128]{1,0:T(8,128)(2,1)}, u32[]{:S(2)}) copy-start(bf16[128,128]{1,0:T(8,128)(2,1)} %out_gate_ref.3) | copy-start | bytes 98308
  14.4 1.6 %collective-permute-start.3 = (bf16[3,144,128]{2,1,0:T(8,128)(2,1)S(1)}, bf16[3,144,128]{2,1,0:T(8,128)(2,1)S(1)}, u32[]{:S(2)}, u32[]{:S(2)}) collective-permute-start(bf16[3,144,128]{2,1,0:T(8,128)(2,1)S(1)} %pad_maximum_fusion.2), channel_id=1, source_target_pairs={{0,1},{1,0},{2,3},{3,2},{4,5},{5,4},{6,7},{7,6},{8,9},{9,8},{10,11... | collective-permute-start | bytes 331784 | tf_op jit(solution)/shard_map/ppermute | solution.py:253
  17.0 1.6 %copy-start.3 = (bf16[128,128]{1,0:T(8,128)(2,1)S(1)}, bf16[128,128]{1,0:T(8,128)(2,1)}, u32[]{:S(2)}) copy-start(bf16[128,128]{1,0:T(8,128)(2,1)} %weight_ref.7) | copy-start | bytes 98308
  17.1 1.5 %collective-permute-start.5 = (f32[2,144,128]{2,1,0:T(8,128)S(1)}, f32[2,144,128]{2,1,0:T(8,128)S(1)}, u32[]{:S(2)}, u32[]{:S(2)}) collective-permute-start(f32[2,144,128]{2,1,0:T(8,128)S(1)} %get-tuple-element.20), channel_id=1, source_target_pairs={{0,1},{1,0},{2,3},{3,2},{4,5},{5,4},{6,7},{7,6},{8,9},{9,8},{10,11... | collective-permute-start | bytes 442376 | tf_op jit(solution)/shard_map/ppermute | solution.py:253

commit v8 on v7

--- a/solution.py
+++ b/solution.py
@@ -30,12 +30,13 @@
     return held
 
 
-def centering(width):
+def centering_kernel(center_ref, share_ref):
+    width = center_ref.shape[0] // 2
     row = lax.broadcasted_iota(jnp.int32, (2 * width, 2 * width), 0)
     col = lax.broadcasted_iota(jnp.int32, (2 * width, 2 * width), 1)
     share = jnp.where((row < width) == (col < width), 1.0 / width, 0.0)
-    center = jnp.where(row == col, 1.0, 0.0) - share
-    return center.astype(BF16), share.astype(BF16)
+    center_ref[...] = (jnp.where(row == col, 1.0, 0.0) - share).astype(BF16)
+    share_ref[...] = share.astype(BF16)
 
 
 def normed(first, second, center, share):
@@ -52,37 +53,21 @@
     return value + value * jnp.tanh(y[:, :width])
 
 
-def right_kernel(length_ref, weight_ref, gate_ref, pair_ref, out_ref, x_ref, sems, *, chunk):
+def right_kernel(center_ref, share_ref, weight_ref, gate_ref, pair_ref, out_ref, *, chunk):
     rows, cols, width = pair_ref.shape
-    turns = rows // chunk
-
-    def piece(turn):
-        here = pl.ds(turn * chunk, chunk)
-        return pltpu.make_async_copy(pair_ref.at[here], x_ref.at[here], sems.at[turn])
-
-    for turn in range(turns):
-        piece(turn).start()
     half = jnp.asarray(0.5, BF16)
     both = jnp.concatenate([gate_ref[...] * half, weight_ref[...] * half], axis=1)
-    live = length_ref[0]
-    first_j = lax.axis_index("row") * rows
-    center, share = centering(width)
-    k = lax.axis_index("col") * cols + lax.broadcasted_iota(jnp.int32, (cols, width), 0)
 
     def some(turn, _):
-        piece(turn).wait()
         j0 = turn * chunk
-        x = x_ref[pl.ds(j0, chunk)].reshape(2, chunk * cols // 2, width)
-        n = normed(x[0], x[1], center, share)
+        x = pair_ref[pl.ds(j0, chunk)].reshape(2, chunk * cols // 2, width)
+        n = normed(x[0], x[1], center_ref[...], share_ref[...])
         for part in range(2):
-            edge = gated(n[:, part * width : (part + 1) * width], both).reshape(chunk // 2, cols, width)
-            for r in range(chunk // 2):
-                j = j0 + part * (chunk // 2) + r
-                reach = jnp.where(first_j + j < live, live, 0)
-                out_ref[j] = jnp.where(k < reach, edge[r], 0.0).astype(BF16)
+            edge = gated(n[:, part * width : (part + 1) * width], both).astype(BF16)
+            out_ref[pl.ds(j0 + part * (chunk // 2), chunk // 2)] = edge.reshape(chunk // 2, cols, width)
         return 0
 
-    lax.fori_loop(0, turns, some, 0)
+    lax.fori_loop(0, rows // chunk, some, 0)
 
 
 def fold(parts):
@@ -100,12 +85,14 @@
     return 0 if blocks == 1 else pl.program_id(0)
 
 
-def project(length_ref, slab_ref, gate_ref, weight_ref, out_gate_ref, left_ref, gates_ref, norm_ref, half_rows, blocks):
+def project(
+    length_ref, center_ref, share_ref, slab_ref, gate_ref, weight_ref, out_gate_ref, left_ref, gates_ref, norm_ref,
+    half_rows, blocks,
+):
     slabs, depth, width = slab_ref.shape
     k_step = block_of(blocks)
     half_cols = depth * blocks
     half = jnp.asarray(0.5, BF16)
-    center, share = centering(width)
     both = jnp.concatenate([gate_ref[...] * half, weight_ref[...] * half], axis=1)
     first_k = lax.axis_index("col") * half_cols + k_step * depth
     live = first_k + lax.broadcasted_iota(jnp.int32, (depth, width), 0) < length_ref[0]
@@ -115,7 +102,7 @@
     def quad(q):
         s = q * QUAD
         x = slab_ref[pl.ds(s, QUAD)].reshape(2, 2 * depth, width)
-        n = normed(x[0], x[1], center, share)
+        n = normed(x[0], x[1], center_ref[...], share_ref[...])
         for part in range(2):
             own = n[:, part * width : (part + 1) * width]
             edge = gated(own, both)
@@ -141,10 +128,12 @@
         pl.loop(0, slabs // QUAD)(quad)
 
 
-def contract(left_ref, right_ref, j_half, sums_ref, blocks):
+def contract(length_ref, left_ref, right_ref, j_half, sums_ref, blocks):
     slabs, depth, _ = left_ref.shape
     rows = right_ref.shape[0] // 2
     group = divisor(rows, 6, 2)
+    live_rows = length_ref[0] - lax.axis_index("row") * (2 * rows)
+    second = lax.broadcasted_iota(jnp.int32, (8, left_ref.shape[2]), 0) // QUAD
 
     def tile(turn, _):
         q = turn // (rows // group)
@@ -161,7 +150,7 @@
                     sums[j][n] = term if k0 == 0 else sums[j][n] + term
         for j in range(0, group, 2):
             dest = sums_ref.at[q, pl.ds(pl.multiple_of((j0 + j) * QUAD, 8), 8), :]
-            total = fold(sums[j] + sums[j + 1])
+            total = jnp.where(first + j + second < live_rows, fold(sums[j] + sums[j + 1]), 0.0)
             dest[...] = total if blocks == 1 else jnp.where(block_of(blocks) == 0, total, total + dest[...])
         return 0
 
@@ -180,29 +169,29 @@
 
 
 def near_kernel(
-    length_ref, right_ref, slab_ref, gate_ref, weight_ref, out_gate_ref,
+    length_ref, center_ref, share_ref, right_ref, slab_ref, gate_ref, weight_ref, out_gate_ref,
     mate_sums_ref, own_sums_ref, gates_ref, left_ref, norm_ref, *, blocks,
 ):
     side = lax.axis_index("col")
     project(
-        length_ref, slab_ref, gate_ref, weight_ref, out_gate_ref, left_ref, gates_ref, norm_ref,
-        right_ref.shape[0] // 2, blocks,
-    )
-    contract(left_ref, right_ref, 1 - side, mate_sums_ref, blocks)
-    contract(left_ref, right_ref, side, own_sums_ref, blocks)
+        length_ref, center_ref, share_ref, slab_ref, gate_ref, weight_ref, out_gate_ref,
+        left_ref, gates_ref, norm_ref, right_ref.shape[0] // 2, blocks,
+    )
+    contract(length_ref, left_ref, right_ref, 1 - side, mate_sums_ref, blocks)
+    contract(length_ref, left_ref, right_ref, side, own_sums_ref, blocks)
 
 
 def send_kernel(
-    length_ref, right_ref, slab_ref, gate_ref, weight_ref, out_gate_ref, near_sums_ref, near_gates_ref,
+    length_ref, center_ref, share_ref, right_ref, slab_ref, gate_ref, weight_ref, out_gate_ref, near_sums_ref, near_gates_ref,
     send_ref, left_out_ref, gates_ref, left_ref, sums_ref, norm_ref, *, blocks, near_places, far_places,
 ):
     flip = 1 - lax.axis_index("col")
     project(
-        length_ref, slab_ref, gate_ref, weight_ref, out_gate_ref, left_ref, gates_ref, norm_ref,
-        right_ref.shape[0] // 2, blocks,
+        length_ref, center_ref, share_ref, slab_ref, gate_ref, weight_ref, out_gate_ref,
+        left_ref, gates_ref, norm_ref, right_ref.shape[0] // 2, blocks,
     )
     left_out_ref[...] = left_ref[...].astype(BF16)
-    contract(left_ref, right_ref, flip, sums_ref, blocks)
+    contract(length_ref, left_ref, right_ref, flip, sums_ref, blocks)
 
     def rest():
         assemble(send_ref, near_sums_ref, near_gates_ref, near_places, flip)
@@ -215,11 +204,11 @@
 
 
 def keep_kernel(
-    right_ref, left_ref, gates_ref, near_sums_ref, near_gates_ref, keep_ref, sums_ref,
+    length_ref, right_ref, left_ref, gates_ref, near_sums_ref, near_gates_ref, keep_ref, sums_ref,
     *, blocks, near_places, far_places,
 ):
     side = lax.axis_index("col")
-    contract(left_ref, right_ref, side, sums_ref, blocks)
+    contract(length_ref, left_ref, right_ref, side, sums_ref, blocks)
 
     def rest():
         assemble(keep_ref, near_sums_ref, near_gates_ref, near_places, side)
@@ -277,14 +266,14 @@
     def part(x, which):
         return lax.dynamic_slice_in_dim(x, which * half_cols, half_cols, 1)
 
-    steps = ((3, 2), (5, 4), (7, 6), (1, 1))
+    steps = ((2, 3), (4, 5), (7, 6), (1, 1))
     first, second, third, beside = [out(*m) for m in steps]
     over = jnp.concatenate([part(x, 1 - side) for x in (first, second, third)], axis=0)
     over, made = between(over)
     over = passed(over, lambda row, core: (row, 1 - core))
     near = jnp.concatenate([half, part(beside, side), part(first, side), part(second, side)], axis=0)
     far = jnp.concatenate([part(third, side), over], axis=0)
-    return near, far, [[0, 1, 3, 5], [0, 1, 2, 4]], [[7, 2, 4, 6], [6, 3, 5, 7]], made
+    return near, far, [[0, 1, 2, 4], [0, 1, 3, 5]], [[7, 3, 5, 6], [6, 2, 4, 7]], made
 
 
 def shards(pair_rep, slab_rep, length, weight_a, gate_a, weight_b, gate_b, weight_gate, weight_out):
@@ -297,7 +286,6 @@
     blocks = half_cols // depth
     grid = () if blocks == 1 else (blocks,)
     near = count // 2
-    hbm = pl.BlockSpec(memory_space=pltpu.HBM)
     smem = pl.BlockSpec(memory_space=pltpu.SMEM)
     vmem = pl.BlockSpec(memory_space=pltpu.VMEM)
     params = pltpu.CompilerParams(vmem_limit_bytes=40 << 20)
@@ -309,14 +297,21 @@
         return vmem if blocks == 1 else pl.BlockSpec((rows, depth, width), lambda k: (0, k, 0))
 
     chunk = divisor(rows_dev, max(2, 1728 // half_cols), 2)
-    turns = rows_dev // chunk
+    square = jax.ShapeDtypeStruct((2 * width, 2 * width), BF16)
+    center, share = pl.pallas_call(
+        centering_kernel,
+        out_shape=(square, square),
+        out_specs=(vmem, vmem),
+        compiler_params=pltpu.CompilerParams(vmem_limit_bytes=8 << 20),
+        cost_estimate=pl.CostEstimate(flops=4 * 10**9, bytes_accessed=8 * 10**6, transcendentals=0),
+        name="centering",
+    )()
     right_call = pl.pallas_call(
         functools.partial(right_kernel, chunk=chunk),
         out_shape=jax.ShapeDtypeStruct((rows_dev, half_cols, hidden), BF16),
-        in_specs=[smem, vmem, vmem, hbm],
+        in_specs=[vmem] * 5,
         out_specs=vmem,
-        scratch_shapes=[pltpu.VMEM((rows_dev, half_cols, width), BF16), pltpu.SemaphoreType.DMA((turns,))],
-        compiler_params=pltpu.CompilerParams(vmem_limit_bytes=52 << 20),
+        compiler_params=params,
         cost_estimate=pl.CostEstimate(
             flops=2 * rows_dev * half_cols * width * hidden * 6,
             bytes_accessed=4 * rows_dev * half_cols * width,
@@ -326,7 +321,7 @@
     )
 
     def between(held):
-        made, held = lax.optimization_barrier((right_call(length, weight_b, gate_b, pair_rep), held))
+        made, held = lax.optimization_barrier((right_call(center, share, weight_b, gate_b, pair_rep), held))
         return held, made
 
     half = lax.dynamic_slice_in_dim(slab_rep, side * half_cols, half_cols, 1)
@@ -343,30 +338,31 @@
         bytes_accessed=2 * rows_dev * half_cols * width,
         transcendentals=near * half_cols * width,
     )
+    squares = [whole(*square.shape)] * 2
     weights = [whole(width, hidden), whole(width, hidden), whole(width, width)]
 
     near_mate, near_own, near_gates = pl.pallas_call(
         functools.partial(near_kernel, blocks=blocks),
         out_shape=(sums, sums, gates),
         grid=grid,
-        in_specs=[smem, deep(rows_dev), deep(near)] + weights,
+        in_specs=[smem] + squares + [deep(rows_dev), deep(near)] + weights,
         out_specs=(whole(*sums.shape), whole(*sums.shape), whole(*gates.shape)),
         scratch_shapes=[left_f32, norm],
         compiler_params=params,
         cost_estimate=cost,
         name="near",
-    )(length, right, near_slabs, gate_a, weight_a, weight_gate)
+    )(length, center, share, right, near_slabs, gate_a, weight_a, weight_gate)
 
     send, left, far_gates = pl.pallas_call(
         functools.partial(send_kernel, blocks=blocks, near_places=near_places, far_places=far_places),
         out_shape=(swapped, jax.ShapeDtypeStruct((near, half_cols, hidden), BF16), gates),
         grid=grid,
-        in_specs=[smem, deep(rows_dev), deep(near)] + weights + [whole(*sums.shape), whole(*gates.shape)],
+        in_specs=[smem] + squares + [deep(rows_dev), deep(near)] + weights + [whole(*sums.shape), whole(*gates.shape)],
         out_specs=(whole(*swapped.shape), deep(near), whole(*gates.shape)),
         scratch_shapes=[left_f32, pltpu.VMEM(sums.shape, F32), norm],
         compiler_params=params,
         name="send",
-    )(length, right, far_slabs, gate_a, weight_a, weight_gate, near_mate, near_gates)
+    )(length, center, share, right, far_slabs, gate_a, weight_a, weight_gate, near_mate, near_gates)
 
     swap = passed(send, lambda row, core: (row, 1 - core))
 
@@ -374,13 +370,13 @@
         functools.partial(keep_kernel, blocks=blocks, near_places=near_places, far_places=far_places),
         out_shape=swapped,
         grid=grid,
-        in_specs=[deep(rows_dev), deep(near), whole(*gates.shape), whole(*sums.shape), whole(*gates.shape)],
+        in_specs=[smem, deep(rows_dev), deep(near), whole(*gates.shape), whole(*sums.shape), whole(*gates.shape)],
         out_specs=whole(*swapped.shape),
         scratch_shapes=[pltpu.VMEM(sums.shape, F32)],
         compiler_params=params,
         cost_estimate=cost,
         name="keep",
-    )(right, left, far_gates, near_own, near_gates)
+    )(length, right, left, far_gates, near_own, near_gates)
 
     update = pl.pallas_call(
         functools.partial(last_kernel, half_cols=half_cols),

time: 19.9 us -> 17.4 us (0.87)
  local copies, waits for them, and re-layouts: 2.38 us -> 0.66 us
  waiting for transfers between devices: 0.5 us -> 1.7 us
  Pallas kernels: 7.17 us -> 6.19 us
  starting transfers between devices: 8.61 us -> 7.71 us
    ppermute x6, waiting for transfers between devices: 0.5 us -> 1.7 us  [passed(): return lax.ppermute(x, ('row', 'col'), pairs)]
    pallas_call x1 -> x2, Pallas kernels: 3.27 us -> 2.27 us  [the longest x1 2.24 us: between(): right_call(center, share, weight_b, gate_b, pair_rep)]
    unnamed x12 -> x16, local copies, waits for them, and re-layouts: 1.53 us -> 0.61 us
    ppermute x6, starting transfers between devices: 8.61 us -> 7.71 us  [passed(): return lax.ppermute(x, ('row', 'col'), pairs)]
    dynamic_slice x1, local copies, waits for them, and re-layouts: 0.78 us -> 0.01 us  [shards(): half = lax.dynamic_slice_in_dim(slab_rep, side * half_cols, half_cols, 1)]
  transfers between devices with their start and end apart: 6 -> 6, of which waited for: 1 -> 2; matrix products, arithmetic and copies ran while one was open for 5% -> 1% of each run, Pallas kernels for 27% -> 25%
where the time goes in v8:
time: 17.4 us; the launch traced here: 17.2 us
  starting transfers between devices  7.71 us (44%)
  Pallas kernels  6.19 us (36%)
  waiting for transfers between devices  1.7 us (10%)
  between operations  0.9 us (5%)
  local copies, waits for them, and re-layouts  0.66 us (4%)
    ppermute x6, starting transfers between devices, passed(): return lax.ppermute(x, ('row', 'col'), pairs)  7.71 us
    pallas_call x1, Pallas kernels, between(): right_call(center, share, weight_b, gate_b, pair_rep)  2.24 us
    ppermute x6, waiting for transfers between devices, passed(): return lax.ppermute(x, ('row', 'col'), pairs)  1.7 us
    pallas_call x1, Pallas kernels, shards(): pl.pallas_call(functools.partial(near_kernel, blocks=blocks), out_shape=(...  1.46 us
    pallas_call x1, Pallas kernels, shards(): pl.pallas_call(functools.partial(send_kernel, blocks=blocks, near_places=...  1.01 us
    pallas_call x1, Pallas kernels, shards(): pl.pallas_call(functools.partial(last_kernel, half_cols=half_cols), out_s...  0.93 us
    unnamed x16, local copies, waits for them, and re-layouts  0.61 us
    pallas_call x1, Pallas kernels, shards(): pl.pallas_call(functools.partial(keep_kernel, blocks=blocks, near_places=...  0.52 us
  transfers between devices with their start and end apart: 6, of which 2 were waited for; matrix products, arithmetic and copies ran while one was open for 1% of the time, Pallas kernels for 25%

profile of v8, /device:TPU:0, one launch (start us, length us, event | category | flops | bytes accessed | tf_op | source)
XLA Modules:
  0.0 17.2 jit_solution(4632611141637891159)
XLA Ops:
  0.0 6.0 %collective-permute-start.2 = (bf16[1,288,128]{2,1,0:T(8,128)(2,1)}, bf16[1,288,128]{2,1,0:T(8,128)(2,1)S(1)}, u32[]{:S(2)}, u32[]{:S(2)}) collective-permute-start(bf16[1,288,128]{2,1,0:T(8,128)(2,1)} %param.10), channel_id=1, source_target_pairs={{0,14},{1,13},{2,12},{3,15},{4,10},{5,9},{6,8},{7,11},{8,6},{9,5},... | collective-permute-start | bytes 221192 | tf_op jit(solution)/shard_map/ppermute | solution.py:242
  6.0 0.0 collective-permute-start.1
  6.0 0.8 %collective-permute-start = (bf16[1,288,128]{2,1,0:T(8,128)(2,1)}, bf16[1,288,128]{2,1,0:T(8,128)(2,1)S(1)}, u32[]{:S(2)}, u32[]{:S(2)}) collective-permute-start(bf16[1,288,128]{2,1,0:T(8,128)(2,1)} %param.10), channel_id=1, source_target_pairs={{0,4},{1,7},{2,6},{3,5},{4,0},{5,3},{6,2},{7,1},{8,12},{9,15},{10,... | collective-permute-start | bytes 221192 | tf_op jit(solution)/shard_map/ppermute | solution.py:242
  6.8 0.3 %collective-permute-start.4 = (bf16[1,288,128]{2,1,0:T(8,128)(2,1)}, bf16[1,288,128]{2,1,0:T(8,128)(2,1)S(1)}, u32[]{:S(2)}, u32[]{:S(2)}) collective-permute-start(bf16[1,288,128]{2,1,0:T(8,128)(2,1)} %param.10), channel_id=1, source_target_pairs={{0,2},{1,3},{2,0},{3,1},{4,6},{5,7},{6,4},{7,5},{8,10},{9,11},{10,... | collective-permute-start | bytes 221192 | tf_op jit(solution)/shard_map/ppermute | solution.py:242
  7.1 0.0 copy-start.7
  7.1 0.0 copy-start.4
  7.1 0.0 copy-start.5
  7.1 0.0 copy-start.6
  7.9 0.1 copy-done.7
  8.0 0.5 %copy-done.4 = bf16[36,144,128]{2,1,0:T(8,128)(2,1)S(1)} copy-done((bf16[36,144,128]{2,1,0:T(8,128)(2,1)S(1)}, bf16[36,144,128]{2,1,0:T(8,128)(2,1)}, u32[]{:S(2)}) %copy-start.4) | copy-done | bytes 1327128
  8.5 0.0 copy-done.5
  8.5 0.0 copy-done.6
  8.5 0.0 copy-start
  8.5 0.0 copy-start.1
  8.5 0.0 copy-start.2
  8.5 2.2 %right.1.right_ref = bf16[36,144,128]{2,1,0:T(8,128)(2,1)S(1)} custom-call(bf16[256,256]{1,0:T(8,128)(2,1)S(1)} %get-tuple-element.15.center_ref, bf16[256,256]{1,0:T(8,128)(2,1)S(1)} %get-tuple-element.16.share_ref, bf16[128,128]{1,0:T(8,128)(2,1)S(1)} %copy-done.5, bf16[128,128]{1,0:T(8,128)(2,1)S(1)} %copy-done.6, bf16[36,144,128]{2,1,0:T(8,128)(2,1)S(1)} %copy-done.4), custom_call_target="tpu_custom_call" | custom-call | flops 1019215872 | bytes 2654208 | tf_op jit(solution)/shard_map/right/pallas_call | solution.py:324
  10.8 0.0 collective-permute-done.2
  10.8 1.2 %collective-permute-done.1 = bf16[1,288,128]{2,1,0:T(8,128)(2,1)S(1)} collective-permute-done((bf16[1,288,128]{2,1,0:T(8,128)(2,1)}, bf16[1,288,128]{2,1,0:T(8,128)(2,1)S(1)}, u32[]{:S(2)}, u32[]{:S(2)}) %collective-permute-start.1) | collective-permute-done | bytes 73760 | tf_op jit(solution)/shard_map/ppermute | solution.py:242
  12.0 0.0 collective-permute-done
  12.0 0.1 collective-permute-start.3
  12.1 0.0 collective-permute-done.4
  12.2 0.0 copy-done
  12.2 0.0 copy-done.1
  12.2 0.0 copy-done.2
  12.2 1.5 %near.1 = (f32[1,72,128]{2,1,0:T(8,128)S(1)}, f32[1,72,128]{2,1,0:T(8,128)S(1)}, f32[160,128]{1,0:T(8,128)S(1)}) custom-call(s32[1]{0:T(128)S(6)} %copy.10.length_ref, bf16[256,256]{1,0:T(8,128)(2,1)S(1)} %get-tuple-element.15.center_ref, bf16[256,256]{1,0:T(8,128)(2,1)S(1)} %get-tuple-element.16.share_ref, bf16[36,144,128]{2,1,0:T(8,128)(2,1)S(1)} %right.1.right_ref, ...), custom_call_target="tpu_custom_call" | custom-call | flops 5308416 | bytes 1327104 | tf_op jit(solution)/shard_map/near/pallas_call | solution.py:344
  13.7 0.0 collective-permute-done.3
  13.7 1.0 %send.1 = (f32[2,144,128]{2,1,0:T(8,128)S(1)}, bf16[4,144,128]{2,1,0:T(8,128)(2,1)S(1)}, f32[160,128]{1,0:T(8,128)S(1)}) custom-call(s32[1]{0:T(128)S(6)} %copy.10.length_ref, bf16[256,256]{1,0:T(8,128)(2,1)S(1)} %get-tuple-element.15.center_ref, bf16[256,256]{1,0:T(8,128)(2,1)S(1)} %get-tuple-element.16.share_ref, ...), custom_call_target="tpu_custom_call" | custom-call | tf_op jit(solution)/shard_map/send/pallas_call | solution.py:356
  14.7 0.0 copy-start.3
  14.7 0.5 %collective-permute-start.5 = (f32[2,144,128]{2,1,0:T(8,128)S(1)}, f32[2,144,128]{2,1,0:T(8,128)S(1)}, u32[]{:S(2)}, u32[]{:S(2)}) collective-permute-start(f32[2,144,128]{2,1,0:T(8,128)S(1)} %get-tuple-element.24), channel_id=1, source_target_pairs={{0,1},{1,0},{2,3},{3,2},{4,5},{5,4},{6,7},{7,6},{8,9},{9,8},{10,11... | collective-permute-start | bytes 442376 | tf_op jit(solution)/shard_map/ppermute | solution.py:242
  15.3 0.5 %keep.1.keep_ref = f32[2,144,128]{2,1,0:T(8,128)S(1)} custom-call(s32[1]{0:T(128)S(6)} %copy.10.length_ref, bf16[36,144,128]{2,1,0:T(8,128)(2,1)S(1)} %right.1.right_ref, bf16[4,144,128]{2,1,0:T(8,128)(2,1)S(1)} %get-tuple-element.21.left_ref, f32[160,128]{1,0:T(8,128)S(1)} %get-tuple-element.22.gates_ref, ...), custom_call_target="tpu_custom_call" | custom-call | flops 5308416 | bytes 1327104 | tf_op jit(solution)/shard_map/keep/pallas_call | solution.py:369
  15.8 0.5 %collective-permute-done.5.got_ref = f32[2,144,128]{2,1,0:T(8,128)S(1)} collective-permute-done((f32[2,144,128]{2,1,0:T(8,128)S(1)}, f32[2,144,128]{2,1,0:T(8,128)S(1)}, u32[]{:S(2)}, u32[]{:S(2)}) %collective-permute-start.5) | collective-permute-done | bytes 147488 | tf_op jit(solution)/shard_map/ppermute | solution.py:242
  16.3 0.0 copy-done.3
  16.3 0.9 %last.1 = bf16[18,8,128]{2,1,0:T(8,128)(2,1)} custom-call(f32[2,144,128]{2,1,0:T(8,128)S(1)} %keep.1.keep_ref, f32[2,144,128]{2,1,0:T(8,128)S(1)} %collective-permute-done.5.got_ref, bf16[128,128]{1,0:T(8,128)(2,1)S(1)} %copy-done.3), custom_call_target="tpu_custom_call" | custom-call | tf_op jit(solution)/shard_map/last/pallas_call | solution.py:381
  (9 shorter events, 0.1 us)
Async XLA Ops:
  0.0 10.8 %collective-permute-start.2 = (bf16[1,288,128]{2,1,0:T(8,128)(2,1)}, bf16[1,288,128]{2,1,0:T(8,128)(2,1)S(1)}, u32[]{:S(2)}, u32[]{:S(2)}) collective-permute-start(bf16[1,288,128]{2,1,0:T(8,128)(2,1)} %param.10), channel_id=1, source_target_pairs={{0,14},{1,13},{2,12},{3,15},{4,10},{5,9},{6,8},{7,11},{8,6},{9,5},... | collective-permute-start | bytes 221192 | tf_op jit(solution)/shard_map/ppermute | solution.py:242
  6.0 6.0 %collective-permute-start.1 = (bf16[1,288,128]{2,1,0:T(8,128)(2,1)}, bf16[1,288,128]{2,1,0:T(8,128)(2,1)S(1)}, u32[]{:S(2)}, u32[]{:S(2)}) collective-permute-start(bf16[1,288,128]{2,1,0:T(8,128)(2,1)} %param.10), channel_id=1, source_target_pairs={{0,8},{1,11},{2,10},{3,9},{4,12},{5,15},{6,14},{7,13},{8,0},{9,3},... | collective-permute-start | bytes 221192 | tf_op jit(solution)/shard_map/ppermute | solution.py:242
  6.0 6.0 %collective-permute-start = (bf16[1,288,128]{2,1,0:T(8,128)(2,1)}, bf16[1,288,128]{2,1,0:T(8,128)(2,1)S(1)}, u32[]{:S(2)}, u32[]{:S(2)}) collective-permute-start(bf16[1,288,128]{2,1,0:T(8,128)(2,1)} %param.10), channel_id=1, source_target_pairs={{0,4},{1,7},{2,6},{3,5},{4,0},{5,3},{6,2},{7,1},{8,12},{9,15},{10,... | collective-permute-start | bytes 221192 | tf_op jit(solution)/shard_map/ppermute | solution.py:242
  6.8 5.4 %collective-permute-start.4 = (bf16[1,288,128]{2,1,0:T(8,128)(2,1)}, bf16[1,288,128]{2,1,0:T(8,128)(2,1)S(1)}, u32[]{:S(2)}, u32[]{:S(2)}) collective-permute-start(bf16[1,288,128]{2,1,0:T(8,128)(2,1)} %param.10), channel_id=1, source_target_pairs={{0,2},{1,3},{2,0},{3,1},{4,6},{5,7},{6,4},{7,5},{8,10},{9,11},{10,... | collective-permute-start | bytes 221192 | tf_op jit(solution)/shard_map/ppermute | solution.py:242
  7.1 0.9 %copy-start.7 = (bf16[1,288,128]{2,1,0:T(8,128)(2,1)S(1)}, bf16[1,288,128]{2,1,0:T(8,128)(2,1)}, u32[]{:S(2)}) copy-start(bf16[1,288,128]{2,1,0:T(8,128)(2,1)} %param.10) | copy-start | bytes 221188
  7.1 1.4 %copy-start.4 = (bf16[36,144,128]{2,1,0:T(8,128)(2,1)S(1)}, bf16[36,144,128]{2,1,0:T(8,128)(2,1)}, u32[]{:S(2)}) copy-start(bf16[36,144,128]{2,1,0:T(8,128)(2,1)} %pair_ref.1) | copy-start | bytes 3981316
  7.1 1.4 %copy-start.5 = (bf16[128,128]{1,0:T(8,128)(2,1)S(1)}, bf16[128,128]{1,0:T(8,128)(2,1)}, u32[]{:S(2)}) copy-start(bf16[128,128]{1,0:T(8,128)(2,1)} %weight_ref.4) | copy-start | bytes 98308
  7.1 1.4 %copy-start.6 = (bf16[128,128]{1,0:T(8,128)(2,1)S(1)}, bf16[128,128]{1,0:T(8,128)(2,1)}, u32[]{:S(2)}) copy-start(bf16[128,128]{1,0:T(8,128)(2,1)} %gate_ref.3) | copy-start | bytes 98308
  8.5 3.7 %copy-start = (bf16[128,128]{1,0:T(8,128)(2,1)S(1)}, bf16[128,128]{1,0:T(8,128)(2,1)}, u32[]{:S(2)}) copy-start(bf16[128,128]{1,0:T(8,128)(2,1)} %gate_ref.5) | copy-start | bytes 98308
  8.5 3.7 %copy-start.1 = (bf16[128,128]{1,0:T(8,128)(2,1)S(1)}, bf16[128,128]{1,0:T(8,128)(2,1)}, u32[]{:S(2)}) copy-start(bf16[128,128]{1,0:T(8,128)(2,1)} %weight_ref.6) | copy-start | bytes 98308
  8.5 3.7 %copy-start.2 = (bf16[128,128]{1,0:T(8,128)(2,1)S(1)}, bf16[128,128]{1,0:T(8,128)(2,1)}, u32[]{:S(2)}) copy-start(bf16[128,128]{1,0:T(8,128)(2,1)} %out_gate_ref.3) | copy-start | bytes 98308
  12.0 1.6 %collective-permute-start.3 = (bf16[3,144,128]{2,1,0:T(8,128)(2,1)S(1)}, bf16[3,144,128]{2,1,0:T(8,128)(2,1)S(1)}, u32[]{:S(2)}, u32[]{:S(2)}) collective-permute-start(bf16[3,144,128]{2,1,0:T(8,128)(2,1)S(1)} %pad_maximum_fusion.2), channel_id=1, source_target_pairs={{0,1},{1,0},{2,3},{3,2},{4,5},{5,4},{6,7},{7,6},{8,9},{9,8},{10,11... | collective-permute-start | bytes 331784 | tf_op jit(solution)/shard_map/ppermute | solution.py:242
  14.7 1.6 %copy-start.3 = (bf16[128,128]{1,0:T(8,128)(2,1)S(1)}, bf16[128,128]{1,0:T(8,128)(2,1)}, u32[]{:S(2)}) copy-start(bf16[128,128]{1,0:T(8,128)(2,1)} %weight_ref.7) | copy-start | bytes 98308
  14.7 1.5 %collective-permute-start.5 = (f32[2,144,128]{2,1,0:T(8,128)S(1)}, f32[2,144,128]{2,1,0:T(8,128)S(1)}, u32[]{:S(2)}, u32[]{:S(2)}) collective-permute-start(f32[2,144,128]{2,1,0:T(8,128)S(1)} %get-tuple-element.24), channel_id=1, source_target_pairs={{0,1},{1,0},{2,3},{3,2},{4,5},{5,4},{6,7},{7,6},{8,9},{9,8},{10,11... | collective-permute-start | bytes 442376 | tf_op jit(solution)/shard_map/ppermute | solution.py:242

commit v9 on v8

--- a/solution.py
+++ b/solution.py
@@ -170,15 +170,14 @@
 
 def near_kernel(
     length_ref, center_ref, share_ref, right_ref, slab_ref, gate_ref, weight_ref, out_gate_ref,
-    mate_sums_ref, own_sums_ref, gates_ref, left_ref, norm_ref, *, blocks,
+    sums_ref, gates_ref, left_out_ref, left_ref, norm_ref, *, blocks,
 ):
-    side = lax.axis_index("col")
     project(
         length_ref, center_ref, share_ref, slab_ref, gate_ref, weight_ref, out_gate_ref,
         left_ref, gates_ref, norm_ref, right_ref.shape[0] // 2, blocks,
     )
-    contract(length_ref, left_ref, right_ref, 1 - side, mate_sums_ref, blocks)
-    contract(length_ref, left_ref, right_ref, side, own_sums_ref, blocks)
+    left_out_ref[...] = left_ref[...].astype(BF16)
+    contract(length_ref, left_ref, right_ref, 1 - lax.axis_index("col"), sums_ref, blocks)
 
 
 def send_kernel(
@@ -204,15 +203,16 @@
 
 
 def keep_kernel(
-    length_ref, right_ref, left_ref, gates_ref, near_sums_ref, near_gates_ref, keep_ref, sums_ref,
-    *, blocks, near_places, far_places,
+    length_ref, right_ref, near_left_ref, far_left_ref, near_gates_ref, far_gates_ref,
+    keep_ref, near_sums_ref, far_sums_ref, *, blocks, near_places, far_places,
 ):
     side = lax.axis_index("col")
-    contract(length_ref, left_ref, right_ref, side, sums_ref, blocks)
+    contract(length_ref, near_left_ref, right_ref, side, near_sums_ref, blocks)
+    contract(length_ref, far_left_ref, right_ref, side, far_sums_ref, blocks)
 
     def rest():
         assemble(keep_ref, near_sums_ref, near_gates_ref, near_places, side)
-        assemble(keep_ref, sums_ref, gates_ref, far_places, side)
+        assemble(keep_ref, far_sums_ref, far_gates_ref, far_places, side)
 
     if blocks == 1:
         rest()
@@ -256,24 +256,24 @@
     return held, got, near, far, made
 
 
-def direct(slab, half, between):
+def direct(slab, slab_late, half, between):
     half_cols = half.shape[1]
     side = lax.axis_index("col")
 
-    def out(*m):
-        return passed(slab, lambda row, core: (row ^ m[core], core))
+    def out(x, *m):
+        return passed(x, lambda row, core: (row ^ m[core], core))
 
     def part(x, which):
         return lax.dynamic_slice_in_dim(x, which * half_cols, half_cols, 1)
 
-    steps = ((2, 3), (4, 5), (7, 6), (1, 1))
-    first, second, third, beside = [out(*m) for m in steps]
+    first, second, third = [out(slab, *m) for m in ((7, 6), (2, 3), (4, 5))]
+    beside = out(slab_late, 1, 1)
     over = jnp.concatenate([part(x, 1 - side) for x in (first, second, third)], axis=0)
     over, made = between(over)
     over = passed(over, lambda row, core: (row, 1 - core))
     near = jnp.concatenate([half, part(beside, side), part(first, side), part(second, side)], axis=0)
     far = jnp.concatenate([part(third, side), over], axis=0)
-    return near, far, [[0, 1, 2, 4], [0, 1, 3, 5]], [[7, 3, 5, 6], [6, 2, 4, 7]], made
+    return near, far, [[0, 1, 7, 2], [0, 1, 6, 3]], [[4, 6, 3, 5], [5, 7, 2, 4]], made
 
 
 def shards(pair_rep, slab_rep, length, weight_a, gate_a, weight_b, gate_b, weight_gate, weight_out):
@@ -296,7 +296,6 @@
     def deep(rows):
         return vmem if blocks == 1 else pl.BlockSpec((rows, depth, width), lambda k: (0, k, 0))
 
-    chunk = divisor(rows_dev, max(2, 1728 // half_cols), 2)
     square = jax.ShapeDtypeStruct((2 * width, 2 * width), BF16)
     center, share = pl.pallas_call(
         centering_kernel,
@@ -306,6 +305,9 @@
         cost_estimate=pl.CostEstimate(flops=4 * 10**9, bytes_accessed=8 * 10**6, transcendentals=0),
         name="centering",
     )()
+    slab_late, center, share = lax.optimization_barrier((slab_rep, center, share))
+
+    chunk = divisor(rows_dev, max(2, 2592 // half_cols), 2)
     right_call = pl.pallas_call(
         functools.partial(right_kernel, chunk=chunk),
         out_shape=jax.ShapeDtypeStruct((rows_dev, half_cols, hidden), BF16),
@@ -324,8 +326,8 @@
         made, held = lax.optimization_barrier((right_call(center, share, weight_b, gate_b, pair_rep), held))
         return held, made
 
-    half = lax.dynamic_slice_in_dim(slab_rep, side * half_cols, half_cols, 1)
-    gather = functools.partial(direct, slab_rep) if count == 8 else functools.partial(doubled, count=count)
+    half = lax.dynamic_slice_in_dim(slab_late, side * half_cols, half_cols, 1)
+    gather = functools.partial(direct, slab_rep, slab_late) if count == 8 else functools.partial(doubled, count=count)
     near_slabs, far_slabs, near_places, far_places, right = gather(half, between=between)
 
     sums = jax.ShapeDtypeStruct((near // QUAD, half_rows * QUAD, hidden), F32)
@@ -341,28 +343,29 @@
     squares = [whole(*square.shape)] * 2
     weights = [whole(width, hidden), whole(width, hidden), whole(width, width)]
 
-    near_mate, near_own, near_gates = pl.pallas_call(
+    left_shape = jax.ShapeDtypeStruct((near, half_cols, hidden), BF16)
+    near_sums, near_gates, near_left = pl.pallas_call(
         functools.partial(near_kernel, blocks=blocks),
-        out_shape=(sums, sums, gates),
+        out_shape=(sums, gates, left_shape),
         grid=grid,
         in_specs=[smem] + squares + [deep(rows_dev), deep(near)] + weights,
-        out_specs=(whole(*sums.shape), whole(*sums.shape), whole(*gates.shape)),
+        out_specs=(whole(*sums.shape), whole(*gates.shape), deep(near)),
         scratch_shapes=[left_f32, norm],
         compiler_params=params,
         cost_estimate=cost,
         name="near",
     )(length, center, share, right, near_slabs, gate_a, weight_a, weight_gate)
 
-    send, left, far_gates = pl.pallas_call(
+    send, far_left, far_gates = pl.pallas_call(
         functools.partial(send_kernel, blocks=blocks, near_places=near_places, far_places=far_places),
-        out_shape=(swapped, jax.ShapeDtypeStruct((near, half_cols, hidden), BF16), gates),
+        out_shape=(swapped, left_shape, gates),
         grid=grid,
         in_specs=[smem] + squares + [deep(rows_dev), deep(near)] + weights + [whole(*sums.shape), whole(*gates.shape)],
         out_specs=(whole(*swapped.shape), deep(near), whole(*gates.shape)),
         scratch_shapes=[left_f32, pltpu.VMEM(sums.shape, F32), norm],
         compiler_params=params,
         name="send",
-    )(length, center, share, right, far_slabs, gate_a, weight_a, weight_gate, near_mate, near_gates)
+    )(length, center, share, right, far_slabs, gate_a, weight_a, weight_gate, near_sums, near_gates)
 
     swap = passed(send, lambda row, core: (row, 1 - core))
 
@@ -370,13 +373,13 @@
         functools.partial(keep_kernel, blocks=blocks, near_places=near_places, far_places=far_places),
         out_shape=swapped,
         grid=grid,
-        in_specs=[smem, deep(rows_dev), deep(near), whole(*gates.shape), whole(*sums.shape), whole(*gates.shape)],
+        in_specs=[smem, deep(rows_dev), deep(near), deep(near), whole(*gates.shape), whole(*gates.shape)],
         out_specs=whole(*swapped.shape),
-        scratch_shapes=[pltpu.VMEM(sums.shape, F32)],
+        scratch_shapes=[pltpu.VMEM(sums.shape, F32), pltpu.VMEM(sums.shape, F32)],
         compiler_params=params,
         cost_estimate=cost,
         name="keep",
-    )(length, right, left, far_gates, near_own, near_gates)
+    )(length, right, near_left, far_left, near_gates, far_gates)
 
     update = pl.pallas_call(
         functools.partial(last_kernel, half_cols=half_cols),

time: 17.4 us -> 17.1 us (0.983)
  waiting for transfers between devices: 1.7 us -> 2.32 us
  local copies, waits for them, and re-layouts: 0.66 us -> 0.1 us
  Pallas kernels: 6.19 us -> 5.93 us
    ppermute x6, waiting for transfers between devices: 1.7 us -> 2.32 us  [passed(): return lax.ppermute(x, ('row', 'col'), pairs)]
    unnamed x16, local copies, waits for them, and re-layouts: 0.61 us -> 0.04 us
    pallas_call x1, Pallas kernels: 0.52 us -> 1.01 us  [shards(): pl.pallas_call(functools.partial(keep_kernel, blocks=blocks, near_places=...]
    pallas_call x1, Pallas kernels: 1.46 us -> 0.99 us  [shards(): pl.pallas_call(functools.partial(near_kernel, blocks=blocks), out_shape=(...]
    pallas_call x1, Pallas kernels: 2.24 us -> 1.96 us  [between(): right_call(center, share, weight_b, gate_b, pair_rep)]
  transfers between devices with their start and end apart: 6 -> 6, of which waited for: 2 -> 3; matrix products, arithmetic and copies ran while one was open for 1% -> 1% of each run, Pallas kernels for 25% -> 23%
where the time goes in v9:
time: 17.1 us; the launch traced here: 17 us
  starting transfers between devices  7.72 us (45%)
  Pallas kernels  5.93 us (35%)
  waiting for transfers between devices  2.32 us (14%)
  between operations  0.83 us (5%)
    ppermute x6, starting transfers between devices, passed(): return lax.ppermute(x, ('row', 'col'), pairs)  7.72 us
    ppermute x6, waiting for transfers between devices, passed(): return lax.ppermute(x, ('row', 'col'), pairs)  2.32 us
    pallas_call x1, Pallas kernels, between(): right_call(center, share, weight_b, gate_b, pair_rep)  1.96 us
    pallas_call x1, Pallas kernels, shards(): pl.pallas_call(functools.partial(keep_kernel, blocks=blocks, near_places=...  1.01 us
    pallas_call x1, Pallas kernels, shards(): pl.pallas_call(functools.partial(send_kernel, blocks=blocks, near_places=...  1.01 us
    pallas_call x1, Pallas kernels, shards(): pl.pallas_call(functools.partial(near_kernel, blocks=blocks), out_shape=(...  0.99 us
    pallas_call x1, Pallas kernels, shards(): pl.pallas_call(functools.partial(last_kernel, half_cols=half_cols), out_s...  0.93 us
  transfers between devices with their start and end apart: 6, of which 3 were waited for; matrix products, arithmetic and copies ran while one was open for 1% of the time, Pallas kernels for 23%

profile of v9, /device:TPU:0, one launch (start us, length us, event | category | flops | bytes accessed | tf_op | source)
XLA Modules:
  0.0 17.0 jit_solution(1438732444508771076)
XLA Ops:
  0.0 0.0 copy-start.7
  0.0 0.0 copy-start.6
  0.0 0.0 copy-start.5
  0.0 0.0 copy-start.4
  0.0 6.1 %collective-permute-start = (bf16[1,288,128]{2,1,0:T(8,128)(2,1)}, bf16[1,288,128]{2,1,0:T(8,128)(2,1)S(1)}, u32[]{:S(2)}, u32[]{:S(2)}) collective-permute-start(bf16[1,288,128]{2,1,0:T(8,128)(2,1)} %param.10), channel_id=1, source_target_pairs={{0,14},{1,13},{2,12},{3,15},{4,10},{5,9},{6,8},{7,11},{8,6},{9,5},... | collective-permute-start | bytes 221192 | tf_op jit(solution)/shard_map/ppermute | solution.py:242
  6.1 0.0 collective-permute-start.2
  6.1 0.8 %collective-permute-start.1 = (bf16[1,288,128]{2,1,0:T(8,128)(2,1)}, bf16[1,288,128]{2,1,0:T(8,128)(2,1)S(1)}, u32[]{:S(2)}, u32[]{:S(2)}) collective-permute-start(bf16[1,288,128]{2,1,0:T(8,128)(2,1)} %param.10), channel_id=1, source_target_pairs={{0,4},{1,7},{2,6},{3,5},{4,0},{5,3},{6,2},{7,1},{8,12},{9,15},{10,... | collective-permute-start | bytes 221192 | tf_op jit(solution)/shard_map/ppermute | solution.py:242
  6.9 0.0 copy-done.7
  6.9 0.5 %collective-permute-start.3 = (bf16[1,288,128]{2,1,0:T(8,128)(2,1)S(1)}, bf16[1,288,128]{2,1,0:T(8,128)(2,1)S(1)}, u32[]{:S(2)}, u32[]{:S(2)}) collective-permute-start(bf16[1,288,128]{2,1,0:T(8,128)(2,1)S(1)} %copy-done.7), channel_id=1, source_target_pairs={{0,2},{1,3},{2,0},{3,1},{4,6},{5,7},{6,4},{7,5},{8,10},{9,11},{10,... | collective-permute-start | bytes 221192 | tf_op jit(solution)/shard_map/ppermute | solution.py:242
  8.0 0.0 copy-done.6
  8.0 0.0 copy-done.5
  8.0 0.0 copy-done.4
  8.1 0.0 copy-start
  8.1 0.0 copy-start.1
  8.1 0.0 copy-start.2
  8.1 2.0 %right.1.right_ref = bf16[36,144,128]{2,1,0:T(8,128)(2,1)S(1)} custom-call(bf16[256,256]{1,0:T(8,128)(2,1)S(1)} %get-tuple-element.20.center_ref, bf16[256,256]{1,0:T(8,128)(2,1)S(1)} %get-tuple-element.21.share_ref, bf16[128,128]{1,0:T(8,128)(2,1)S(1)} %copy-done.5, bf16[128,128]{1,0:T(8,128)(2,1)S(1)} %copy-done.6, bf16[36,144,128]{2,1,0:T(8,128)(2,1)S(1)} %copy-done.4), custom_call_target="tpu_custom_call" | custom-call | flops 1019215872 | bytes 2654208 | tf_op jit(solution)/shard_map/right/pallas_call | solution.py:326
  10.1 0.0 collective-permute-done
  10.1 2.0 %collective-permute-done.1 = bf16[1,288,128]{2,1,0:T(8,128)(2,1)S(1)} collective-permute-done((bf16[1,288,128]{2,1,0:T(8,128)(2,1)}, bf16[1,288,128]{2,1,0:T(8,128)(2,1)S(1)}, u32[]{:S(2)}, u32[]{:S(2)}) %collective-permute-start.1) | collective-permute-done | bytes 73760 | tf_op jit(solution)/shard_map/ppermute | solution.py:242
  12.1 0.0 collective-permute-done.2
  12.2 0.1 collective-permute-start.4
  12.2 0.0 collective-permute-done.3
  12.3 0.0 copy-done
  12.3 0.0 copy-done.1
  12.3 0.0 copy-done.2
  12.3 1.0 %near.1 = (f32[1,72,128]{2,1,0:T(8,128)S(1)}, f32[160,128]{1,0:T(8,128)S(1)}, bf16[4,144,128]{2,1,0:T(8,128)(2,1)S(1)}) custom-call(s32[1]{0:T(128)S(6)} %copy.10.length_ref, bf16[256,256]{1,0:T(8,128)(2,1)S(1)} %get-tuple-element.20.center_ref, bf16[256,256]{1,0:T(8,128)(2,1)S(1)} %get-tuple-element.21.share_ref, bf16[36,144,128]{2,1,0:T(8,128)(2,1)S(1)} %right.1.right_ref, ...), custom_call_target="tpu_custom_call" | custom-call | flops 5308416 | bytes 1327104 | tf_op jit(solution)/shard_map/near/pallas_call | solution.py:347
  13.3 0.2 %collective-permute-done.4 = bf16[3,144,128]{2,1,0:T(8,128)(2,1)S(1)} collective-permute-done((bf16[3,144,128]{2,1,0:T(8,128)(2,1)S(1)}, bf16[3,144,128]{2,1,0:T(8,128)(2,1)S(1)}, u32[]{:S(2)}, u32[]{:S(2)}) %collective-permute-start.4) | collective-permute-done | bytes 110624 | tf_op jit(solution)/shard_map/ppermute | solution.py:242
  13.6 1.0 %send.1 = (f32[2,144,128]{2,1,0:T(8,128)S(1)}, bf16[4,144,128]{2,1,0:T(8,128)(2,1)S(1)}, f32[160,128]{1,0:T(8,128)S(1)}) custom-call(s32[1]{0:T(128)S(6)} %copy.10.length_ref, bf16[256,256]{1,0:T(8,128)(2,1)S(1)} %get-tuple-element.20.center_ref, bf16[256,256]{1,0:T(8,128)(2,1)S(1)} %get-tuple-element.21.share_ref, ...), custom_call_target="tpu_custom_call" | custom-call | tf_op jit(solution)/shard_map/send/pallas_call | solution.py:359
  14.6 0.0 copy-start.3
  14.6 0.3 %collective-permute-start.5 = (f32[2,144,128]{2,1,0:T(8,128)S(1)}, f32[2,144,128]{2,1,0:T(8,128)S(1)}, u32[]{:S(2)}, u32[]{:S(2)}) collective-permute-start(f32[2,144,128]{2,1,0:T(8,128)S(1)} %get-tuple-element.30), channel_id=1, source_target_pairs={{0,1},{1,0},{2,3},{3,2},{4,5},{5,4},{6,7},{7,6},{8,9},{9,8},{10,11... | collective-permute-start | bytes 442376 | tf_op jit(solution)/shard_map/ppermute | solution.py:242
  14.9 1.0 %keep.1.keep_ref = f32[2,144,128]{2,1,0:T(8,128)S(1)} custom-call(s32[1]{0:T(128)S(6)} %copy.10.length_ref, bf16[36,144,128]{2,1,0:T(8,128)(2,1)S(1)} %right.1.right_ref, bf16[4,144,128]{2,1,0:T(8,128)(2,1)S(1)} %get-tuple-element.24.near_left_ref, bf16[4,144,128]{2,1,0:T(8,128)(2,1)S(1)} %get-tuple-element.28.far_left_ref, ...), custom_call_target="tpu_custom_call" | custom-call | flops 5308416 | bytes 1327104 | tf_op jit(solution)/shard_map/keep/pallas_call | solution.py:372
  15.9 0.1 collective-permute-done.5.got_ref
  16.0 0.0 copy-done.3
  16.0 0.9 %last.1 = bf16[18,8,128]{2,1,0:T(8,128)(2,1)} custom-call(f32[2,144,128]{2,1,0:T(8,128)S(1)} %keep.1.keep_ref, f32[2,144,128]{2,1,0:T(8,128)S(1)} %collective-permute-done.5.got_ref, bf16[128,128]{1,0:T(8,128)(2,1)S(1)} %copy-done.3), custom_call_target="tpu_custom_call" | custom-call | tf_op jit(solution)/shard_map/last/pallas_call | solution.py:384
  (8 shorter events, 0.1 us)
Async XLA Ops:
  0.0 6.9 %copy-start.7 = (bf16[1,288,128]{2,1,0:T(8,128)(2,1)S(1)}, bf16[1,288,128]{2,1,0:T(8,128)(2,1)}, u32[]{:S(2)}) copy-start(bf16[1,288,128]{2,1,0:T(8,128)(2,1)} %param.10) | copy-start | bytes 221188
  0.0 8.0 %copy-start.6 = (bf16[128,128]{1,0:T(8,128)(2,1)S(1)}, bf16[128,128]{1,0:T(8,128)(2,1)}, u32[]{:S(2)}) copy-start(bf16[128,128]{1,0:T(8,128)(2,1)} %gate_ref.3) | copy-start | bytes 98308
  0.0 8.0 %copy-start.5 = (bf16[128,128]{1,0:T(8,128)(2,1)S(1)}, bf16[128,128]{1,0:T(8,128)(2,1)}, u32[]{:S(2)}) copy-start(bf16[128,128]{1,0:T(8,128)(2,1)} %weight_ref.4) | copy-start | bytes 98308
  0.0 8.0 %copy-start.4 = (bf16[36,144,128]{2,1,0:T(8,128)(2,1)S(1)}, bf16[36,144,128]{2,1,0:T(8,128)(2,1)}, u32[]{:S(2)}) copy-start(bf16[36,144,128]{2,1,0:T(8,128)(2,1)} %pair_ref.1) | copy-start | bytes 3981316
  0.0 10.1 %collective-permute-start = (bf16[1,288,128]{2,1,0:T(8,128)(2,1)}, bf16[1,288,128]{2,1,0:T(8,128)(2,1)S(1)}, u32[]{:S(2)}, u32[]{:S(2)}) collective-permute-start(bf16[1,288,128]{2,1,0:T(8,128)(2,1)} %param.10), channel_id=1, source_target_pairs={{0,14},{1,13},{2,12},{3,15},{4,10},{5,9},{6,8},{7,11},{8,6},{9,5},... | collective-permute-start | bytes 221192 | tf_op jit(solution)/shard_map/ppermute | solution.py:242
  6.1 6.0 %collective-permute-start.2 = (bf16[1,288,128]{2,1,0:T(8,128)(2,1)}, bf16[1,288,128]{2,1,0:T(8,128)(2,1)S(1)}, u32[]{:S(2)}, u32[]{:S(2)}) collective-permute-start(bf16[1,288,128]{2,1,0:T(8,128)(2,1)} %param.10), channel_id=1, source_target_pairs={{0,8},{1,11},{2,10},{3,9},{4,12},{5,15},{6,14},{7,13},{8,0},{9,3},... | collective-permute-start | bytes 221192 | tf_op jit(solution)/shard_map/ppermute | solution.py:242
  6.1 6.0 %collective-permute-start.1 = (bf16[1,288,128]{2,1,0:T(8,128)(2,1)}, bf16[1,288,128]{2,1,0:T(8,128)(2,1)S(1)}, u32[]{:S(2)}, u32[]{:S(2)}) collective-permute-start(bf16[1,288,128]{2,1,0:T(8,128)(2,1)} %param.10), channel_id=1, source_target_pairs={{0,4},{1,7},{2,6},{3,5},{4,0},{5,3},{6,2},{7,1},{8,12},{9,15},{10,... | collective-permute-start | bytes 221192 | tf_op jit(solution)/shard_map/ppermute | solution.py:242
  6.9 5.4 %collective-permute-start.3 = (bf16[1,288,128]{2,1,0:T(8,128)(2,1)S(1)}, bf16[1,288,128]{2,1,0:T(8,128)(2,1)S(1)}, u32[]{:S(2)}, u32[]{:S(2)}) collective-permute-start(bf16[1,288,128]{2,1,0:T(8,128)(2,1)S(1)} %copy-done.7), channel_id=1, source_target_pairs={{0,2},{1,3},{2,0},{3,1},{4,6},{5,7},{6,4},{7,5},{8,10},{9,11},{10,... | collective-permute-start | bytes 221192 | tf_op jit(solution)/shard_map/ppermute | solution.py:242
  8.1 4.2 %copy-start = (bf16[128,128]{1,0:T(8,128)(2,1)S(1)}, bf16[128,128]{1,0:T(8,128)(2,1)}, u32[]{:S(2)}) copy-start(bf16[128,128]{1,0:T(8,128)(2,1)} %gate_ref.5) | copy-start | bytes 98308
  8.1 4.2 %copy-start.1 = (bf16[128,128]{1,0:T(8,128)(2,1)S(1)}, bf16[128,128]{1,0:T(8,128)(2,1)}, u32[]{:S(2)}) copy-start(bf16[128,128]{1,0:T(8,128)(2,1)} %weight_ref.6) | copy-start | bytes 98308
  8.1 4.2 %copy-start.2 = (bf16[128,128]{1,0:T(8,128)(2,1)S(1)}, bf16[128,128]{1,0:T(8,128)(2,1)}, u32[]{:S(2)}) copy-start(bf16[128,128]{1,0:T(8,128)(2,1)} %out_gate_ref.3) | copy-start | bytes 98308
  12.2 1.4 %collective-permute-start.4 = (bf16[3,144,128]{2,1,0:T(8,128)(2,1)S(1)}, bf16[3,144,128]{2,1,0:T(8,128)(2,1)S(1)}, u32[]{:S(2)}, u32[]{:S(2)}) collective-permute-start(bf16[3,144,128]{2,1,0:T(8,128)(2,1)S(1)} %pad_maximum_fusion.2), channel_id=1, source_target_pairs={{0,1},{1,0},{2,3},{3,2},{4,5},{5,4},{6,7},{7,6},{8,9},{9,8},{10,11... | collective-permute-start | bytes 331784 | tf_op jit(solution)/shard_map/ppermute | solution.py:242
  14.6 1.5 %copy-start.3 = (bf16[128,128]{1,0:T(8,128)(2,1)S(1)}, bf16[128,128]{1,0:T(8,128)(2,1)}, u32[]{:S(2)}) copy-start(bf16[128,128]{1,0:T(8,128)(2,1)} %weight_ref.7) | copy-start | bytes 98308
  14.6 1.4 %collective-permute-start.5 = (f32[2,144,128]{2,1,0:T(8,128)S(1)}, f32[2,144,128]{2,1,0:T(8,128)S(1)}, u32[]{:S(2)}, u32[]{:S(2)}) collective-permute-start(f32[2,144,128]{2,1,0:T(8,128)S(1)} %get-tuple-element.30), channel_id=1, source_target_pairs={{0,1},{1,0},{2,3},{3,2},{4,5},{5,4},{6,7},{7,6},{8,9},{9,8},{10,11... | collective-permute-start | bytes 442376 | tf_op jit(solution)/shard_map/ppermute | solution.py:242

commit v10 on v9

--- a/solution.py
+++ b/solution.py
@@ -266,14 +266,14 @@
     def part(x, which):
         return lax.dynamic_slice_in_dim(x, which * half_cols, half_cols, 1)
 
-    first, second, third = [out(slab, *m) for m in ((7, 6), (2, 3), (4, 5))]
+    first, second, third = [out(slab, *m) for m in ((5, 4), (2, 3), (6, 7))]
     beside = out(slab_late, 1, 1)
     over = jnp.concatenate([part(x, 1 - side) for x in (first, second, third)], axis=0)
     over, made = between(over)
     over = passed(over, lambda row, core: (row, 1 - core))
     near = jnp.concatenate([half, part(beside, side), part(first, side), part(second, side)], axis=0)
     far = jnp.concatenate([part(third, side), over], axis=0)
-    return near, far, [[0, 1, 7, 2], [0, 1, 6, 3]], [[4, 6, 3, 5], [5, 7, 2, 4]], made
+    return near, far, [[0, 1, 5, 2], [0, 1, 4, 3]], [[6, 4, 3, 7], [7, 5, 2, 6]], made
 
 
 def shards(pair_rep, slab_rep, length, weight_a, gate_a, weight_b, gate_b, weight_gate, weight_out):

time: 17.1 us -> 16.9 us (0.988)
  waiting for transfers between devices: 2.32 us -> 1.9 us
  starting transfers between devices: 7.72 us -> 8.01 us
    ppermute x6, waiting for transfers between devices: 2.32 us -> 1.9 us  [passed(): return lax.ppermute(x, ('row', 'col'), pairs)]
    ppermute x6, starting transfers between devices: 7.72 us -> 8.01 us  [passed(): return lax.ppermute(x, ('row', 'col'), pairs)]
  transfers between devices with their start and end apart: 6 -> 6, of which waited for: 3 -> 3; matrix products, arithmetic and copies ran while one was open for 1% -> 0% of each run, Pallas kernels for 23% -> 24%
where the time goes in v10:
time: 16.9 us; the launch traced here: 16.8 us
  starting transfers between devices  8.01 us (47%)
  Pallas kernels  5.93 us (35%)
  waiting for transfers between devices  1.9 us (11%)
  between operations  0.81 us (5%)
    ppermute x6, starting transfers between devices, passed(): return lax.ppermute(x, ('row', 'col'), pairs)  8.01 us
    pallas_call x1, Pallas kernels, between(): right_call(center, share, weight_b, gate_b, pair_rep)  1.96 us
    ppermute x6, waiting for transfers between devices, passed(): return lax.ppermute(x, ('row', 'col'), pairs)  1.9 us
    pallas_call x1, Pallas kernels, shards(): pl.pallas_call(functools.partial(send_kernel, blocks=blocks, near_places=...  1.01 us
    pallas_call x1, Pallas kernels, shards(): pl.pallas_call(functools.partial(keep_kernel, blocks=blocks, near_places=...  1.01 us
    pallas_call x1, Pallas kernels, shards(): pl.pallas_call(functools.partial(near_kernel, blocks=blocks), out_shape=(...  0.99 us
    pallas_call x1, Pallas kernels, shards(): pl.pallas_call(functools.partial(last_kernel, half_cols=half_cols), out_s...  0.93 us
  transfers between devices with their start and end apart: 6, of which 3 were waited for; matrix products, arithmetic and copies ran while one was open for 0% of the time, Pallas kernels for 24%

profile of v10, /device:TPU:0, one launch (start us, length us, event | category | flops | bytes accessed | tf_op | source)
XLA Modules:
  0.0 16.8 jit_solution(11445329364866975848)
XLA Ops:
  0.0 0.0 copy-start.7
  0.0 0.0 copy-start.6
  0.0 0.0 copy-start.5
  0.0 0.0 copy-start.4
  0.0 5.0 %collective-permute-start = (bf16[1,288,128]{2,1,0:T(8,128)(2,1)}, bf16[1,288,128]{2,1,0:T(8,128)(2,1)S(1)}, u32[]{:S(2)}, u32[]{:S(2)}) collective-permute-start(bf16[1,288,128]{2,1,0:T(8,128)(2,1)} %param.10), channel_id=1, source_target_pairs={{0,10},{1,9},{2,8},{3,11},{4,14},{5,13},{6,12},{7,15},{8,2},{9,1},... | collective-permute-start | bytes 221192 | tf_op jit(solution)/shard_map/ppermute | solution.py:242
  5.0 1.3 %collective-permute-start.2 = (bf16[1,288,128]{2,1,0:T(8,128)(2,1)}, bf16[1,288,128]{2,1,0:T(8,128)(2,1)S(1)}, u32[]{:S(2)}, u32[]{:S(2)}) collective-permute-start(bf16[1,288,128]{2,1,0:T(8,128)(2,1)} %param.10), channel_id=1, source_target_pairs={{0,12},{1,15},{2,14},{3,13},{4,8},{5,11},{6,10},{7,9},{8,4},{9,7},... | collective-permute-start | bytes 221192 | tf_op jit(solution)/shard_map/ppermute | solution.py:242
  6.4 0.2 %collective-permute-start.1 = (bf16[1,288,128]{2,1,0:T(8,128)(2,1)}, bf16[1,288,128]{2,1,0:T(8,128)(2,1)S(1)}, u32[]{:S(2)}, u32[]{:S(2)}) collective-permute-start(bf16[1,288,128]{2,1,0:T(8,128)(2,1)} %param.10), channel_id=1, source_target_pairs={{0,4},{1,7},{2,6},{3,5},{4,0},{5,3},{6,2},{7,1},{8,12},{9,15},{10,... | collective-permute-start | bytes 221192 | tf_op jit(solution)/shard_map/ppermute | solution.py:242
  6.7 0.0 copy-done.7
  6.7 0.6 %collective-permute-start.3 = (bf16[1,288,128]{2,1,0:T(8,128)(2,1)S(1)}, bf16[1,288,128]{2,1,0:T(8,128)(2,1)S(1)}, u32[]{:S(2)}, u32[]{:S(2)}) collective-permute-start(bf16[1,288,128]{2,1,0:T(8,128)(2,1)S(1)} %copy-done.7), channel_id=1, source_target_pairs={{0,2},{1,3},{2,0},{3,1},{4,6},{5,7},{6,4},{7,5},{8,10},{9,11},{10,... | collective-permute-start | bytes 221192 | tf_op jit(solution)/shard_map/ppermute | solution.py:242
  7.9 0.0 copy-done.6
  7.9 0.0 copy-done.5
  7.9 0.0 copy-done.4
  8.0 0.0 copy-start
  8.0 0.0 copy-start.1
  8.0 0.0 copy-start.2
  8.0 2.0 %right.1.right_ref = bf16[36,144,128]{2,1,0:T(8,128)(2,1)S(1)} custom-call(bf16[256,256]{1,0:T(8,128)(2,1)S(1)} %get-tuple-element.20.center_ref, bf16[256,256]{1,0:T(8,128)(2,1)S(1)} %get-tuple-element.21.share_ref, bf16[128,128]{1,0:T(8,128)(2,1)S(1)} %copy-done.5, bf16[128,128]{1,0:T(8,128)(2,1)S(1)} %copy-done.6, bf16[36,144,128]{2,1,0:T(8,128)(2,1)S(1)} %copy-done.4), custom_call_target="tpu_custom_call" | custom-call | flops 1019215872 | bytes 2654208 | tf_op jit(solution)/shard_map/right/pallas_call | solution.py:326
  10.0 0.3 %collective-permute-done = bf16[1,288,128]{2,1,0:T(8,128)(2,1)S(1)} collective-permute-done((bf16[1,288,128]{2,1,0:T(8,128)(2,1)}, bf16[1,288,128]{2,1,0:T(8,128)(2,1)S(1)}, u32[]{:S(2)}, u32[]{:S(2)}) %collective-permute-start) | collective-permute-done | bytes 73760 | tf_op jit(solution)/shard_map/ppermute | solution.py:242
  10.2 1.5 %collective-permute-done.1 = bf16[1,288,128]{2,1,0:T(8,128)(2,1)S(1)} collective-permute-done((bf16[1,288,128]{2,1,0:T(8,128)(2,1)}, bf16[1,288,128]{2,1,0:T(8,128)(2,1)S(1)}, u32[]{:S(2)}, u32[]{:S(2)}) %collective-permute-start.1) | collective-permute-done | bytes 73760 | tf_op jit(solution)/shard_map/ppermute | solution.py:242
  11.8 0.0 collective-permute-done.2
  11.8 0.5 %collective-permute-start.4 = (bf16[3,144,128]{2,1,0:T(8,128)(2,1)S(1)}, bf16[3,144,128]{2,1,0:T(8,128)(2,1)S(1)}, u32[]{:S(2)}, u32[]{:S(2)}) collective-permute-start(bf16[3,144,128]{2,1,0:T(8,128)(2,1)S(1)} %pad_maximum_fusion.2), channel_id=1, source_target_pairs={{0,1},{1,0},{2,3},{3,2},{4,5},{5,4},{6,7},{7,6},{8,9},{9,8},{10,11... | collective-permute-start | bytes 331784 | tf_op jit(solution)/shard_map/ppermute | solution.py:242
  12.3 0.0 collective-permute-done.3
  12.3 0.0 copy-done
  12.3 0.0 copy-done.1
  12.3 0.0 copy-done.2
  12.4 1.0 %near.1 = (f32[1,72,128]{2,1,0:T(8,128)S(1)}, f32[160,128]{1,0:T(8,128)S(1)}, bf16[4,144,128]{2,1,0:T(8,128)(2,1)S(1)}) custom-call(s32[1]{0:T(128)S(6)} %copy.10.length_ref, bf16[256,256]{1,0:T(8,128)(2,1)S(1)} %get-tuple-element.20.center_ref, bf16[256,256]{1,0:T(8,128)(2,1)S(1)} %get-tuple-element.21.share_ref, bf16[36,144,128]{2,1,0:T(8,128)(2,1)S(1)} %right.1.right_ref, ...), custom_call_target="tpu_custom_call" | custom-call | flops 5308416 | bytes 1327104 | tf_op jit(solution)/shard_map/near/pallas_call | solution.py:347
  13.4 0.0 collective-permute-done.4
  13.4 1.0 %send.1 = (f32[2,144,128]{2,1,0:T(8,128)S(1)}, bf16[4,144,128]{2,1,0:T(8,128)(2,1)S(1)}, f32[160,128]{1,0:T(8,128)S(1)}) custom-call(s32[1]{0:T(128)S(6)} %copy.10.length_ref, bf16[256,256]{1,0:T(8,128)(2,1)S(1)} %get-tuple-element.20.center_ref, bf16[256,256]{1,0:T(8,128)(2,1)S(1)} %get-tuple-element.21.share_ref, ...), custom_call_target="tpu_custom_call" | custom-call | tf_op jit(solution)/shard_map/send/pallas_call | solution.py:359
  14.4 0.0 copy-start.3
  14.4 0.3 %collective-permute-start.5 = (f32[2,144,128]{2,1,0:T(8,128)S(1)}, f32[2,144,128]{2,1,0:T(8,128)S(1)}, u32[]{:S(2)}, u32[]{:S(2)}) collective-permute-start(f32[2,144,128]{2,1,0:T(8,128)S(1)} %get-tuple-element.30), channel_id=1, source_target_pairs={{0,1},{1,0},{2,3},{3,2},{4,5},{5,4},{6,7},{7,6},{8,9},{9,8},{10,11... | collective-permute-start | bytes 442376 | tf_op jit(solution)/shard_map/ppermute | solution.py:242
  14.7 1.0 %keep.1.keep_ref = f32[2,144,128]{2,1,0:T(8,128)S(1)} custom-call(s32[1]{0:T(128)S(6)} %copy.10.length_ref, bf16[36,144,128]{2,1,0:T(8,128)(2,1)S(1)} %right.1.right_ref, bf16[4,144,128]{2,1,0:T(8,128)(2,1)S(1)} %get-tuple-element.24.near_left_ref, bf16[4,144,128]{2,1,0:T(8,128)(2,1)S(1)} %get-tuple-element.28.far_left_ref, ...), custom_call_target="tpu_custom_call" | custom-call | flops 5308416 | bytes 1327104 | tf_op jit(solution)/shard_map/keep/pallas_call | solution.py:372
  15.7 0.1 collective-permute-done.5.got_ref
  15.9 0.0 copy-done.3
  15.9 0.9 %last.1 = bf16[18,8,128]{2,1,0:T(8,128)(2,1)} custom-call(f32[2,144,128]{2,1,0:T(8,128)S(1)} %keep.1.keep_ref, f32[2,144,128]{2,1,0:T(8,128)S(1)} %collective-permute-done.5.got_ref, bf16[128,128]{1,0:T(8,128)(2,1)S(1)} %copy-done.3), custom_call_target="tpu_custom_call" | custom-call | tf_op jit(solution)/shard_map/last/pallas_call | solution.py:384
  (8 shorter events, 0.1 us)
Async XLA Ops:
  0.0 6.7 %copy-start.7 = (bf16[1,288,128]{2,1,0:T(8,128)(2,1)S(1)}, bf16[1,288,128]{2,1,0:T(8,128)(2,1)}, u32[]{:S(2)}) copy-start(bf16[1,288,128]{2,1,0:T(8,128)(2,1)} %param.10) | copy-start | bytes 221188
  0.0 7.9 %copy-start.6 = (bf16[128,128]{1,0:T(8,128)(2,1)S(1)}, bf16[128,128]{1,0:T(8,128)(2,1)}, u32[]{:S(2)}) copy-start(bf16[128,128]{1,0:T(8,128)(2,1)} %gate_ref.3) | copy-start | bytes 98308
  0.0 7.9 %copy-start.5 = (bf16[128,128]{1,0:T(8,128)(2,1)S(1)}, bf16[128,128]{1,0:T(8,128)(2,1)}, u32[]{:S(2)}) copy-start(bf16[128,128]{1,0:T(8,128)(2,1)} %weight_ref.4) | copy-start | bytes 98308
  0.0 7.9 %copy-start.4 = (bf16[36,144,128]{2,1,0:T(8,128)(2,1)S(1)}, bf16[36,144,128]{2,1,0:T(8,128)(2,1)}, u32[]{:S(2)}) copy-start(bf16[36,144,128]{2,1,0:T(8,128)(2,1)} %pair_ref.1) | copy-start | bytes 3981316
  0.0 10.2 %collective-permute-start = (bf16[1,288,128]{2,1,0:T(8,128)(2,1)}, bf16[1,288,128]{2,1,0:T(8,128)(2,1)S(1)}, u32[]{:S(2)}, u32[]{:S(2)}) collective-permute-start(bf16[1,288,128]{2,1,0:T(8,128)(2,1)} %param.10), channel_id=1, source_target_pairs={{0,10},{1,9},{2,8},{3,11},{4,14},{5,13},{6,12},{7,15},{8,2},{9,1},... | collective-permute-start | bytes 221192 | tf_op jit(solution)/shard_map/ppermute | solution.py:242
  5.0 6.7 %collective-permute-start.2 = (bf16[1,288,128]{2,1,0:T(8,128)(2,1)}, bf16[1,288,128]{2,1,0:T(8,128)(2,1)S(1)}, u32[]{:S(2)}, u32[]{:S(2)}) collective-permute-start(bf16[1,288,128]{2,1,0:T(8,128)(2,1)} %param.10), channel_id=1, source_target_pairs={{0,12},{1,15},{2,14},{3,13},{4,8},{5,11},{6,10},{7,9},{8,4},{9,7},... | collective-permute-start | bytes 221192 | tf_op jit(solution)/shard_map/ppermute | solution.py:242
  6.4 5.4 %collective-permute-start.1 = (bf16[1,288,128]{2,1,0:T(8,128)(2,1)}, bf16[1,288,128]{2,1,0:T(8,128)(2,1)S(1)}, u32[]{:S(2)}, u32[]{:S(2)}) collective-permute-start(bf16[1,288,128]{2,1,0:T(8,128)(2,1)} %param.10), channel_id=1, source_target_pairs={{0,4},{1,7},{2,6},{3,5},{4,0},{5,3},{6,2},{7,1},{8,12},{9,15},{10,... | collective-permute-start | bytes 221192 | tf_op jit(solution)/shard_map/ppermute | solution.py:242
  6.7 5.6 %collective-permute-start.3 = (bf16[1,288,128]{2,1,0:T(8,128)(2,1)S(1)}, bf16[1,288,128]{2,1,0:T(8,128)(2,1)S(1)}, u32[]{:S(2)}, u32[]{:S(2)}) collective-permute-start(bf16[1,288,128]{2,1,0:T(8,128)(2,1)S(1)} %copy-done.7), channel_id=1, source_target_pairs={{0,2},{1,3},{2,0},{3,1},{4,6},{5,7},{6,4},{7,5},{8,10},{9,11},{10,... | collective-permute-start | bytes 221192 | tf_op jit(solution)/shard_map/ppermute | solution.py:242
  8.0 4.4 %copy-start = (bf16[128,128]{1,0:T(8,128)(2,1)S(1)}, bf16[128,128]{1,0:T(8,128)(2,1)}, u32[]{:S(2)}) copy-start(bf16[128,128]{1,0:T(8,128)(2,1)} %gate_ref.5) | copy-start | bytes 98308
  8.0 4.4 %copy-start.1 = (bf16[128,128]{1,0:T(8,128)(2,1)S(1)}, bf16[128,128]{1,0:T(8,128)(2,1)}, u32[]{:S(2)}) copy-start(bf16[128,128]{1,0:T(8,128)(2,1)} %weight_ref.6) | copy-start | bytes 98308
  8.0 4.4 %copy-start.2 = (bf16[128,128]{1,0:T(8,128)(2,1)S(1)}, bf16[128,128]{1,0:T(8,128)(2,1)}, u32[]{:S(2)}) copy-start(bf16[128,128]{1,0:T(8,128)(2,1)} %out_gate_ref.3) | copy-start | bytes 98308
  11.8 1.5 %collective-permute-start.4 = (bf16[3,144,128]{2,1,0:T(8,128)(2,1)S(1)}, bf16[3,144,128]{2,1,0:T(8,128)(2,1)S(1)}, u32[]{:S(2)}, u32[]{:S(2)}) collective-permute-start(bf16[3,144,128]{2,1,0:T(8,128)(2,1)S(1)} %pad_maximum_fusion.2), channel_id=1, source_target_pairs={{0,1},{1,0},{2,3},{3,2},{4,5},{5,4},{6,7},{7,6},{8,9},{9,8},{10,11... | collective-permute-start | bytes 331784 | tf_op jit(solution)/shard_map/ppermute | solution.py:242
  14.4 1.5 %copy-start.3 = (bf16[128,128]{1,0:T(8,128)(2,1)S(1)}, bf16[128,128]{1,0:T(8,128)(2,1)}, u32[]{:S(2)}) copy-start(bf16[128,128]{1,0:T(8,128)(2,1)} %weight_ref.7) | copy-start | bytes 98308
  14.4 1.4 %collective-permute-start.5 = (f32[2,144,128]{2,1,0:T(8,128)S(1)}, f32[2,144,128]{2,1,0:T(8,128)S(1)}, u32[]{:S(2)}, u32[]{:S(2)}) collective-permute-start(f32[2,144,128]{2,1,0:T(8,128)S(1)} %get-tuple-element.30), channel_id=1, source_target_pairs={{0,1},{1,0},{2,3},{3,2},{4,5},{5,4},{6,7},{7,6},{8,9},{9,8},{10,11... | collective-permute-start | bytes 442376 | tf_op jit(solution)/shard_map/ppermute | solution.py:242

commit v11 on v9

--- a/solution.py
+++ b/solution.py
@@ -108,7 +108,7 @@
             edge = gated(own, both)
             for r in range(2):
                 here = slice(r * depth, (r + 1) * depth)
-                left_ref[s + 2 * part + r] = jnp.where(live, edge[here], 0.0).astype(BF16).astype(F32)
+                left_ref[s + 2 * part + r] = jnp.where(live, edge[here], 0.0).astype(BF16).astype(left_ref.dtype)
                 norm_ref[2 * part + r, pl.ds(0, depth), :] = own[here].astype(F32)
 
         def gates():
@@ -170,36 +170,35 @@
 
 def near_kernel(
     length_ref, center_ref, share_ref, right_ref, slab_ref, gate_ref, weight_ref, out_gate_ref,
-    sums_ref, gates_ref, left_out_ref, left_ref, norm_ref, *, blocks,
+    sums_ref, gates_ref, left_ref, norm_ref, *, blocks,
 ):
     project(
         length_ref, center_ref, share_ref, slab_ref, gate_ref, weight_ref, out_gate_ref,
         left_ref, gates_ref, norm_ref, right_ref.shape[0] // 2, blocks,
     )
-    left_out_ref[...] = left_ref[...].astype(BF16)
     contract(length_ref, left_ref, right_ref, 1 - lax.axis_index("col"), sums_ref, blocks)
 
 
 def send_kernel(
     length_ref, center_ref, share_ref, right_ref, slab_ref, gate_ref, weight_ref, out_gate_ref, near_sums_ref, near_gates_ref,
-    send_ref, left_out_ref, gates_ref, left_ref, sums_ref, norm_ref, *, blocks, near_places, far_places,
+    send_ref, left_ref, gates_ref, sums_ref, norm_ref, *, blocks, near_places, far_places,
 ):
     flip = 1 - lax.axis_index("col")
+
+    def at_end(body):
+        if blocks == 1:
+            body()
+        else:
+            pl.when(pl.program_id(0) == blocks - 1)(body)
+
+    at_end(lambda: assemble(send_ref, near_sums_ref, near_gates_ref, near_places, flip))
     project(
         length_ref, center_ref, share_ref, slab_ref, gate_ref, weight_ref, out_gate_ref,
         left_ref, gates_ref, norm_ref, right_ref.shape[0] // 2, blocks,
     )
-    left_out_ref[...] = left_ref[...].astype(BF16)
     contract(length_ref, left_ref, right_ref, flip, sums_ref, blocks)
 
-    def rest():
-        assemble(send_ref, near_sums_ref, near_gates_ref, near_places, flip)
-        assemble(send_ref, sums_ref, gates_ref, far_places, flip)
-
-    if blocks == 1:
-        rest()
-    else:
-        pl.when(pl.program_id(0) == blocks - 1)(rest)
+    at_end(lambda: assemble(send_ref, sums_ref, gates_ref, far_places, flip))
 
 
 def keep_kernel(
@@ -334,7 +333,6 @@
     gates = jax.ShapeDtypeStruct((near * GATE_ROWS, width), F32)
     swapped = jax.ShapeDtypeStruct((2, half_rows * count, hidden), F32)
     norm = pltpu.VMEM((QUAD, depth + GATE_ROWS, width), F32)
-    left_f32 = pltpu.VMEM((near, depth, hidden), F32)
     cost = pl.CostEstimate(
         flops=2 * rows_dev * half_cols * near * hidden,
         bytes_accessed=2 * rows_dev * half_cols * width,
@@ -343,14 +341,14 @@
     squares = [whole(*square.shape)] * 2
     weights = [whole(width, hidden), whole(width, hidden), whole(width, width)]
 
-    left_shape = jax.ShapeDtypeStruct((near, half_cols, hidden), BF16)
+    left_shape = jax.ShapeDtypeStruct((near, half_cols, hidden), F32 if blocks == 1 else BF16)
     near_sums, near_gates, near_left = pl.pallas_call(
         functools.partial(near_kernel, blocks=blocks),
         out_shape=(sums, gates, left_shape),
         grid=grid,
         in_specs=[smem] + squares + [deep(rows_dev), deep(near)] + weights,
         out_specs=(whole(*sums.shape), whole(*gates.shape), deep(near)),
-        scratch_shapes=[left_f32, norm],
+        scratch_shapes=[norm],
         compiler_params=params,
         cost_estimate=cost,
         name="near",
@@ -362,7 +360,7 @@
         grid=grid,
         in_specs=[smem] + squares + [deep(rows_dev), deep(near)] + weights + [whole(*sums.shape), whole(*gates.shape)],
         out_specs=(whole(*swapped.shape), deep(near), whole(*gates.shape)),
-        scratch_shapes=[left_f32, pltpu.VMEM(sums.shape, F32), norm],
+        scratch_shapes=[pltpu.VMEM(sums.shape, F32), norm],
         compiler_params=params,
         name="send",
     )(length, center, share, right, far_slabs, gate_a, weight_a, weight_gate, near_sums, near_gates)

time: 17.1 us -> 17.1 us (level)
  no operation moved by 1% of the time
where the time goes in v11:
time: 17.1 us; the launch traced here: 17 us
  starting transfers between devices  7.72 us (45%)
  Pallas kernels  5.87 us (34%)
  waiting for transfers between devices  2.38 us (14%)
  between operations  0.83 us (5%)
    ppermute x6, starting transfers between devices, passed(): return lax.ppermute(x, ('row', 'col'), pairs)  7.72 us
    ppermute x6, waiting for transfers between devices, passed(): return lax.ppermute(x, ('row', 'col'), pairs)  2.38 us
    pallas_call x1, Pallas kernels, between(): right_call(center, share, weight_b, gate_b, pair_rep)  1.96 us
    pallas_call x1, Pallas kernels, shards(): pl.pallas_call(functools.partial(send_kernel, blocks=blocks, near_places=...  1 us
    pallas_call x1, Pallas kernels, shards(): pl.pallas_call(functools.partial(near_kernel, blocks=blocks), out_shape=(...  0.99 us
    pallas_call x1, Pallas kernels, shards(): pl.pallas_call(functools.partial(keep_kernel, blocks=blocks, near_places=...  0.96 us
    pallas_call x1, Pallas kernels, shards(): pl.pallas_call(functools.partial(last_kernel, half_cols=half_cols), out_s...  0.93 us
  transfers between devices with their start and end apart: 6, of which 3 were waited for; matrix products, arithmetic and copies ran while one was open for 1% of the time, Pallas kernels for 23%

profile of v11, /device:TPU:0, one launch (start us, length us, event | category | flops | bytes accessed | tf_op | source)
XLA Modules:
  0.0 17.0 jit_solution(12155824001487937474)
XLA Ops:
  0.0 0.0 copy-start.7
  0.0 0.0 copy-start.6
  0.0 0.0 copy-start.5
  0.0 0.0 copy-start.4
  0.0 6.1 %collective-permute-start = (bf16[1,288,128]{2,1,0:T(8,128)(2,1)}, bf16[1,288,128]{2,1,0:T(8,128)(2,1)S(1)}, u32[]{:S(2)}, u32[]{:S(2)}) collective-permute-start(bf16[1,288,128]{2,1,0:T(8,128)(2,1)} %param.10), channel_id=1, source_target_pairs={{0,14},{1,13},{2,12},{3,15},{4,10},{5,9},{6,8},{7,11},{8,6},{9,5},... | collective-permute-start | bytes 221192 | tf_op jit(solution)/shard_map/ppermute | solution.py:241
  6.1 0.0 collective-permute-start.2
  6.1 0.8 %collective-permute-start.1 = (bf16[1,288,128]{2,1,0:T(8,128)(2,1)}, bf16[1,288,128]{2,1,0:T(8,128)(2,1)S(1)}, u32[]{:S(2)}, u32[]{:S(2)}) collective-permute-start(bf16[1,288,128]{2,1,0:T(8,128)(2,1)} %param.10), channel_id=1, source_target_pairs={{0,4},{1,7},{2,6},{3,5},{4,0},{5,3},{6,2},{7,1},{8,12},{9,15},{10,... | collective-permute-start | bytes 221192 | tf_op jit(solution)/shard_map/ppermute | solution.py:241
  6.9 0.0 copy-done.7
  6.9 0.5 %collective-permute-start.3 = (bf16[1,288,128]{2,1,0:T(8,128)(2,1)S(1)}, bf16[1,288,128]{2,1,0:T(8,128)(2,1)S(1)}, u32[]{:S(2)}, u32[]{:S(2)}) collective-permute-start(bf16[1,288,128]{2,1,0:T(8,128)(2,1)S(1)} %copy-done.7), channel_id=1, source_target_pairs={{0,2},{1,3},{2,0},{3,1},{4,6},{5,7},{6,4},{7,5},{8,10},{9,11},{10,... | collective-permute-start | bytes 221192 | tf_op jit(solution)/shard_map/ppermute | solution.py:241
  8.0 0.0 copy-done.6
  8.0 0.0 copy-done.5
  8.0 0.0 copy-done.4
  8.1 0.0 copy-start
  8.1 0.0 copy-start.1
  8.1 0.0 copy-start.2
  8.1 2.0 %right.1.right_ref = bf16[36,144,128]{2,1,0:T(8,128)(2,1)S(1)} custom-call(bf16[256,256]{1,0:T(8,128)(2,1)S(1)} %get-tuple-element.20.center_ref, bf16[256,256]{1,0:T(8,128)(2,1)S(1)} %get-tuple-element.21.share_ref, bf16[128,128]{1,0:T(8,128)(2,1)S(1)} %copy-done.5, bf16[128,128]{1,0:T(8,128)(2,1)S(1)} %copy-done.6, bf16[36,144,128]{2,1,0:T(8,128)(2,1)S(1)} %copy-done.4), custom_call_target="tpu_custom_call" | custom-call | flops 1019215872 | bytes 2654208 | tf_op jit(solution)/shard_map/right/pallas_call | solution.py:325
  10.1 0.0 collective-permute-done
  10.1 2.0 %collective-permute-done.1 = bf16[1,288,128]{2,1,0:T(8,128)(2,1)S(1)} collective-permute-done((bf16[1,288,128]{2,1,0:T(8,128)(2,1)}, bf16[1,288,128]{2,1,0:T(8,128)(2,1)S(1)}, u32[]{:S(2)}, u32[]{:S(2)}) %collective-permute-start.1) | collective-permute-done | bytes 73760 | tf_op jit(solution)/shard_map/ppermute | solution.py:241
  12.1 0.0 collective-permute-done.2
  12.2 0.1 collective-permute-start.4
  12.2 0.0 collective-permute-done.3
  12.3 0.0 copy-done
  12.3 0.0 copy-done.1
  12.3 0.0 copy-done.2
  12.3 1.0 %near.1 = (f32[1,72,128]{2,1,0:T(8,128)S(1)}, f32[160,128]{1,0:T(8,128)S(1)}, f32[4,144,128]{2,1,0:T(8,128)S(1)}) custom-call(s32[1]{0:T(128)S(6)} %copy.10.length_ref, bf16[256,256]{1,0:T(8,128)(2,1)S(1)} %get-tuple-element.20.center_ref, bf16[256,256]{1,0:T(8,128)(2,1)S(1)} %get-tuple-element.21.share_ref, bf16[36,144,128]{2,1,0:T(8,128)(2,1)S(1)} %right.1.right_ref, ...), custom_call_target="tpu_custom_call" | custom-call | flops 5308416 | bytes 1327104 | tf_op jit(solution)/shard_map/near/pallas_call | solution.py:345
  13.3 0.2 %collective-permute-done.4 = bf16[3,144,128]{2,1,0:T(8,128)(2,1)S(1)} collective-permute-done((bf16[3,144,128]{2,1,0:T(8,128)(2,1)S(1)}, bf16[3,144,128]{2,1,0:T(8,128)(2,1)S(1)}, u32[]{:S(2)}, u32[]{:S(2)}) %collective-permute-start.4) | collective-permute-done | bytes 110624 | tf_op jit(solution)/shard_map/ppermute | solution.py:241
  13.6 1.0 %send.1 = (f32[2,144,128]{2,1,0:T(8,128)S(1)}, f32[4,144,128]{2,1,0:T(8,128)S(1)}, f32[160,128]{1,0:T(8,128)S(1)}) custom-call(s32[1]{0:T(128)S(6)} %copy.10.length_ref, bf16[256,256]{1,0:T(8,128)(2,1)S(1)} %get-tuple-element.20.center_ref, bf16[256,256]{1,0:T(8,128)(2,1)S(1)} %get-tuple-element.21.share_ref, bf16[36,144,128]{2,1,0:T(8,128)(2,1)S(1)} %right.1.right_ref, ...), custom_call_target="tpu_custom_call" | custom-call | tf_op jit(solution)/shard_map/send/pallas_call | solution.py:357
  14.6 0.0 copy-start.3
  14.6 0.3 %collective-permute-start.5 = (f32[2,144,128]{2,1,0:T(8,128)S(1)}, f32[2,144,128]{2,1,0:T(8,128)S(1)}, u32[]{:S(2)}, u32[]{:S(2)}) collective-permute-start(f32[2,144,128]{2,1,0:T(8,128)S(1)} %get-tuple-element.30), channel_id=1, source_target_pairs={{0,1},{1,0},{2,3},{3,2},{4,5},{5,4},{6,7},{7,6},{8,9},{9,8},{10,11... | collective-permute-start | bytes 442376 | tf_op jit(solution)/shard_map/ppermute | solution.py:241
  14.9 1.0 %keep.1.keep_ref = f32[2,144,128]{2,1,0:T(8,128)S(1)} custom-call(s32[1]{0:T(128)S(6)} %copy.10.length_ref, bf16[36,144,128]{2,1,0:T(8,128)(2,1)S(1)} %right.1.right_ref, f32[4,144,128]{2,1,0:T(8,128)S(1)} %get-tuple-element.24.near_left_ref, f32[4,144,128]{2,1,0:T(8,128)S(1)} %get-tuple-element.28.far_left_ref, ...), custom_call_target="tpu_custom_call" | custom-call | flops 5308416 | bytes 1327104 | tf_op jit(solution)/shard_map/keep/pallas_call | solution.py:370
  15.9 0.1 collective-permute-done.5.got_ref
  16.0 0.0 copy-done.3
  16.0 0.9 %last.1 = bf16[18,8,128]{2,1,0:T(8,128)(2,1)} custom-call(f32[2,144,128]{2,1,0:T(8,128)S(1)} %keep.1.keep_ref, f32[2,144,128]{2,1,0:T(8,128)S(1)} %collective-permute-done.5.got_ref, bf16[128,128]{1,0:T(8,128)(2,1)S(1)} %copy-done.3), custom_call_target="tpu_custom_call" | custom-call | tf_op jit(solution)/shard_map/last/pallas_call | solution.py:382
  (8 shorter events, 0.1 us)
Async XLA Ops:
  0.0 6.9 %copy-start.7 = (bf16[1,288,128]{2,1,0:T(8,128)(2,1)S(1)}, bf16[1,288,128]{2,1,0:T(8,128)(2,1)}, u32[]{:S(2)}) copy-start(bf16[1,288,128]{2,1,0:T(8,128)(2,1)} %param.10) | copy-start | bytes 221188
  0.0 8.0 %copy-start.6 = (bf16[128,128]{1,0:T(8,128)(2,1)S(1)}, bf16[128,128]{1,0:T(8,128)(2,1)}, u32[]{:S(2)}) copy-start(bf16[128,128]{1,0:T(8,128)(2,1)} %gate_ref.3) | copy-start | bytes 98308
  0.0 8.0 %copy-start.5 = (bf16[128,128]{1,0:T(8,128)(2,1)S(1)}, bf16[128,128]{1,0:T(8,128)(2,1)}, u32[]{:S(2)}) copy-start(bf16[128,128]{1,0:T(8,128)(2,1)} %weight_ref.4) | copy-start | bytes 98308
  0.0 8.0 %copy-start.4 = (bf16[36,144,128]{2,1,0:T(8,128)(2,1)S(1)}, bf16[36,144,128]{2,1,0:T(8,128)(2,1)}, u32[]{:S(2)}) copy-start(bf16[36,144,128]{2,1,0:T(8,128)(2,1)} %pair_ref.1) | copy-start | bytes 3981316
  0.0 10.1 %collective-permute-start = (bf16[1,288,128]{2,1,0:T(8,128)(2,1)}, bf16[1,288,128]{2,1,0:T(8,128)(2,1)S(1)}, u32[]{:S(2)}, u32[]{:S(2)}) collective-permute-start(bf16[1,288,128]{2,1,0:T(8,128)(2,1)} %param.10), channel_id=1, source_target_pairs={{0,14},{1,13},{2,12},{3,15},{4,10},{5,9},{6,8},{7,11},{8,6},{9,5},... | collective-permute-start | bytes 221192 | tf_op jit(solution)/shard_map/ppermute | solution.py:241
  6.1 6.0 %collective-permute-start.2 = (bf16[1,288,128]{2,1,0:T(8,128)(2,1)}, bf16[1,288,128]{2,1,0:T(8,128)(2,1)S(1)}, u32[]{:S(2)}, u32[]{:S(2)}) collective-permute-start(bf16[1,288,128]{2,1,0:T(8,128)(2,1)} %param.10), channel_id=1, source_target_pairs={{0,8},{1,11},{2,10},{3,9},{4,12},{5,15},{6,14},{7,13},{8,0},{9,3},... | collective-permute-start | bytes 221192 | tf_op jit(solution)/shard_map/ppermute | solution.py:241
  6.1 6.0 %collective-permute-start.1 = (bf16[1,288,128]{2,1,0:T(8,128)(2,1)}, bf16[1,288,128]{2,1,0:T(8,128)(2,1)S(1)}, u32[]{:S(2)}, u32[]{:S(2)}) collective-permute-start(bf16[1,288,128]{2,1,0:T(8,128)(2,1)} %param.10), channel_id=1, source_target_pairs={{0,4},{1,7},{2,6},{3,5},{4,0},{5,3},{6,2},{7,1},{8,12},{9,15},{10,... | collective-permute-start | bytes 221192 | tf_op jit(solution)/shard_map/ppermute | solution.py:241
  6.9 5.4 %collective-permute-start.3 = (bf16[1,288,128]{2,1,0:T(8,128)(2,1)S(1)}, bf16[1,288,128]{2,1,0:T(8,128)(2,1)S(1)}, u32[]{:S(2)}, u32[]{:S(2)}) collective-permute-start(bf16[1,288,128]{2,1,0:T(8,128)(2,1)S(1)} %copy-done.7), channel_id=1, source_target_pairs={{0,2},{1,3},{2,0},{3,1},{4,6},{5,7},{6,4},{7,5},{8,10},{9,11},{10,... | collective-permute-start | bytes 221192 | tf_op jit(solution)/shard_map/ppermute | solution.py:241
  8.1 4.2 %copy-start = (bf16[128,128]{1,0:T(8,128)(2,1)S(1)}, bf16[128,128]{1,0:T(8,128)(2,1)}, u32[]{:S(2)}) copy-start(bf16[128,128]{1,0:T(8,128)(2,1)} %gate_ref.5) | copy-start | bytes 98308
  8.1 4.2 %copy-start.1 = (bf16[128,128]{1,0:T(8,128)(2,1)S(1)}, bf16[128,128]{1,0:T(8,128)(2,1)}, u32[]{:S(2)}) copy-start(bf16[128,128]{1,0:T(8,128)(2,1)} %weight_ref.6) | copy-start | bytes 98308
  8.1 4.2 %copy-start.2 = (bf16[128,128]{1,0:T(8,128)(2,1)S(1)}, bf16[128,128]{1,0:T(8,128)(2,1)}, u32[]{:S(2)}) copy-start(bf16[128,128]{1,0:T(8,128)(2,1)} %out_gate_ref.3) | copy-start | bytes 98308
  12.2 1.4 %collective-permute-start.4 = (bf16[3,144,128]{2,1,0:T(8,128)(2,1)S(1)}, bf16[3,144,128]{2,1,0:T(8,128)(2,1)S(1)}, u32[]{:S(2)}, u32[]{:S(2)}) collective-permute-start(bf16[3,144,128]{2,1,0:T(8,128)(2,1)S(1)} %pad_maximum_fusion.2), channel_id=1, source_target_pairs={{0,1},{1,0},{2,3},{3,2},{4,5},{5,4},{6,7},{7,6},{8,9},{9,8},{10,11... | collective-permute-start | bytes 331784 | tf_op jit(solution)/shard_map/ppermute | solution.py:241
  14.6 1.5 %copy-start.3 = (bf16[128,128]{1,0:T(8,128)(2,1)S(1)}, bf16[128,128]{1,0:T(8,128)(2,1)}, u32[]{:S(2)}) copy-start(bf16[128,128]{1,0:T(8,128)(2,1)} %weight_ref.7) | copy-start | bytes 98308
  14.6 1.4 %collective-permute-start.5 = (f32[2,144,128]{2,1,0:T(8,128)S(1)}, f32[2,144,128]{2,1,0:T(8,128)S(1)}, u32[]{:S(2)}, u32[]{:S(2)}) collective-permute-start(f32[2,144,128]{2,1,0:T(8,128)S(1)} %get-tuple-element.30), channel_id=1, source_target_pairs={{0,1},{1,0},{2,3},{3,2},{4,5},{5,4},{6,7},{7,6},{8,9},{9,8},{10,11... | collective-permute-start | bytes 442376 | tf_op jit(solution)/shard_map/ppermute | solution.py:241

commit v12 on v11

--- a/solution.py
+++ b/solution.py
@@ -265,14 +265,14 @@
     def part(x, which):
         return lax.dynamic_slice_in_dim(x, which * half_cols, half_cols, 1)
 
-    first, second, third = [out(slab, *m) for m in ((7, 6), (2, 3), (4, 5))]
+    first, second, third = [out(slab, *m) for m in ((4, 7), (3, 6), (5, 2))]
     beside = out(slab_late, 1, 1)
     over = jnp.concatenate([part(x, 1 - side) for x in (first, second, third)], axis=0)
     over, made = between(over)
     over = passed(over, lambda row, core: (row, 1 - core))
     near = jnp.concatenate([half, part(beside, side), part(first, side), part(second, side)], axis=0)
     far = jnp.concatenate([part(third, side), over], axis=0)
-    return near, far, [[0, 1, 7, 2], [0, 1, 6, 3]], [[4, 6, 3, 5], [5, 7, 2, 4]], made
+    return near, far, [[0, 1, 4, 3], [0, 1, 7, 6]], [[5, 7, 6, 2], [2, 4, 3, 5]], made
 
 
 def shards(pair_rep, slab_rep, length, weight_a, gate_a, weight_b, gate_b, weight_gate, weight_out):

time: 17.1 us -> 17.7 us (1.035)
  starting transfers between devices: 7.72 us -> 8.88 us
  waiting for transfers between devices: 2.38 us -> 1.84 us
    ppermute x6, starting transfers between devices: 7.72 us -> 8.88 us  [passed(): return lax.ppermute(x, ('row', 'col'), pairs)]
    ppermute x6, waiting for transfers between devices: 2.38 us -> 1.84 us  [passed(): return lax.ppermute(x, ('row', 'col'), pairs)]
  transfers between devices with their start and end apart: 6 -> 6, of which waited for: 3 -> 4; matrix products, arithmetic and copies ran while one was open for 1% -> 1% of each run, Pallas kernels for 23% -> 22%
where the time goes in v12:
time: 17.7 us; the launch traced here: 17.6 us
  starting transfers between devices  8.88 us (50%)
  Pallas kernels  5.87 us (33%)
  waiting for transfers between devices  1.84 us (10%)
  between operations  0.83 us (5%)
    ppermute x6, starting transfers between devices, passed(): return lax.ppermute(x, ('row', 'col'), pairs)  8.88 us
    pallas_call x1, Pallas kernels, between(): right_call(center, share, weight_b, gate_b, pair_rep)  1.96 us
    ppermute x6, waiting for transfers between devices, passed(): return lax.ppermute(x, ('row', 'col'), pairs)  1.84 us
    pallas_call x1, Pallas kernels, shards(): pl.pallas_call(functools.partial(send_kernel, blocks=blocks, near_places=...  1 us
    pallas_call x1, Pallas kernels, shards(): pl.pallas_call(functools.partial(near_kernel, blocks=blocks), out_shape=(...  0.99 us
    pallas_call x1, Pallas kernels, shards(): pl.pallas_call(functools.partial(keep_kernel, blocks=blocks, near_places=...  0.96 us
    pallas_call x1, Pallas kernels, shards(): pl.pallas_call(functools.partial(last_kernel, half_cols=half_cols), out_s...  0.93 us
  transfers between devices with their start and end apart: 6, of which 4 were waited for; matrix products, arithmetic and copies ran while one was open for 1% of the time, Pallas kernels for 22%

profile of v12, /device:TPU:0, one launch (start us, length us, event | category | flops | bytes accessed | tf_op | source)
XLA Modules:
  0.0 17.6 jit_solution(9601620444451025029)
XLA Ops:
  0.0 0.0 copy-start.7
  0.0 0.0 copy-start.6
  0.0 0.0 copy-start.5
  0.0 0.0 copy-start.4
  0.0 4.1 %collective-permute-start = (bf16[1,288,128]{2,1,0:T(8,128)(2,1)}, bf16[1,288,128]{2,1,0:T(8,128)(2,1)S(1)}, u32[]{:S(2)}, u32[]{:S(2)}) collective-permute-start(bf16[1,288,128]{2,1,0:T(8,128)(2,1)} %param.10), channel_id=1, source_target_pairs={{0,8},{1,15},{2,10},{3,13},{4,12},{5,11},{6,14},{7,9},{8,0},{9,7},... | collective-permute-start | bytes 221192 | tf_op jit(solution)/shard_map/ppermute | solution.py:241
  4.1 1.3 %collective-permute-start.2 = (bf16[1,288,128]{2,1,0:T(8,128)(2,1)}, bf16[1,288,128]{2,1,0:T(8,128)(2,1)S(1)}, u32[]{:S(2)}, u32[]{:S(2)}) collective-permute-start(bf16[1,288,128]{2,1,0:T(8,128)(2,1)} %param.10), channel_id=1, source_target_pairs={{0,10},{1,5},{2,8},{3,7},{4,14},{5,1},{6,12},{7,3},{8,2},{9,13},{1... | collective-permute-start | bytes 221192 | tf_op jit(solution)/shard_map/ppermute | solution.py:241
  5.4 1.5 %collective-permute-start.1 = (bf16[1,288,128]{2,1,0:T(8,128)(2,1)}, bf16[1,288,128]{2,1,0:T(8,128)(2,1)S(1)}, u32[]{:S(2)}, u32[]{:S(2)}) collective-permute-start(bf16[1,288,128]{2,1,0:T(8,128)(2,1)} %param.10), channel_id=1, source_target_pairs={{0,6},{1,13},{2,4},{3,15},{4,2},{5,9},{6,0},{7,11},{8,14},{9,5},{1... | collective-permute-start | bytes 221192 | tf_op jit(solution)/shard_map/ppermute | solution.py:241
  7.0 0.0 copy-done.7
  7.0 1.6 %collective-permute-start.3 = (bf16[1,288,128]{2,1,0:T(8,128)(2,1)S(1)}, bf16[1,288,128]{2,1,0:T(8,128)(2,1)S(1)}, u32[]{:S(2)}, u32[]{:S(2)}) collective-permute-start(bf16[1,288,128]{2,1,0:T(8,128)(2,1)S(1)} %copy-done.7), channel_id=1, source_target_pairs={{0,2},{1,3},{2,0},{3,1},{4,6},{5,7},{6,4},{7,5},{8,10},{9,11},{10,... | collective-permute-start | bytes 221192 | tf_op jit(solution)/shard_map/ppermute | solution.py:241
  9.2 0.0 copy-done.6
  9.2 0.0 copy-done.5
  9.2 0.0 copy-done.4
  9.2 0.0 copy-start
  9.2 0.0 copy-start.1
  9.2 0.0 copy-start.2
  9.2 2.0 %right.1.right_ref = bf16[36,144,128]{2,1,0:T(8,128)(2,1)S(1)} custom-call(bf16[256,256]{1,0:T(8,128)(2,1)S(1)} %get-tuple-element.20.center_ref, bf16[256,256]{1,0:T(8,128)(2,1)S(1)} %get-tuple-element.21.share_ref, bf16[128,128]{1,0:T(8,128)(2,1)S(1)} %copy-done.5, bf16[128,128]{1,0:T(8,128)(2,1)S(1)} %copy-done.6, bf16[36,144,128]{2,1,0:T(8,128)(2,1)S(1)} %copy-done.4), custom_call_target="tpu_custom_call" | custom-call | flops 1019215872 | bytes 2654208 | tf_op jit(solution)/shard_map/right/pallas_call | solution.py:325
  11.2 0.0 collective-permute-done
  11.2 0.5 %collective-permute-done.1 = bf16[1,288,128]{2,1,0:T(8,128)(2,1)S(1)} collective-permute-done((bf16[1,288,128]{2,1,0:T(8,128)(2,1)}, bf16[1,288,128]{2,1,0:T(8,128)(2,1)S(1)}, u32[]{:S(2)}, u32[]{:S(2)}) %collective-permute-start.1) | collective-permute-done | bytes 73760 | tf_op jit(solution)/shard_map/ppermute | solution.py:241
  11.8 0.9 %collective-permute-done.2 = bf16[1,288,128]{2,1,0:T(8,128)(2,1)S(1)} collective-permute-done((bf16[1,288,128]{2,1,0:T(8,128)(2,1)}, bf16[1,288,128]{2,1,0:T(8,128)(2,1)S(1)}, u32[]{:S(2)}, u32[]{:S(2)}) %collective-permute-start.2) | collective-permute-done | bytes 73760 | tf_op jit(solution)/shard_map/ppermute | solution.py:241
  12.8 0.1 collective-permute-start.4
  12.8 0.0 collective-permute-done.3
  12.9 0.0 copy-done
  12.9 0.0 copy-done.1
  12.9 0.0 copy-done.2
  12.9 1.0 %near.1 = (f32[1,72,128]{2,1,0:T(8,128)S(1)}, f32[160,128]{1,0:T(8,128)S(1)}, f32[4,144,128]{2,1,0:T(8,128)S(1)}) custom-call(s32[1]{0:T(128)S(6)} %copy.10.length_ref, bf16[256,256]{1,0:T(8,128)(2,1)S(1)} %get-tuple-element.20.center_ref, bf16[256,256]{1,0:T(8,128)(2,1)S(1)} %get-tuple-element.21.share_ref, bf16[36,144,128]{2,1,0:T(8,128)(2,1)S(1)} %right.1.right_ref, ...), custom_call_target="tpu_custom_call" | custom-call | flops 5308416 | bytes 1327104 | tf_op jit(solution)/shard_map/near/pallas_call | solution.py:345
  13.9 0.2 %collective-permute-done.4 = bf16[3,144,128]{2,1,0:T(8,128)(2,1)S(1)} collective-permute-done((bf16[3,144,128]{2,1,0:T(8,128)(2,1)S(1)}, bf16[3,144,128]{2,1,0:T(8,128)(2,1)S(1)}, u32[]{:S(2)}, u32[]{:S(2)}) %collective-permute-start.4) | collective-permute-done | bytes 110624 | tf_op jit(solution)/shard_map/ppermute | solution.py:241
  14.2 1.0 %send.1 = (f32[2,144,128]{2,1,0:T(8,128)S(1)}, f32[4,144,128]{2,1,0:T(8,128)S(1)}, f32[160,128]{1,0:T(8,128)S(1)}) custom-call(s32[1]{0:T(128)S(6)} %copy.10.length_ref, bf16[256,256]{1,0:T(8,128)(2,1)S(1)} %get-tuple-element.20.center_ref, bf16[256,256]{1,0:T(8,128)(2,1)S(1)} %get-tuple-element.21.share_ref, bf16[36,144,128]{2,1,0:T(8,128)(2,1)S(1)} %right.1.right_ref, ...), custom_call_target="tpu_custom_call" | custom-call | tf_op jit(solution)/shard_map/send/pallas_call | solution.py:357
  15.2 0.0 copy-start.3
  15.2 0.3 %collective-permute-start.5 = (f32[2,144,128]{2,1,0:T(8,128)S(1)}, f32[2,144,128]{2,1,0:T(8,128)S(1)}, u32[]{:S(2)}, u32[]{:S(2)}) collective-permute-start(f32[2,144,128]{2,1,0:T(8,128)S(1)} %get-tuple-element.30), channel_id=1, source_target_pairs={{0,1},{1,0},{2,3},{3,2},{4,5},{5,4},{6,7},{7,6},{8,9},{9,8},{10,11... | collective-permute-start | bytes 442376 | tf_op jit(solution)/shard_map/ppermute | solution.py:241
  15.5 1.0 %keep.1.keep_ref = f32[2,144,128]{2,1,0:T(8,128)S(1)} custom-call(s32[1]{0:T(128)S(6)} %copy.10.length_ref, bf16[36,144,128]{2,1,0:T(8,128)(2,1)S(1)} %right.1.right_ref, f32[4,144,128]{2,1,0:T(8,128)S(1)} %get-tuple-element.24.near_left_ref, f32[4,144,128]{2,1,0:T(8,128)S(1)} %get-tuple-element.28.far_left_ref, ...), custom_call_target="tpu_custom_call" | custom-call | flops 5308416 | bytes 1327104 | tf_op jit(solution)/shard_map/keep/pallas_call | solution.py:370
  16.5 0.1 collective-permute-done.5.got_ref
  16.6 0.0 copy-done.3
  16.6 0.9 %last.1 = bf16[18,8,128]{2,1,0:T(8,128)(2,1)} custom-call(f32[2,144,128]{2,1,0:T(8,128)S(1)} %keep.1.keep_ref, f32[2,144,128]{2,1,0:T(8,128)S(1)} %collective-permute-done.5.got_ref, bf16[128,128]{1,0:T(8,128)(2,1)S(1)} %copy-done.3), custom_call_target="tpu_custom_call" | custom-call | tf_op jit(solution)/shard_map/last/pallas_call | solution.py:382
  (8 shorter events, 0.1 us)
Async XLA Ops:
  0.0 7.0 %copy-start.7 = (bf16[1,288,128]{2,1,0:T(8,128)(2,1)S(1)}, bf16[1,288,128]{2,1,0:T(8,128)(2,1)}, u32[]{:S(2)}) copy-start(bf16[1,288,128]{2,1,0:T(8,128)(2,1)} %param.10) | copy-start | bytes 221188
  0.0 9.2 %copy-start.6 = (bf16[128,128]{1,0:T(8,128)(2,1)S(1)}, bf16[128,128]{1,0:T(8,128)(2,1)}, u32[]{:S(2)}) copy-start(bf16[128,128]{1,0:T(8,128)(2,1)} %gate_ref.3) | copy-start | bytes 98308
  0.0 9.2 %copy-start.5 = (bf16[128,128]{1,0:T(8,128)(2,1)S(1)}, bf16[128,128]{1,0:T(8,128)(2,1)}, u32[]{:S(2)}) copy-start(bf16[128,128]{1,0:T(8,128)(2,1)} %weight_ref.4) | copy-start | bytes 98308
  0.0 9.2 %copy-start.4 = (bf16[36,144,128]{2,1,0:T(8,128)(2,1)S(1)}, bf16[36,144,128]{2,1,0:T(8,128)(2,1)}, u32[]{:S(2)}) copy-start(bf16[36,144,128]{2,1,0:T(8,128)(2,1)} %pair_ref.1) | copy-start | bytes 3981316
  0.0 11.2 %collective-permute-start = (bf16[1,288,128]{2,1,0:T(8,128)(2,1)}, bf16[1,288,128]{2,1,0:T(8,128)(2,1)S(1)}, u32[]{:S(2)}, u32[]{:S(2)}) collective-permute-start(bf16[1,288,128]{2,1,0:T(8,128)(2,1)} %param.10), channel_id=1, source_target_pairs={{0,8},{1,15},{2,10},{3,13},{4,12},{5,11},{6,14},{7,9},{8,0},{9,7},... | collective-permute-start | bytes 221192 | tf_op jit(solution)/shard_map/ppermute | solution.py:241
  4.1 8.6 %collective-permute-start.2 = (bf16[1,288,128]{2,1,0:T(8,128)(2,1)}, bf16[1,288,128]{2,1,0:T(8,128)(2,1)S(1)}, u32[]{:S(2)}, u32[]{:S(2)}) collective-permute-start(bf16[1,288,128]{2,1,0:T(8,128)(2,1)} %param.10), channel_id=1, source_target_pairs={{0,10},{1,5},{2,8},{3,7},{4,14},{5,1},{6,12},{7,3},{8,2},{9,13},{1... | collective-permute-start | bytes 221192 | tf_op jit(solution)/shard_map/ppermute | solution.py:241
  5.4 6.4 %collective-permute-start.1 = (bf16[1,288,128]{2,1,0:T(8,128)(2,1)}, bf16[1,288,128]{2,1,0:T(8,128)(2,1)S(1)}, u32[]{:S(2)}, u32[]{:S(2)}) collective-permute-start(bf16[1,288,128]{2,1,0:T(8,128)(2,1)} %param.10), channel_id=1, source_target_pairs={{0,6},{1,13},{2,4},{3,15},{4,2},{5,9},{6,0},{7,11},{8,14},{9,5},{1... | collective-permute-start | bytes 221192 | tf_op jit(solution)/shard_map/ppermute | solution.py:241
  7.0 5.9 %collective-permute-start.3 = (bf16[1,288,128]{2,1,0:T(8,128)(2,1)S(1)}, bf16[1,288,128]{2,1,0:T(8,128)(2,1)S(1)}, u32[]{:S(2)}, u32[]{:S(2)}) collective-permute-start(bf16[1,288,128]{2,1,0:T(8,128)(2,1)S(1)} %copy-done.7), channel_id=1, source_target_pairs={{0,2},{1,3},{2,0},{3,1},{4,6},{5,7},{6,4},{7,5},{8,10},{9,11},{10,... | collective-permute-start | bytes 221192 | tf_op jit(solution)/shard_map/ppermute | solution.py:241
  9.2 3.7 %copy-start = (bf16[128,128]{1,0:T(8,128)(2,1)S(1)}, bf16[128,128]{1,0:T(8,128)(2,1)}, u32[]{:S(2)}) copy-start(bf16[128,128]{1,0:T(8,128)(2,1)} %gate_ref.5) | copy-start | bytes 98308
  9.2 3.7 %copy-start.1 = (bf16[128,128]{1,0:T(8,128)(2,1)S(1)}, bf16[128,128]{1,0:T(8,128)(2,1)}, u32[]{:S(2)}) copy-start(bf16[128,128]{1,0:T(8,128)(2,1)} %weight_ref.6) | copy-start | bytes 98308
  9.2 3.7 %copy-start.2 = (bf16[128,128]{1,0:T(8,128)(2,1)S(1)}, bf16[128,128]{1,0:T(8,128)(2,1)}, u32[]{:S(2)}) copy-start(bf16[128,128]{1,0:T(8,128)(2,1)} %out_gate_ref.3) | copy-start | bytes 98308
  12.8 1.4 %collective-permute-start.4 = (bf16[3,144,128]{2,1,0:T(8,128)(2,1)S(1)}, bf16[3,144,128]{2,1,0:T(8,128)(2,1)S(1)}, u32[]{:S(2)}, u32[]{:S(2)}) collective-permute-start(bf16[3,144,128]{2,1,0:T(8,128)(2,1)S(1)} %pad_maximum_fusion.2), channel_id=1, source_target_pairs={{0,1},{1,0},{2,3},{3,2},{4,5},{5,4},{6,7},{7,6},{8,9},{9,8},{10,11... | collective-permute-start | bytes 331784 | tf_op jit(solution)/shard_map/ppermute | solution.py:241
  15.2 1.5 %copy-start.3 = (bf16[128,128]{1,0:T(8,128)(2,1)S(1)}, bf16[128,128]{1,0:T(8,128)(2,1)}, u32[]{:S(2)}) copy-start(bf16[128,128]{1,0:T(8,128)(2,1)} %weight_ref.7) | copy-start | bytes 98308
  15.2 1.4 %collective-permute-start.5 = (f32[2,144,128]{2,1,0:T(8,128)S(1)}, f32[2,144,128]{2,1,0:T(8,128)S(1)}, u32[]{:S(2)}, u32[]{:S(2)}) collective-permute-start(f32[2,144,128]{2,1,0:T(8,128)S(1)} %get-tuple-element.30), channel_id=1, source_target_pairs={{0,1},{1,0},{2,3},{3,2},{4,5},{5,4},{6,7},{7,6},{8,9},{9,8},{10,11... | collective-permute-start | bytes 442376 | tf_op jit(solution)/shard_map/ppermute | solution.py:241

commit v13 on v12

--- a/solution.py
+++ b/solution.py
@@ -181,7 +181,7 @@
 
 def send_kernel(
     length_ref, center_ref, share_ref, right_ref, slab_ref, gate_ref, weight_ref, out_gate_ref, near_sums_ref, near_gates_ref,
-    send_ref, left_ref, gates_ref, sums_ref, norm_ref, *, blocks, near_places, far_places,
+    send_ref, left_ref, gates_ref, wide_ref, sums_ref, norm_ref, *, blocks, near_places, far_places,
 ):
     flip = 1 - lax.axis_index("col")
 
@@ -191,14 +191,18 @@
         else:
             pl.when(pl.program_id(0) == blocks - 1)(body)
 
-    at_end(lambda: assemble(send_ref, near_sums_ref, near_gates_ref, near_places, flip))
+    at_end(lambda: assemble(wide_ref, near_sums_ref, near_gates_ref, near_places, flip))
     project(
         length_ref, center_ref, share_ref, slab_ref, gate_ref, weight_ref, out_gate_ref,
         left_ref, gates_ref, norm_ref, right_ref.shape[0] // 2, blocks,
     )
     contract(length_ref, left_ref, right_ref, flip, sums_ref, blocks)
 
-    at_end(lambda: assemble(send_ref, sums_ref, gates_ref, far_places, flip))
+    def rest():
+        assemble(wide_ref, sums_ref, gates_ref, far_places, flip)
+        send_ref[...] = wide_ref[...].astype(BF16)
+
+    at_end(rest)
 
 
 def keep_kernel(
@@ -221,13 +225,13 @@
 
 def last_kernel(keep_ref, got_ref, weight_ref, out_ref, *, half_cols):
     rows_dev = 2 * out_ref.shape[0]
-    tri = keep_ref[0] + got_ref[0]
+    tri = keep_ref[0] + got_ref[0].astype(F32)
     d = tri - jnp.mean(tri, axis=-1, keepdims=True)
     var = jnp.mean(d * d, axis=-1, keepdims=True)
     n = (d * lax.rsqrt(var + EPS)).astype(BF16)
     projected = jnp.dot(n, weight_ref[...], preferred_element_type=F32)
     mine = lax.axis_index("row") * rows_dev // half_cols == lax.axis_index("col")
-    update = projected * jnp.where(mine, keep_ref[1], got_ref[1])
+    update = projected * jnp.where(mine, keep_ref[1], got_ref[1].astype(F32))
     out_ref[...] = update.astype(BF16).reshape(out_ref.shape)
 
 
@@ -265,14 +269,14 @@
     def part(x, which):
         return lax.dynamic_slice_in_dim(x, which * half_cols, half_cols, 1)
 
-    first, second, third = [out(slab, *m) for m in ((4, 7), (3, 6), (5, 2))]
+    first, second, third = [out(slab, *m) for m in ((5, 4), (2, 3), (6, 7))]
     beside = out(slab_late, 1, 1)
     over = jnp.concatenate([part(x, 1 - side) for x in (first, second, third)], axis=0)
     over, made = between(over)
     over = passed(over, lambda row, core: (row, 1 - core))
     near = jnp.concatenate([half, part(beside, side), part(first, side), part(second, side)], axis=0)
     far = jnp.concatenate([part(third, side), over], axis=0)
-    return near, far, [[0, 1, 4, 3], [0, 1, 7, 6]], [[5, 7, 6, 2], [2, 4, 3, 5]], made
+    return near, far, [[0, 1, 5, 2], [0, 1, 4, 3]], [[6, 4, 3, 7], [7, 5, 2, 6]], made
 
 
 def shards(pair_rep, slab_rep, length, weight_a, gate_a, weight_b, gate_b, weight_gate, weight_out):
@@ -356,11 +360,11 @@
 
     send, far_left, far_gates = pl.pallas_call(
         functools.partial(send_kernel, blocks=blocks, near_places=near_places, far_places=far_places),
-        out_shape=(swapped, left_shape, gates),
+        out_shape=(jax.ShapeDtypeStruct(swapped.shape, BF16), left_shape, gates),
         grid=grid,
         in_specs=[smem] + squares + [deep(rows_dev), deep(near)] + weights + [whole(*sums.shape), whole(*gates.shape)],
         out_specs=(whole(*swapped.shape), deep(near), whole(*gates.shape)),
-        scratch_shapes=[pltpu.VMEM(sums.shape, F32), norm],
+        scratch_shapes=[pltpu.VMEM(swapped.shape, F32), pltpu.VMEM(sums.shape, F32), norm],
         compiler_params=params,
         name="send",
     )(length, center, share, right, far_slabs, gate_a, weight_a, weight_gate, near_sums, near_gates)

time: 17.7 us -> 16.8 us (0.949)
  starting transfers between devices: 8.88 us -> 8.01 us
    ppermute x6, starting transfers between devices: 8.88 us -> 8.01 us  [passed(): return lax.ppermute(x, ('row', 'col'), pairs)]
  transfers between devices with their start and end apart: 6 -> 6, of which waited for: 4 -> 3; matrix products, arithmetic and copies ran while one was open for 1% -> 0% of each run, Pallas kernels for 22% -> 24%
where the time goes in v13:
time: 16.8 us; the launch traced here: 16.7 us
  starting transfers between devices  8.01 us (48%)
  Pallas kernels  5.88 us (35%)
  waiting for transfers between devices  1.85 us (11%)
  between operations  0.81 us (5%)
    ppermute x6, starting transfers between devices, passed(): return lax.ppermute(x, ('row', 'col'), pairs)  8.01 us
    pallas_call x1, Pallas kernels, between(): right_call(center, share, weight_b, gate_b, pair_rep)  1.96 us
    ppermute x6, waiting for transfers between devices, passed(): return lax.ppermute(x, ('row', 'col'), pairs)  1.85 us
    pallas_call x1, Pallas kernels, shards(): pl.pallas_call(functools.partial(send_kernel, blocks=blocks, near_places=...  1.02 us
    pallas_call x1, Pallas kernels, shards(): pl.pallas_call(functools.partial(near_kernel, blocks=blocks), out_shape=(...  0.99 us
    pallas_call x1, Pallas kernels, shards(): pl.pallas_call(functools.partial(keep_kernel, blocks=blocks, near_places=...  0.96 us
    pallas_call x1, Pallas kernels, shards(): pl.pallas_call(functools.partial(last_kernel, half_cols=half_cols), out_s...  0.93 us
  transfers between devices with their start and end apart: 6, of which 3 were waited for; matrix products, arithmetic and copies ran while one was open for 0% of the time, Pallas kernels for 24%

profile of v13, /device:TPU:0, one launch (start us, length us, event | category | flops | bytes accessed | tf_op | source)
XLA Modules:
  0.0 16.7 jit_solution(14835558863147642664)
XLA Ops:
  0.0 0.0 copy-start.7
  0.0 0.0 copy-start.6
  0.0 0.0 copy-start.5
  0.0 0.0 copy-start.4
  0.0 5.0 %collective-permute-start = (bf16[1,288,128]{2,1,0:T(8,128)(2,1)}, bf16[1,288,128]{2,1,0:T(8,128)(2,1)S(1)}, u32[]{:S(2)}, u32[]{:S(2)}) collective-permute-start(bf16[1,288,128]{2,1,0:T(8,128)(2,1)} %param.10), channel_id=1, source_target_pairs={{0,10},{1,9},{2,8},{3,11},{4,14},{5,13},{6,12},{7,15},{8,2},{9,1},... | collective-permute-start | bytes 221192 | tf_op jit(solution)/shard_map/ppermute | solution.py:245
  5.0 1.3 %collective-permute-start.2 = (bf16[1,288,128]{2,1,0:T(8,128)(2,1)}, bf16[1,288,128]{2,1,0:T(8,128)(2,1)S(1)}, u32[]{:S(2)}, u32[]{:S(2)}) collective-permute-start(bf16[1,288,128]{2,1,0:T(8,128)(2,1)} %param.10), channel_id=1, source_target_pairs={{0,12},{1,15},{2,14},{3,13},{4,8},{5,11},{6,10},{7,9},{8,4},{9,7},... | collective-permute-start | bytes 221192 | tf_op jit(solution)/shard_map/ppermute | solution.py:245
  6.4 0.2 %collective-permute-start.1 = (bf16[1,288,128]{2,1,0:T(8,128)(2,1)}, bf16[1,288,128]{2,1,0:T(8,128)(2,1)S(1)}, u32[]{:S(2)}, u32[]{:S(2)}) collective-permute-start(bf16[1,288,128]{2,1,0:T(8,128)(2,1)} %param.10), channel_id=1, source_target_pairs={{0,4},{1,7},{2,6},{3,5},{4,0},{5,3},{6,2},{7,1},{8,12},{9,15},{10,... | collective-permute-start | bytes 221192 | tf_op jit(solution)/shard_map/ppermute | solution.py:245
  6.7 0.0 copy-done.7
  6.7 0.6 %collective-permute-start.3 = (bf16[1,288,128]{2,1,0:T(8,128)(2,1)S(1)}, bf16[1,288,128]{2,1,0:T(8,128)(2,1)S(1)}, u32[]{:S(2)}, u32[]{:S(2)}) collective-permute-start(bf16[1,288,128]{2,1,0:T(8,128)(2,1)S(1)} %copy-done.7), channel_id=1, source_target_pairs={{0,2},{1,3},{2,0},{3,1},{4,6},{5,7},{6,4},{7,5},{8,10},{9,11},{10,... | collective-permute-start | bytes 221192 | tf_op jit(solution)/shard_map/ppermute | solution.py:245
  7.9 0.0 copy-done.6
  7.9 0.0 copy-done.5
  7.9 0.0 copy-done.4
  8.0 0.0 copy-start
  8.0 0.0 copy-start.1
  8.0 0.0 copy-start.2
  8.0 2.0 %right.1.right_ref = bf16[36,144,128]{2,1,0:T(8,128)(2,1)S(1)} custom-call(bf16[256,256]{1,0:T(8,128)(2,1)S(1)} %get-tuple-element.20.center_ref, bf16[256,256]{1,0:T(8,128)(2,1)S(1)} %get-tuple-element.21.share_ref, bf16[128,128]{1,0:T(8,128)(2,1)S(1)} %copy-done.5, bf16[128,128]{1,0:T(8,128)(2,1)S(1)} %copy-done.6, bf16[36,144,128]{2,1,0:T(8,128)(2,1)S(1)} %copy-done.4), custom_call_target="tpu_custom_call" | custom-call | flops 1019215872 | bytes 2654208 | tf_op jit(solution)/shard_map/right/pallas_call | solution.py:329
  10.0 0.3 %collective-permute-done = bf16[1,288,128]{2,1,0:T(8,128)(2,1)S(1)} collective-permute-done((bf16[1,288,128]{2,1,0:T(8,128)(2,1)}, bf16[1,288,128]{2,1,0:T(8,128)(2,1)S(1)}, u32[]{:S(2)}, u32[]{:S(2)}) %collective-permute-start) | collective-permute-done | bytes 73760 | tf_op jit(solution)/shard_map/ppermute | solution.py:245
  10.2 1.5 %collective-permute-done.1 = bf16[1,288,128]{2,1,0:T(8,128)(2,1)S(1)} collective-permute-done((bf16[1,288,128]{2,1,0:T(8,128)(2,1)}, bf16[1,288,128]{2,1,0:T(8,128)(2,1)S(1)}, u32[]{:S(2)}, u32[]{:S(2)}) %collective-permute-start.1) | collective-permute-done | bytes 73760 | tf_op jit(solution)/shard_map/ppermute | solution.py:245
  11.8 0.0 collective-permute-done.2
  11.8 0.5 %collective-permute-start.4 = (bf16[3,144,128]{2,1,0:T(8,128)(2,1)S(1)}, bf16[3,144,128]{2,1,0:T(8,128)(2,1)S(1)}, u32[]{:S(2)}, u32[]{:S(2)}) collective-permute-start(bf16[3,144,128]{2,1,0:T(8,128)(2,1)S(1)} %pad_maximum_fusion.2), channel_id=1, source_target_pairs={{0,1},{1,0},{2,3},{3,2},{4,5},{5,4},{6,7},{7,6},{8,9},{9,8},{10,11... | collective-permute-start | bytes 331784 | tf_op jit(solution)/shard_map/ppermute | solution.py:245
  12.3 0.0 collective-permute-done.3
  12.3 0.0 copy-done
  12.3 0.0 copy-done.1
  12.3 0.0 copy-done.2
  12.4 1.0 %near.1 = (f32[1,72,128]{2,1,0:T(8,128)S(1)}, f32[160,128]{1,0:T(8,128)S(1)}, f32[4,144,128]{2,1,0:T(8,128)S(1)}) custom-call(s32[1]{0:T(128)S(6)} %copy.10.length_ref, bf16[256,256]{1,0:T(8,128)(2,1)S(1)} %get-tuple-element.20.center_ref, bf16[256,256]{1,0:T(8,128)(2,1)S(1)} %get-tuple-element.21.share_ref, bf16[36,144,128]{2,1,0:T(8,128)(2,1)S(1)} %right.1.right_ref, ...), custom_call_target="tpu_custom_call" | custom-call | flops 5308416 | bytes 1327104 | tf_op jit(solution)/shard_map/near/pallas_call | solution.py:349
  13.4 0.0 collective-permute-done.4
  13.4 1.0 %send.1 = (bf16[2,144,128]{2,1,0:T(8,128)(2,1)S(1)}, f32[4,144,128]{2,1,0:T(8,128)S(1)}, f32[160,128]{1,0:T(8,128)S(1)}) custom-call(s32[1]{0:T(128)S(6)} %copy.10.length_ref, bf16[256,256]{1,0:T(8,128)(2,1)S(1)} %get-tuple-element.20.center_ref, bf16[256,256]{1,0:T(8,128)(2,1)S(1)} %get-tuple-element.21.share_ref, ...), custom_call_target="tpu_custom_call" | custom-call | tf_op jit(solution)/shard_map/send/pallas_call | solution.py:361
  14.4 0.0 copy-start.3
  14.4 0.3 %collective-permute-start.5 = (bf16[2,144,128]{2,1,0:T(8,128)(2,1)S(1)}, bf16[2,144,128]{2,1,0:T(8,128)(2,1)S(1)}, u32[]{:S(2)}, u32[]{:S(2)}) collective-permute-start(bf16[2,144,128]{2,1,0:T(8,128)(2,1)S(1)} %get-tuple-element.30), channel_id=1, source_target_pairs={{0,1},{1,0},{2,3},{3,2},{4,5},{5,4},{6,7},{7,6},{8,9},{9,8},{10,11... | collective-permute-start | bytes 221192 | tf_op jit(solution)/shard_map/ppermute | solution.py:245
  14.7 1.0 %keep.1.keep_ref = f32[2,144,128]{2,1,0:T(8,128)S(1)} custom-call(s32[1]{0:T(128)S(6)} %copy.10.length_ref, bf16[36,144,128]{2,1,0:T(8,128)(2,1)S(1)} %right.1.right_ref, f32[4,144,128]{2,1,0:T(8,128)S(1)} %get-tuple-element.24.near_left_ref, f32[4,144,128]{2,1,0:T(8,128)S(1)} %get-tuple-element.28.far_left_ref, ...), custom_call_target="tpu_custom_call" | custom-call | flops 5308416 | bytes 1327104 | tf_op jit(solution)/shard_map/keep/pallas_call | solution.py:374
  15.7 0.1 collective-permute-done.5.got_ref
  15.8 0.0 copy-done.3
  15.8 0.9 %last.1 = bf16[18,8,128]{2,1,0:T(8,128)(2,1)} custom-call(f32[2,144,128]{2,1,0:T(8,128)S(1)} %keep.1.keep_ref, bf16[2,144,128]{2,1,0:T(8,128)(2,1)S(1)} %collective-permute-done.5.got_ref, bf16[128,128]{1,0:T(8,128)(2,1)S(1)} %copy-done.3), custom_call_target="tpu_custom_call" | custom-call | tf_op jit(solution)/shard_map/last/pallas_call | solution.py:386
  (8 shorter events, 0.1 us)
Async XLA Ops:
  0.0 6.7 %copy-start.7 = (bf16[1,288,128]{2,1,0:T(8,128)(2,1)S(1)}, bf16[1,288,128]{2,1,0:T(8,128)(2,1)}, u32[]{:S(2)}) copy-start(bf16[1,288,128]{2,1,0:T(8,128)(2,1)} %param.10) | copy-start | bytes 221188
  0.0 7.9 %copy-start.6 = (bf16[128,128]{1,0:T(8,128)(2,1)S(1)}, bf16[128,128]{1,0:T(8,128)(2,1)}, u32[]{:S(2)}) copy-start(bf16[128,128]{1,0:T(8,128)(2,1)} %gate_ref.3) | copy-start | bytes 98308
  0.0 7.9 %copy-start.5 = (bf16[128,128]{1,0:T(8,128)(2,1)S(1)}, bf16[128,128]{1,0:T(8,128)(2,1)}, u32[]{:S(2)}) copy-start(bf16[128,128]{1,0:T(8,128)(2,1)} %weight_ref.4) | copy-start | bytes 98308
  0.0 7.9 %copy-start.4 = (bf16[36,144,128]{2,1,0:T(8,128)(2,1)S(1)}, bf16[36,144,128]{2,1,0:T(8,128)(2,1)}, u32[]{:S(2)}) copy-start(bf16[36,144,128]{2,1,0:T(8,128)(2,1)} %pair_ref.1) | copy-start | bytes 3981316
  0.0 10.2 %collective-permute-start = (bf16[1,288,128]{2,1,0:T(8,128)(2,1)}, bf16[1,288,128]{2,1,0:T(8,128)(2,1)S(1)}, u32[]{:S(2)}, u32[]{:S(2)}) collective-permute-start(bf16[1,288,128]{2,1,0:T(8,128)(2,1)} %param.10), channel_id=1, source_target_pairs={{0,10},{1,9},{2,8},{3,11},{4,14},{5,13},{6,12},{7,15},{8,2},{9,1},... | collective-permute-start | bytes 221192 | tf_op jit(solution)/shard_map/ppermute | solution.py:245
  5.0 6.7 %collective-permute-start.2 = (bf16[1,288,128]{2,1,0:T(8,128)(2,1)}, bf16[1,288,128]{2,1,0:T(8,128)(2,1)S(1)}, u32[]{:S(2)}, u32[]{:S(2)}) collective-permute-start(bf16[1,288,128]{2,1,0:T(8,128)(2,1)} %param.10), channel_id=1, source_target_pairs={{0,12},{1,15},{2,14},{3,13},{4,8},{5,11},{6,10},{7,9},{8,4},{9,7},... | collective-permute-start | bytes 221192 | tf_op jit(solution)/shard_map/ppermute | solution.py:245
  6.4 5.4 %collective-permute-start.1 = (bf16[1,288,128]{2,1,0:T(8,128)(2,1)}, bf16[1,288,128]{2,1,0:T(8,128)(2,1)S(1)}, u32[]{:S(2)}, u32[]{:S(2)}) collective-permute-start(bf16[1,288,128]{2,1,0:T(8,128)(2,1)} %param.10), channel_id=1, source_target_pairs={{0,4},{1,7},{2,6},{3,5},{4,0},{5,3},{6,2},{7,1},{8,12},{9,15},{10,... | collective-permute-start | bytes 221192 | tf_op jit(solution)/shard_map/ppermute | solution.py:245
  6.7 5.6 %collective-permute-start.3 = (bf16[1,288,128]{2,1,0:T(8,128)(2,1)S(1)}, bf16[1,288,128]{2,1,0:T(8,128)(2,1)S(1)}, u32[]{:S(2)}, u32[]{:S(2)}) collective-permute-start(bf16[1,288,128]{2,1,0:T(8,128)(2,1)S(1)} %copy-done.7), channel_id=1, source_target_pairs={{0,2},{1,3},{2,0},{3,1},{4,6},{5,7},{6,4},{7,5},{8,10},{9,11},{10,... | collective-permute-start | bytes 221192 | tf_op jit(solution)/shard_map/ppermute | solution.py:245
  8.0 4.4 %copy-start = (bf16[128,128]{1,0:T(8,128)(2,1)S(1)}, bf16[128,128]{1,0:T(8,128)(2,1)}, u32[]{:S(2)}) copy-start(bf16[128,128]{1,0:T(8,128)(2,1)} %gate_ref.5) | copy-start | bytes 98308
  8.0 4.4 %copy-start.1 = (bf16[128,128]{1,0:T(8,128)(2,1)S(1)}, bf16[128,128]{1,0:T(8,128)(2,1)}, u32[]{:S(2)}) copy-start(bf16[128,128]{1,0:T(8,128)(2,1)} %weight_ref.6) | copy-start | bytes 98308
  8.0 4.4 %copy-start.2 = (bf16[128,128]{1,0:T(8,128)(2,1)S(1)}, bf16[128,128]{1,0:T(8,128)(2,1)}, u32[]{:S(2)}) copy-start(bf16[128,128]{1,0:T(8,128)(2,1)} %out_gate_ref.3) | copy-start | bytes 98308
  11.8 1.5 %collective-permute-start.4 = (bf16[3,144,128]{2,1,0:T(8,128)(2,1)S(1)}, bf16[3,144,128]{2,1,0:T(8,128)(2,1)S(1)}, u32[]{:S(2)}, u32[]{:S(2)}) collective-permute-start(bf16[3,144,128]{2,1,0:T(8,128)(2,1)S(1)} %pad_maximum_fusion.2), channel_id=1, source_target_pairs={{0,1},{1,0},{2,3},{3,2},{4,5},{5,4},{6,7},{7,6},{8,9},{9,8},{10,11... | collective-permute-start | bytes 331784 | tf_op jit(solution)/shard_map/ppermute | solution.py:245
  14.4 1.3 %copy-start.3 = (bf16[128,128]{1,0:T(8,128)(2,1)S(1)}, bf16[128,128]{1,0:T(8,128)(2,1)}, u32[]{:S(2)}) copy-start(bf16[128,128]{1,0:T(8,128)(2,1)} %weight_ref.7) | copy-start | bytes 98308
  14.4 1.3 %collective-permute-start.5 = (bf16[2,144,128]{2,1,0:T(8,128)(2,1)S(1)}, bf16[2,144,128]{2,1,0:T(8,128)(2,1)S(1)}, u32[]{:S(2)}, u32[]{:S(2)}) collective-permute-start(bf16[2,144,128]{2,1,0:T(8,128)(2,1)S(1)} %get-tuple-element.30), channel_id=1, source_target_pairs={{0,1},{1,0},{2,3},{3,2},{4,5},{5,4},{6,7},{7,6},{8,9},{9,8},{10,11... | collective-permute-start | bytes 221192 | tf_op jit(solution)/shard_map/ppermute | solution.py:245
